TPU v7x, 128 devices: a whole 4x4x4 slice. The times are simulated.
128 devices in a mesh: grp: 4 (over z), dev: 32 (over y, x, core).
Axes of the slice: x: 4, y: 4, z: 4, core: 2. Of those that a mesh axis runs over, the one named last changes fastest.
Arguments:
- prior_iterate_velocity: float32 [8192, 2, 4096], P(('grp', 'dev')), may hold values from -3 to 3
- forcing: float32 [8192, 2, 4096], P(('grp', 'dev')), may hold values from -18 to 18
- mass_with_drag: float32 [8192, 4096], P(('grp', 'dev')), may hold values from 0.5 to 3
- coriolis: float32 [8192, 4096], P(('grp', 'dev')), may hold values from -1 to 1
- bulk_viscosity: float32 [8192, 4096], P(('grp', 'dev')), may hold values from 0.05 to 1.5
- line_inverse: float32 [8192, 4096], P(('grp', 'dev')), may hold values from -0.35 to 1.2
- tile_source_slot: int32 [4096], P(('grp', 'dev')), may hold values from 0 to 8191, as said below
- ocean_tile: int32 [8192], P(('grp', 'dev')), may hold values from -1 to 4095, as said below
Outputs:
- new_velocity: float32 [8192, 2, 4096], P(('grp', 'dev'))
Inputs may be any that keep to these rules, and one draw needn't show every extreme that they name: Tile t's data sit in slot tile_source_slot[t]; distinct tiles name distinct slots; the slot's ocean device, slot // 64, has the same index along grp as tile t's ice device t // 32; no ocean device holds more than 2 tiles of one ice device, and some pair holds exactly 2. ocean_tile[s] is the tile t with tile_source_slot[t] = s, or -1 where no tile names slot s.
All inputs are finite; a program needn't handle non-finite values.
Results may differ from a plain program's by a relative error of at most 0.0003.
Values sent between devices are 32-bit elements; how exact they have to be, the bound alone decides.
No kernel may reach another device: no remote copies, remote signals or barrier semaphores. Data moves between devices by JAX's collectives and lax.ppermute only.
A program may use at most 128 MiB of HBM per device.

v0:
```python
import jax
import jax.numpy as jnp
from jax import lax
from jax.sharding import PartitionSpec as P

TILE_SIDE = 64
TR = 4
TC = 8
SWEEPS = 3


EPSILON = 1e-06


def with_halo(x, sides, width):
    for axis, dim in sides:
        size, length = (lax.axis_size(axis), x.shape[dim])
        up = [(i, (i + 1) % size) for i in range(size - 1)]
        down = [(j, i) for i, j in up]
        last = lax.slice_in_dim(x, length - width, length, axis=dim)
        first = lax.slice_in_dim(x, 0, width, axis=dim)
        before = lax.ppermute(last, axis, up)
        after = lax.ppermute(first, axis, down)
        x = jnp.concatenate([before, x, after], axis=dim)
    return x


def face_values(padded):
    centre = padded[1:-1, 1:-1]
    west_face = 0.5 * (centre + padded[1:-1, :-2])
    east_face = 0.5 * (centre + padded[1:-1, 2:])
    south_face = 0.5 * (centre + padded[:-2, 1:-1])
    north_face = 0.5 * (centre + padded[2:, 1:-1])
    return (west_face, east_face, south_face, north_face)


def component_factors():
    along_x = jnp.array([1.25, 0.25], jnp.float32)[:, None, None]
    along_y = jnp.array([0.25, 1.25], jnp.float32)[:, None, None]
    return (along_x, along_y)


def jacobian(padded, damping, turning_rate, face_set, tile_cuts):
    centre = padded[:, 1:-1, 1:-1]
    west_cell = padded[:, 1:-1, :-2]
    east_cell = padded[:, 1:-1, 2:]
    south_cell = padded[:, :-2, 1:-1]
    north_cell = padded[:, 2:, 1:-1]
    if tile_cuts is not None:
        west_cell = west_cell * tile_cuts[0]
        east_cell = east_cell * tile_cuts[1]
        south_cell = south_cell * tile_cuts[2]
        north_cell = north_cell * tile_cuts[3]
    along_x, along_y = component_factors()
    west_face, east_face, south_face, north_face = face_set
    viscous = along_x * (west_face * (centre - west_cell) + east_face * (centre - east_cell))
    viscous = viscous + along_y * (
        south_face * (centre - south_cell) + north_face * (centre - north_cell)
    )
    turning = jnp.stack([-turning_rate * centre[1], turning_rate * centre[0]])
    return damping * centre + turning + viscous


def diagonal_scale(damping, face_set):
    along_x, along_y = component_factors()
    west_face, east_face, south_face, north_face = face_set
    return lax.rsqrt(
        damping + along_x * (west_face + east_face) + along_y * (south_face + north_face)
    )


def tile_masks(row_count, col_count):
    row_place = lax.broadcasted_iota(jnp.int32, (row_count, col_count), 0) % TILE_SIDE
    col_place = lax.broadcasted_iota(jnp.int32, (row_count, col_count), 1) % TILE_SIDE
    return (
        (col_place != 0).astype(jnp.float32),
        (col_place != TILE_SIDE - 1).astype(jnp.float32),
        (row_place != 0).astype(jnp.float32),
        (row_place != TILE_SIDE - 1).astype(jnp.float32),
    )


def precondition(source_index, apply_lines, damping, turning_rate, face_set, tile_cuts):
    iterate = apply_lines(source_index)
    for sweep in range(SWEEPS - 1):
        padded = jnp.pad(iterate, ((0, 0), (1, 1), (1, 1)))
        iterate = iterate + apply_lines(
            source_index - jacobian(padded, damping, turning_rate, face_set, tile_cuts)
        )
    return iterate


def least_squares(magnitude, upper_first, below_first, upper_cross, upper_second, below_second):
    radius_first = jnp.sqrt(upper_first * upper_first + below_first * below_first)
    cosine_first = upper_first / radius_first
    sine_first = below_first / radius_first
    lifted_top = cosine_first * upper_cross + sine_first * upper_second
    lifted_low = cosine_first * upper_second - sine_first * upper_cross
    radius_second = jnp.sqrt(lifted_low * lifted_low + below_second * below_second)
    weight_second = -(sine_first * magnitude) * (lifted_low / radius_second) / radius_second
    weight_first = (cosine_first * magnitude - lifted_top * weight_second) / radius_first
    return (weight_first, weight_second)


def to_block(tile_data):
    channels = tile_data.shape[1]
    blocks = tile_data.reshape(TR, TC, channels, TILE_SIDE, TILE_SIDE)
    return blocks.transpose(2, 0, 3, 1, 4).reshape(channels, TR * TILE_SIDE, TC * TILE_SIDE)


def to_tiles(ice_block):
    channels = ice_block.shape[0]
    blocks = ice_block.reshape(channels, TR, TILE_SIDE, TC, TILE_SIDE)
    return blocks.transpose(1, 3, 0, 2, 4).reshape(TR * TC, channels, TILE_SIDE * TILE_SIDE)


def shards(
    prior_iterate_velocity,
    forcing,
    mass_with_drag,
    coriolis,
    bulk_viscosity,
    line_inverse,
    tile_source_slot,
    ocean_tile,
):
    dev_count = lax.axis_size("dev")
    slot_count = ocean_tile.shape[0]
    tile_count = tile_source_slot.shape[0]
    pair_room = slot_count // dev_count
    cell_count = TILE_SIDE * TILE_SIDE
    occupied = ocean_tile >= 0
    target = ocean_tile // tile_count % dev_count
    within = ocean_tile % tile_count
    earlier = (
        (target[None, :] == target[:, None])
        & (within[None, :] < within[:, None])
        & occupied[None, :]
    )
    position = jnp.where(
        occupied, target * pair_room + jnp.sum(earlier.astype(jnp.int32), axis=1), 0
    )
    matches = (position[None, :] == jnp.arange(slot_count)[:, None]) & occupied[None, :]
    source_slot = jnp.sum(jnp.where(matches, jnp.arange(slot_count)[None, :], 0), axis=1)
    filled = jnp.any(matches, axis=1).astype(jnp.float32)[:, None, None]
    anchor = tile_source_slot // slot_count % dev_count
    tile_order = jnp.arange(tile_count)
    sooner = (anchor[None, :] == anchor[:, None]) & (tile_order[None, :] < tile_order[:, None])
    arrival = anchor * pair_room + jnp.sum(sooner.astype(jnp.int32), axis=1)
    fields = jnp.concatenate(
        [
            prior_iterate_velocity,
            forcing,
            mass_with_drag[:, None],
            coriolis[:, None],
            bulk_viscosity[:, None],
        ],
        axis=1,
    )
    line_tiles = None
    bundle = jnp.concatenate([fields, line_inverse[:, None]], axis=1)
    landed = lax.all_to_all(
        (bundle[source_slot] * filled).reshape(dev_count, pair_room, bundle.shape[1], cell_count),
        "dev",
        split_axis=0,
        concat_axis=0,
        tiled=True,
    ).reshape(slot_count, 8, cell_count)[arrival]
    ice_block = to_block(landed[:, :7])
    line_tiles = landed[:, 7]
    velocity = ice_block[0:2]
    forcing_grid = ice_block[2:4]
    damping = ice_block[4]
    turning_rate = ice_block[5]
    viscosity = ice_block[6]
    wide_visc = with_halo(viscosity, (("grp", 0), ("dev", 1)), 1)
    face_set = face_values(wide_visc)
    scale = diagonal_scale(damping, face_set)
    tile_cuts = tile_masks(viscosity.shape[0], viscosity.shape[1])

    def operator(values):
        padded = with_halo(values, (("grp", 1), ("dev", 2)), 1)
        return jacobian(padded, damping, turning_rate, face_set, None)

    def length(values):
        return jnp.sqrt(lax.psum(jnp.sum(values * values), ("grp", "dev")) + EPSILON)

    def project(mapped, basis_set):
        return lax.psum(
            jnp.stack([jnp.sum(mapped * vector) for vector in basis_set]), ("grp", "dev")
        )

    residual = forcing_grid - operator(velocity)
    magnitude = length(residual)
    basis_one = residual / magnitude
    line_mats = line_tiles.reshape(TR, TC, TILE_SIDE, TILE_SIDE)

    def apply_lines(source_index):
        scaled = (scale * source_index).reshape(2, TR, TILE_SIDE, TC, TILE_SIDE)
        output = jnp.einsum("caybx,abwx->caybw", scaled, line_mats, precision=lax.Precision.HIGHEST)
        return output.reshape(2, TR * TILE_SIDE, TC * TILE_SIDE) * scale

    step_one = precondition(basis_one, apply_lines, damping, turning_rate, face_set, tile_cuts)
    mapped = operator(step_one)
    upper_first = project(mapped, (basis_one,))[0]
    mapped = mapped - upper_first * basis_one
    below_first = length(mapped)
    basis_two = mapped / below_first
    step_two = precondition(basis_two, apply_lines, damping, turning_rate, face_set, tile_cuts)
    mapped = operator(step_two)
    totals = project(mapped, (basis_one, basis_two))
    upper_cross = totals[0]
    upper_second = totals[1]
    mapped = mapped - upper_cross * basis_one - upper_second * basis_two
    below_second = length(mapped)
    weight_first, weight_second = least_squares(
        magnitude, upper_first, below_first, upper_cross, upper_second, below_second
    )
    updated_velocity = velocity + weight_first * step_one + weight_second * step_two
    homeward = (
        jnp.zeros((slot_count, 2, cell_count), jnp.float32)
        .at[arrival]
        .set(to_tiles(updated_velocity))
    )
    returned = lax.all_to_all(
        homeward.reshape(dev_count, pair_room, 2, cell_count),
        "dev",
        split_axis=0,
        concat_axis=0,
        tiled=True,
    )
    returned = returned.reshape(slot_count, 2, cell_count)
    return returned[position] * occupied.astype(jnp.float32)[:, None, None]


def solution(mesh):
    return jax.shard_map(
        shards,
        mesh=mesh,
        in_specs=(
            P(("grp", "dev"), None, None),
            P(("grp", "dev"), None, None),
            P(("grp", "dev"), None),
            P(("grp", "dev"), None),
            P(("grp", "dev"), None),
            P(("grp", "dev"), None),
            P(("grp", "dev")),
            P(("grp", "dev")),
        ),
        out_specs=P(("grp", "dev"), None, None),
        check_vma=False,
    )
```

profile of v0, /device:TPU:1, one launch (start us, length us, event | category | flops | bytes accessed | tf_op | source)
XLA Modules:
  0.0 856.7 jit_solution(14234233244095312451)
XLA Ops:
  9.3 21.3 %concatenate.67 = f32[64,8,4096]{2,1,0:T(8,128)} concatenate(f32[64,2,4096]{2,1,0:T(2,128)} %param.24, f32[64,2,4096]{2,1,0:T(2,128)} %param.25, f32[64,1,4096]{2,1,0:T(1,128)S(1)} %copy.86, f32[64,1,4096]{2,1,0:T(1,128)S(1)} %copy.87, f32[64,1,4096]{2,1,0:T(1,128)S(1)} %copy.88, f32[64,1,4096]{2,1,0:T(1,128)} %copy.89), dimensions={1} | concatenate | bytes 16777216 | tf_op jit(solution)/shard_map/concatenate | solution.py:161
  30.6 7.8 gather_fusion
  38.4 8.0 broadcast_multiply_fusion
  46.4 8.8 %all-to-all-start = ((f32[32,2,8,4096]{3,2,1,0:T(8,128)}), f32[32,2,8,4096]{3,2,1,0:T(8,128)}, u32[]{:S(2)}, u32[]{:S(2)}) async-start(f32[32,2,8,4096]{3,2,1,0:T(8,128)} %broadcast_multiply_fusion), calls=%async_computation | async-start | bytes 16777216 | tf_op jit(solution)/shard_map/all_to_all | solution.py:162
  57.7 97.2 %all-to-all-done = f32[32,2,8,4096]{3,2,1,0:T(8,128)} async-done(((f32[32,2,8,4096]{3,2,1,0:T(8,128)}), f32[32,2,8,4096]{3,2,1,0:T(8,128)}, u32[]{:S(2)}, u32[]{:S(2)}) %all-to-all-start) | async-done | bytes 8388640 | tf_op jit(solution)/shard_map/all_to_all | solution.py:162
  154.9 6.2 gather_fusion.1
  161.1 7.5 reshape.390
  168.6 8.1 copy.91
  176.7 5.5 slice_bitcast_fusion
  184.8 4.4 slice_reduce_fusion
  192.0 3.8 collective-permute-start
  213.9 4.2 collective-permute-start.4
  222.4 2.9 copy.94
  229.7 4.2 collective-permute-start.2
  233.9 6.2 collective-permute-start.3
  246.0 4.4 collective-permute-done.7
  253.1 73.3 %psum.35 = f32[]{:T(128)} all-reduce(f32[]{:T(128)} %get-tuple-element.14), channel_id=1, replica_groups=mesh['grp'=4,'dev'=32] {'grp','dev'}, use_global_device_ids=true, to_apply=%region_5.6 | all-reduce | flops 1 | bytes 8 | tf_op jit(solution)/shard_map/psum | solution.py:186
  331.1 9.5 %fusion.15 = f32[2,4,64,8,64]{2,4,0,3,1:T(8,128)} fusion(f32[2,4,64,8,64]{4,3,2,1,0:T(8,128)} %reshape.337, f32[4,8,64,64,1]{3,2,1,0,4:T(8,128)} %reshape.389), kind=kOutput, calls=%fused_computation.22 | convolution fusion | flops 201326592 | bytes 2621440 | tf_op jit(solution)/shard_map/caybx,abwx->caybw/dot_general | solution.py:200
  340.6 2.9 copy.100
  354.9 9.4 %fusion.18 = f32[2,4,64,8,64]{2,4,0,3,1:T(8,128)} fusion(f32[2,4,64,8,64]{4,3,2,1,0:T(8,128)} %reshape.339, f32[4,8,64,64,1]{3,2,1,0,4:T(8,128)} %reshape.389), kind=kOutput, calls=%fused_computation.23 | convolution fusion | flops 201326592 | bytes 2621440 | tf_op jit(solution)/shard_map/caybx,abwx->caybw/dot_general | solution.py:200
  364.3 2.9 copy.102
  379.3 9.4 %fusion.21 = f32[2,4,64,8,64]{2,4,0,3,1:T(8,128)} fusion(f32[2,4,64,8,64]{4,3,2,1,0:T(8,128)} %reshape.341, f32[4,8,64,64,1]{3,2,1,0,4:T(8,128)} %reshape.389), kind=kOutput, calls=%fused_computation.24 | convolution fusion | flops 201326592 | bytes 2621440 | tf_op jit(solution)/shard_map/caybx,abwx->caybw/dot_general | solution.py:200
  388.6 2.9 copy.104
  391.5 3.1 reshape.342
  399.4 3.3 collective-permute-done.9
  402.9 4.5 collective-permute-start.10
  410.7 4.4 collective-permute-done.11
  415.2 3.4 multiply_reduce_fusion.4
  418.6 67.0 %psum.36 = f32[]{:T(128)} all-reduce(f32[]{:T(128)} %get-tuple-element.12), channel_id=1, replica_groups=mesh['grp'=4,'dev'=32] {'grp','dev'}, use_global_device_ids=true, to_apply=%region_7.8 | all-reduce | flops 1 | bytes 8 | tf_op jit(solution)/shard_map/psum | solution.py:189
  488.3 62.6 %psum.37 = f32[]{:T(128)} all-reduce(f32[]{:T(128)} %multiply_reduce_fusion.3), channel_id=1, replica_groups=mesh['grp'=4,'dev'=32] {'grp','dev'}, use_global_device_ids=true, to_apply=%region_9.10 | all-reduce | flops 1 | bytes 8 | tf_op jit(solution)/shard_map/psum | solution.py:186
  551.5 3.8 fusion.163
  558.0 9.4 %fusion.24 = f32[2,4,64,8,64]{2,4,0,3,1:T(8,128)} fusion(f32[2,4,64,8,64]{4,3,2,1,0:T(8,128)} %reshape.343, f32[4,8,64,64,1]{3,2,1,0,4:T(8,128)} %reshape.389), kind=kOutput, calls=%fused_computation.25 | convolution fusion | flops 201326592 | bytes 2621440 | tf_op jit(solution)/shard_map/caybx,abwx->caybw/dot_general | solution.py:200
  567.4 2.9 copy.106
  581.8 9.4 %fusion.27 = f32[2,4,64,8,64]{2,4,0,3,1:T(8,128)} fusion(f32[2,4,64,8,64]{4,3,2,1,0:T(8,128)} %reshape.345, f32[4,8,64,64,1]{3,2,1,0,4:T(8,128)} %reshape.389), kind=kOutput, calls=%fused_computation.26 | convolution fusion | flops 201326592 | bytes 2621440 | tf_op jit(solution)/shard_map/caybx,abwx->caybw/dot_general | solution.py:200
  591.2 2.9 copy.108
  606.2 9.4 %fusion.30 = f32[2,4,64,8,64]{2,4,0,3,1:T(8,128)} fusion(f32[2,4,64,8,64]{4,3,2,1,0:T(8,128)} %reshape.347, f32[4,8,64,64,1]{3,2,1,0,4:T(8,128)} %reshape.389), kind=kOutput, calls=%fused_computation.27 | convolution fusion | flops 201326592 | bytes 2621440 | tf_op jit(solution)/shard_map/caybx,abwx->caybw/dot_general | solution.py:200
  615.6 2.9 copy.110
  624.4 3.3 collective-permute-start.12
  647.3 7.1 multiply_reduce_fusion.2
  655.8 68.1 %psum.38 = f32[2]{0:T(128)S(1)} all-reduce(f32[2]{0:T(128)S(1)} %pad_maximum_fusion.44), channel_id=1, replica_groups=mesh['grp'=4,'dev'=32] {'grp','dev'}, use_global_device_ids=true, to_apply=%region_12.13 | all-reduce | flops 2 | bytes 16 | tf_op jit(solution)/shard_map/psum | solution.py:189
  726.5 3.7 multiply_reduce_fusion
  730.8 63.0 %psum.39 = f32[]{:T(128)} all-reduce(f32[]{:T(128)} %multiply_reduce_fusion), channel_id=1, replica_groups=mesh['grp'=4,'dev'=32] {'grp','dev'}, use_global_device_ids=true, to_apply=%region_14.15 | all-reduce | flops 1 | bytes 8 | tf_op jit(solution)/shard_map/psum | solution.py:186
  794.8 8.5 fusion.13
  809.8 4.6 scatter_fusion
  814.4 5.6 all-to-all-start.1
  820.0 27.8 %all-to-all-done.1 = f32[32,2,2,4096]{3,2,1,0:T(2,128)S(1)} async-done(((f32[32,2,2,4096]{3,2,1,0:T(2,128)}), f32[32,2,2,4096]{3,2,1,0:T(2,128)S(1)}, u32[]{:S(2)}, u32[]{:S(2)}) %all-to-all-start.1) | async-done | bytes 2097184 | tf_op jit(solution)/shard_map/all_to_all | solution.py:225
  847.9 4.0 gather_fusion.2
  851.8 4.4 broadcast_multiply_fusion.1
  (244 shorter events, 148.9 us)
Async XLA Ops:
  0.0 4.9 copy-start.60
  2.5 3.5 copy-start.61
  46.4 8.8 %copy-start.65 = (s32[32]{0:T(128)S(1)}, s32[32]{0:T(128)}, u32[]{:S(2)}) copy-start(s32[32]{0:T(128)} %param.30) | copy-start | bytes 388
  46.4 108.5 %all-to-all-start = ((f32[32,2,8,4096]{3,2,1,0:T(8,128)}), f32[32,2,8,4096]{3,2,1,0:T(8,128)}, u32[]{:S(2)}, u32[]{:S(2)}) async-start(f32[32,2,8,4096]{3,2,1,0:T(8,128)} %broadcast_multiply_fusion), calls=%async_computation | async-start | bytes 16777216 | tf_op jit(solution)/shard_map/all_to_all | solution.py:162
  176.7 6.5 copy-start
  192.0 5.1 copy-start.50
  192.0 37.5 %collective-permute-start = (f32[1,512]{1,0:T(1,128)S(1)}, f32[1,512]{1,0:T(1,128)S(1)}, u32[]{:S(2)}, u32[]{:S(2)}) collective-permute-start(f32[1,512]{1,0:T(1,128)S(1)} %get-tuple-element.61), channel_id=1, source_target_pairs={{0,32},{32,64},{64,96},{1,33},{33,65},{65,97},{2,34},{34,66},{66,9... | collective-permute-start | bytes 6152 | tf_op jit(solution)/shard_map/ppermute | solution.py:22
  195.8 33.7 %collective-permute-start.1 = (f32[1,512]{1,0:T(1,128)S(1)}, f32[1,512]{1,0:T(1,128)S(1)}, u32[]{:S(2)}, u32[]{:S(2)}) collective-permute-start(f32[1,512]{1,0:T(1,128)S(1)} %get-tuple-element.62), channel_id=1, source_target_pairs={{32,0},{64,32},{96,64},{33,1},{65,33},{97,65},{34,2},{66,34},{98,6... | collective-permute-start | bytes 6152 | tf_op jit(solution)/shard_map/ppermute | solution.py:23
  211.9 7.5 copy-start.58
  213.9 26.3 %copy-start.48 = (f32[2,256,512]{2,1,0:T(8,128)}, f32[2,256,512]{2,1,0:T(8,128)S(1)}, u32[]{:S(2)}) copy-start(f32[2,256,512]{2,1,0:T(8,128)S(1)} %slice.261) | copy-start | bytes 3145732
  213.9 26.2 %collective-permute-start.4 = (f32[2,1,512]{2,1,0:T(1,128)S(1)}, f32[2,1,512]{2,1,0:T(1,128)S(1)}, u32[]{:S(2)}, u32[]{:S(2)}) collective-permute-start(f32[2,1,512]{2,1,0:T(1,128)S(1)} %get-tuple-element.52), channel_id=1, source_target_pairs={{0,32},{32,64},{64,96},{1,33},{33,65},{65,97},{2,34},{34,66},{66,9... | collective-permute-start | bytes 12296 | tf_op jit(solution)/shard_map/ppermute | solution.py:22
  218.1 22.1 %collective-permute-start.5 = (f32[2,1,512]{2,1,0:T(1,128)S(1)}, f32[2,1,512]{2,1,0:T(1,128)S(1)}, u32[]{:S(2)}, u32[]{:S(2)}) collective-permute-start(f32[2,1,512]{2,1,0:T(1,128)S(1)} %get-tuple-element.53), channel_id=1, source_target_pairs={{32,0},{64,32},{96,64},{33,1},{65,33},{97,65},{34,2},{66,34},{98,6... | collective-permute-start | bytes 12296 | tf_op jit(solution)/shard_map/ppermute | solution.py:23
  225.4 4.2 copy-start.51
  229.5 15.5 %copy-start.52 = (f32[256,512]{1,0:T(8,128)S(1)}, f32[256,512]{1,0:T(8,128)}, u32[]{:S(2)}) copy-start(f32[256,512]{1,0:T(8,128)} %copy-done.50) | copy-start | bytes 1572868
  229.7 15.3 %collective-permute-start.2 = (f32[258,1]{1,0:T(8,128)S(1)}, f32[258,1]{1,0:T(8,128)S(1)}, u32[]{:S(2)}, u32[]{:S(2)}) collective-permute-start(f32[258,1]{1,0:T(8,128)S(1)} %get-tuple-element.57), channel_id=1, source_target_pairs={{0,1},{1,2},{2,3},{3,4},{4,5},{5,6},{6,7},{7,8},{8,9},{9,10},{10,1... | collective-permute-start | bytes 3104 | tf_op jit(solution)/shard_map/ppermute | solution.py:22
  233.9 11.1 %collective-permute-start.3 = (f32[258,1]{1,0:T(8,128)S(1)}, f32[258,1]{1,0:T(8,128)S(1)}, u32[]{:S(2)}, u32[]{:S(2)}) collective-permute-start(f32[258,1]{1,0:T(8,128)S(1)} %get-tuple-element.58), channel_id=1, source_target_pairs={{1,0},{2,1},{3,2},{4,3},{5,4},{6,5},{7,6},{8,7},{9,8},{10,9},{11,1... | collective-permute-start | bytes 3104 | tf_op jit(solution)/shard_map/ppermute | solution.py:23
  240.3 10.0 %copy-start.49 = (f32[2,256,512]{2,1,0:T(8,128)S(1)}, f32[2,256,512]{2,1,0:T(8,128)}, u32[]{:S(2)}) copy-start(f32[2,256,512]{2,1,0:T(8,128)} %copy-done.48) | copy-start | bytes 3145732
  240.3 10.0 %copy-start.53 = (f32[2,256,512]{2,1,0:T(8,128)S(1)}, f32[2,256,512]{2,1,0:T(8,128)}, u32[]{:S(2)}) copy-start(f32[2,256,512]{2,1,0:T(8,128)} %slice.260) | copy-start | bytes 3145732
  240.3 10.0 %copy-start.56 = (f32[1,256,512]{2,1,0:T(8,128)S(1)}, f32[1,256,512]{2,1,0:T(8,128)}, u32[]{:S(2)}) copy-start(f32[1,256,512]{2,1,0:T(8,128)} %get-tuple-element.59) | copy-start | bytes 1572868
  240.3 10.0 %copy-start.57 = (f32[1,256,512]{2,1,0:T(8,128)S(1)}, f32[1,256,512]{2,1,0:T(8,128)}, u32[]{:S(2)}) copy-start(f32[1,256,512]{2,1,0:T(8,128)} %get-tuple-element.60) | copy-start | bytes 1572868
  240.4 10.0 %copy-start.63 = (f32[2]{0:T(128)S(1)}, f32[2]{0:T(128)}, u32[]{:S(2)}) copy-start(f32[2]{0:T(128)} %constant.97.clone) | copy-start | bytes 28
  240.4 10.0 %copy-start.64 = (f32[2]{0:T(128)S(1)}, f32[2]{0:T(128)}, u32[]{:S(2)}) copy-start(f32[2]{0:T(128)} %constant.98.clone) | copy-start | bytes 28
  240.4 5.6 collective-permute-start.6
  242.6 7.8 collective-permute-start.7
  245.4 7.6 copy-start.1
  245.5 7.6 copy-start.8
  245.5 7.6 copy-start.15
  245.5 7.6 copy-start.21
  396.6 2.8 collective-permute-start.8
  397.9 17.2 %copy-start.4 = (f32[256,512]{1,0:T(8,128)S(1)}, f32[256,512]{1,0:T(8,128)}, u32[]{:S(2)}) copy-start(f32[256,512]{1,0:T(8,128)} %copy-done.1) | copy-start | bytes 1572868
  397.9 17.2 %copy-start.11 = (f32[256,512]{1,0:T(8,128)S(1)}, f32[256,512]{1,0:T(8,128)}, u32[]{:S(2)}) copy-start(f32[256,512]{1,0:T(8,128)} %copy-done.8) | copy-start | bytes 1572868
  397.9 17.2 %copy-start.18 = (f32[256,512]{1,0:T(8,128)S(1)}, f32[256,512]{1,0:T(8,128)}, u32[]{:S(2)}) copy-start(f32[256,512]{1,0:T(8,128)} %copy-done.15) | copy-start | bytes 1572868
  398.0 17.2 %copy-start.24 = (f32[256,512]{1,0:T(8,128)S(1)}, f32[256,512]{1,0:T(8,128)}, u32[]{:S(2)}) copy-start(f32[256,512]{1,0:T(8,128)} %copy-done.21) | copy-start | bytes 1572868
  398.0 4.8 collective-permute-start.9
  402.9 7.9 collective-permute-start.10
  407.4 7.8 collective-permute-start.11
  596.8 3.2 copy-start.28
  596.8 3.2 copy-start.39
  596.8 3.2 copy-start.43
  596.8 3.2 copy-start.47
  624.4 10.9 %collective-permute-start.12 = (f32[2,1,512]{2,1,0:T(1,128)S(1)}, f32[2,1,512]{2,1,0:T(1,128)S(1)}, u32[]{:S(2)}, u32[]{:S(2)}) collective-permute-start(f32[2,1,512]{2,1,0:T(1,128)S(1)} %get-tuple-element.48), channel_id=1, source_target_pairs={{0,32},{32,64},{64,96},{1,33},{33,65},{65,97},{2,34},{34,66},{66,9... | collective-permute-start | bytes 12296 | tf_op jit(solution)/shard_map/ppermute | solution.py:22
  627.7 7.7 collective-permute-start.13
  635.3 12.0 %copy-start.7 = (f32[256,512]{1,0:T(8,128)S(1)}, f32[256,512]{1,0:T(8,128)}, u32[]{:S(2)}) copy-start(f32[256,512]{1,0:T(8,128)} %copy-done.1) | copy-start | bytes 1572868
  635.3 12.0 %copy-start.14 = (f32[256,512]{1,0:T(8,128)S(1)}, f32[256,512]{1,0:T(8,128)}, u32[]{:S(2)}) copy-start(f32[256,512]{1,0:T(8,128)} %copy-done.8) | copy-start | bytes 1572868
  637.3 8.8 %collective-permute-start.14 = (f32[2,258,1]{2,1,0:T(8,128)}, f32[2,258,1]{2,1,0:T(8,128)S(1)}, u32[]{:S(2)}, u32[]{:S(2)}) collective-permute-start(f32[2,258,1]{2,1,0:T(8,128)} %get-tuple-element.42), channel_id=1, source_target_pairs={{0,1},{1,2},{2,3},{3,4},{4,5},{5,6},{6,7},{7,8},{8,9},{9,10},{10,1... | collective-permute-start | bytes 6200 | tf_op jit(solution)/shard_map/ppermute | solution.py:22
  639.2 8.1 collective-permute-start.15
  654.4 140.4 %copy-start.54 = (f32[4,64,8,64]{1,3,2,0:T(8,128)S(1)}, f32[4,64,8,64]{1,3,2,0:T(8,128)}, u32[]{:S(2)}) copy-start(f32[4,64,8,64]{1,3,2,0:T(8,128)} %copy.111) | copy-start | bytes 1572868
  814.4 33.5 %all-to-all-start.1 = ((f32[32,2,2,4096]{3,2,1,0:T(2,128)}), f32[32,2,2,4096]{3,2,1,0:T(2,128)S(1)}, u32[]{:S(2)}, u32[]{:S(2)}) async-start(f32[32,2,2,4096]{3,2,1,0:T(2,128)} %bitcast.22), calls=%async_computation.1 | async-start | bytes 4194304 | tf_op jit(solution)/shard_map/all_to_all | solution.py:225
  (36 other events, 64.7 us)
where the time goes:
time: 871 us; the launch traced here: 857 us
  blocking collectives  334 us (38%)
  local copies, waits for them, and re-layouts  179 us (21%)
  waiting for transfers between devices  140 us (16%)
  other arithmetic  81.1 us (9%)
  starting transfers between devices  58 us (7%)
  matrix products  56.4 us (6%)
    psum x3, blocking collectives, length(): lax.psum(jnp.sum(values * values), ('grp', 'dev')) + EPSILON  199 us
    psum x2, blocking collectives, project(): lax.psum(jnp.stack([jnp.sum(mapped * vector) for vector in basis_set]), (...  135 us
    all_to_all x1, waiting for transfers between devices, shards(): lax.all_to_all((bundle[source_slot] * filled).reshape(dev_count, pair_roo...  97.2 us
    dot_general x6, matrix products, apply_lines(): jnp.einsum('caybx,abwx->caybw', scaled, line_mats, precision=lax.Precisio...  56.4 us
    all_to_all x1, waiting for transfers between devices, shards(): lax.all_to_all(homeward.reshape(dev_count, pair_room, 2, cell_count), 'de...  27.8 us
    ppermute x8, starting transfers between devices, with_halo(): before = lax.ppermute(last, axis, up)  25.3 us
    concatenate x1, local copies, waits for them, and re-layouts, shards(): bundle = jnp.concatenate([fields, line_inverse[:, None]], axis=1)  21.3 us
    ppermute x8, starting transfers between devices, with_halo(): after = lax.ppermute(first, axis, down)  18.4 us
  transfers between devices with their start and end apart: 18, of which 8 were waited for; matrix products, arithmetic and copies ran while one was open for 5% of the time, Pallas kernels for 0%

commit v1 on v0

v1 whole, which is shorter than its diff:
```python
import jax
import jax.numpy as jnp
from jax import lax
from jax.experimental import pallas as pl
from jax.experimental.pallas import tpu as pltpu
from jax.sharding import PartitionSpec as P

F32 = jnp.float32
BF16 = jnp.bfloat16
SLOTS = 64
PAIRS = 32
TILES = 32
EPSILON = 1e-06
VMEM_LIMIT = 56 * 1024 * 1024


def params():
    return pltpu.CompilerParams(vmem_limit_bytes=VMEM_LIMIT)


def vmem():
    return pl.BlockSpec(memory_space=pltpu.VMEM)


def smem():
    return pl.BlockSpec(memory_space=pltpu.SMEM)


def struct(*shape, dtype=F32):
    return jax.ShapeDtypeStruct(shape, dtype)


def iota(shape, dim):
    return lax.broadcasted_iota(jnp.int32, shape, dim)


def roll(x, shift, axis):
    return pltpu.roll(x, shift, axis)


def pair_up(t0, t1):
    low = iota(t0.shape, 1) < 64
    return jnp.concatenate(
        [jnp.where(low, t0, roll(t1, 64, 1)), jnp.where(low, roll(t0, 64, 1), t1)], axis=0
    )


def split_up(q):
    even, odd = q[:32], q[32:]
    low = iota(even.shape, 1) < 64
    return (
        jnp.where(low, even, roll(odd, 64, 1)),
        jnp.where(low, roll(even, 64, 1), odd),
    )


def load_field(ref, table, j, empty):
    tiles = []
    for r in range(2):
        s = table[2 * j + r]
        t = jnp.maximum(s, 0)
        x = ref[t // 8, pl.ds(t % 8, 32, stride=8), :]
        tiles.append(jnp.where(s >= 0, x, empty))
    return pair_up(*tiles)


def load_vector(ref, table, j):
    parts = []
    for c in range(2):
        tiles = []
        for r in range(2):
            s = table[2 * j + r]
            x = ref[jnp.maximum(s, 0), pl.ds(c, 32, stride=2), :]
            tiles.append(jnp.where(s >= 0, x, 0.0))
        parts.append(pair_up(*tiles))
    return parts


def put_columns(acc_ref, x, j):
    mine = ((iota(x.shape, 1) % 64) // 2) == j
    acc_ref[...] = jnp.where(mine, roll(x, 2 * j + 1, 1), acc_ref[...])


def get_columns(acc, j):
    return roll(acc, 128 - (2 * j + 1), 1)


COLUMN_ROWS = (1, 64, 65, 0)


def columns_to_message(acc_ref, turned_ref, message_ref, first, stride):
    turned_ref[...] = acc_ref[...].T
    for row, source in enumerate(COLUMN_ROWS):
        message_ref[pl.ds(first + row, 32, stride=stride), :] = turned_ref[pl.ds(source, 32, stride=2), :]


def message_to_columns(message_ref, turned_ref, acc_ref, first, stride):
    for row, source in enumerate(COLUMN_ROWS):
        turned_ref[pl.ds(source, 32, stride=2), :] = message_ref[pl.ds(first + row, 32, stride=stride), :]
    acc_ref[...] = turned_ref[...].T


def put_rows(message_ref, x, base):
    for row, source in enumerate((0, 63, 64, 127)):
        message_ref[pl.ds(base + 4 + row, 1), :] = x[source : source + 1, :]


def south_of(x, halo=None):
    even, odd = x[:32], x[32:]
    below = roll(odd, 1, 0)
    if halo is not None:
        below = jnp.where(iota(below.shape, 0) == 0, halo, below)
    return jnp.concatenate([below, even], axis=0)


def north_of(x, halo=None):
    even, odd = x[:32], x[32:]
    above = roll(even, 31, 0)
    if halo is not None:
        above = jnp.where(iota(above.shape, 0) == 31, halo, above)
    return jnp.concatenate([odd, above], axis=0)


def tile_part(y, west, south, turn):
    parts = []
    for c in range(2):
        rows = slice(64 * c, 64 * c + 64)
        x, w, s = y[rows], west[rows], south[rows]
        even, odd = x[:32], x[32:]
        s_even, s_odd = s[:32], s[32:]
        across = w * roll(x, 1, 1) + roll(w * x, 127, 1)
        along = jnp.concatenate(
            [
                s_even * roll(odd, 1, 0) + s_odd * odd,
                s_odd * even + roll(s_even * even, 31, 0),
            ],
            axis=0,
        )
        other = y[64:] if c == 0 else y[:64]
        spin = turn * other
        parts.append(x - across - along - spin if c == 0 else x - across - along + spin)
    return jnp.concatenate(parts, axis=0)


def line_solve(t, weight):
    high = t.astype(BF16)
    low = (t - high.astype(F32)).astype(BF16)
    out = lax.dot_general(
        jnp.concatenate([high, low], axis=1),
        weight,
        (((1,), (0,)), ((), ())),
        preferred_element_type=F32,
    )
    return out[:, :128] + out[:, 128:]


def relax(q, weight, west, south, turn):
    y = line_solve(q, weight)
    for _ in range(2):
        y = y + line_solve(q - tile_part(y, west, south, turn), weight)
    return y


def first_edges(table, u_ref, z_ref, message_ref, acc_v, acc_z, turned):
    def body(j, carry):
        u, v = load_vector(u_ref, table, j)
        z = load_field(z_ref, table, j, 0.0)
        vector = jnp.concatenate([u, v], axis=0)
        visc = jnp.concatenate([z, z], axis=0)
        put_columns(acc_v, vector, j)
        put_columns(acc_z, visc, j)
        put_rows(message_ref, vector, 16 * j)
        put_rows(message_ref, visc, 16 * j + 8)
        return carry

    lax.fori_loop(0, PAIRS, body, 0)
    columns_to_message(acc_v, turned, message_ref, 0, 16)
    columns_to_message(acc_z, turned, message_ref, 8, 16)


def line_weights(table, p_ref, weight_ref, natural):
    low = iota((32, 128), 1) < 64

    def body(j, carry):
        tiles = []
        for r in range(2):
            s = table[2 * j + r]
            t = jnp.maximum(s, 0)
            x = p_ref[t // 8, pl.ds(t % 8, 32, stride=8), :]
            tiles.append(jnp.where(s >= 0, x, 0.0))
        t0, t1 = tiles
        natural[pl.ds(0, 32, stride=2), :] = jnp.where(low, t0, 0.0)
        natural[pl.ds(1, 32, stride=2), :] = jnp.where(low, roll(t0, 64, 1), 0.0)
        natural[pl.ds(64, 32, stride=2), :] = jnp.where(low, 0.0, roll(t1, 64, 1))
        natural[pl.ds(65, 32, stride=2), :] = jnp.where(low, 0.0, t1)
        turned = natural[...].T
        high = turned.astype(BF16)
        rest = (turned - high.astype(F32)).astype(BF16)
        both = jnp.concatenate([high, rest], axis=1)
        weight_ref[j, 0:128, :] = both
        weight_ref[j, 128:256, :] = both
        return carry

    lax.fori_loop(0, PAIRS, body, 0)


def side_masks():
    x = iota((64, 128), 1) % 64
    return x == 0, x == 63


KX = (1.25, 0.25)
KY = (0.25, 1.25)


def first_step(
    table, u_ref, b_ref, a_ref, f_ref, z_ref, halo_ref, weight_ref,
    west_ref, south_ref, turn_ref, diag_ref, r_ref, z0_ref, message_ref, rowcoef_ref, colcoef_ref,
    acc, hv, hz, turned,
):
    message_to_columns(halo_ref, turned, hv, 0, 16)
    message_to_columns(halo_ref, turned, hz, 8, 16)
    at_west, at_east = side_masks()

    def body(j, carry):
        u0 = load_vector(u_ref, table, j)
        b = load_vector(b_ref, table, j)
        a = load_field(a_ref, table, j, 1.0)
        f = load_field(f_ref, table, j, 0.0)
        z = load_field(z_ref, table, j, 0.0)
        side_v = get_columns(hv[...], j)
        side_z = get_columns(hz[0:64, :], j)
        rows = halo_ref[pl.ds(pl.multiple_of(16 * j, 16), 16), :]
        face_w = 0.5 * (z + jnp.where(at_west, side_z, roll(z, 1, 1)))
        face_e = 0.5 * (z + jnp.where(at_east, side_z, roll(z, 127, 1)))
        face_s = 0.5 * (z + south_of(z, rows[12:13]))
        face_n = 0.5 * (z + north_of(z, rows[13:14]))
        scale, diag = [], []
        for c in range(2):
            d = a + KX[c] * (face_w + face_e) + KY[c] * (face_s + face_n)
            diag.append(d)
            scale.append(lax.rsqrt(d))
        turn = f * scale[0] * scale[1]
        rhat, west, south, column, south_row, north_row = [], [], [], [], [], []
        for c in range(2):
            x, s = u0[c], scale[c]
            side = side_v[64 * c : 64 * c + 64]
            x_w = jnp.where(at_west, side, roll(x, 1, 1))
            x_e = jnp.where(at_east, side, roll(x, 127, 1))
            x_s = south_of(x, rows[4 + 2 * c : 5 + 2 * c])
            x_n = north_of(x, rows[5 + 2 * c : 6 + 2 * c])
            spin = -f * u0[1] if c == 0 else f * u0[0]
            applied = (
                diag[c] * x + spin
                - KX[c] * (face_w * x_w + face_e * x_e)
                - KY[c] * (face_s * x_s + face_n * x_n)
            )
            rhat.append(s * (b[c] - applied))
            k_w = KX[c] * s * face_w
            k_e = KX[c] * s * face_e
            k_s = KY[c] * s * face_s
            west.append(jnp.where(at_west, 0.0, k_w * roll(s, 1, 1)))
            south.append(k_s * south_of(s, jnp.zeros((1, 128), F32)))
            column.append(jnp.where(at_west, k_w, k_e))
            south_row.append(k_s[0:1])
            north_row.append(KY[c] * s[63:64] * face_n[63:64])
        rhat = jnp.concatenate(rhat, axis=0)
        west = jnp.concatenate(west, axis=0)
        south = jnp.concatenate(south, axis=0)
        put_columns(colcoef_ref, jnp.concatenate(column, axis=0), j)
        for c in range(2):
            rowcoef_ref[pl.ds(8 * j + 4 + 2 * c, 1), :] = south_row[c]
            rowcoef_ref[pl.ds(8 * j + 5 + 2 * c, 1), :] = north_row[c]
        west_ref[j] = west
        south_ref[j] = south
        turn_ref[j] = turn
        diag_ref[j] = jnp.concatenate(diag, axis=0)
        r_ref[j] = rhat
        y = relax(rhat, weight_ref[j], west, south, turn)
        z0 = jnp.concatenate(scale, axis=0) * y
        z0_ref[j] = z0
        put_columns(acc, z0, j)
        put_rows(message_ref, z0, 8 * j)
        return carry

    lax.fori_loop(0, PAIRS, body, 0)
    columns_to_message(acc, turned, message_ref, 0, 8)


def second_step(
    west_ref, south_ref, turn_ref, diag_ref, r_ref, z0_ref, rowcoef_ref, colcoef_ref, halo_ref, weight_ref,
    z1_ref, message_ref, sums_ref,
    acc_z, acc_p, acc_r, acc_d, hv, turned,
):
    message_to_columns(halo_ref, turned, hv, 0, 8)
    hv[...] = hv[...] * colcoef_ref[...]
    lane = iota((128, 128), 1) % 64
    at_side = (lane == 0) | (lane == 63)
    sums_ref[...] = jnp.zeros((6, 8, 128), F32)

    def body(j, carry):
        west, south, turn = west_ref[j], south_ref[j], turn_ref[j]
        diag = diag_ref[j]
        scale = lax.rsqrt(diag)
        root = diag * scale
        rhat = r_ref[j]
        y0 = root * z0_ref[j]
        what = tile_part(y0, west, south, turn)
        what = what - jnp.where(at_side, get_columns(hv[...], j), 0.0)
        base = pl.multiple_of(8 * j, 8)
        rows = halo_ref[pl.ds(base, 8), :] * rowcoef_ref[pl.ds(base, 8), :]
        fixed = []
        first, last = iota((8, 128), 0) == 0, iota((8, 128), 0) == 7
        for c in range(2):
            part = what[64 * c : 64 * c + 64]
            low = part[:8] - jnp.where(first, rows[4 + 2 * c : 5 + 2 * c], 0.0)
            high = part[56:] - jnp.where(last, rows[5 + 2 * c : 6 + 2 * c], 0.0)
            fixed += [low, part[8:56], high]
        what = jnp.concatenate(fixed, axis=0)
        dhat = what - rhat
        y1 = relax(dhat, weight_ref[j], west, south, turn)
        phat = tile_part(y1, west, south, turn) - dhat
        z1 = scale * y1
        z1_ref[j] = z1
        r, d, p = root * rhat, root * dhat, root * phat
        for index, (left, right) in enumerate(((r, r), (r, d), (d, d), (r, p), (d, p), (p, p))):
            product = left * right
            total = product[0:8]
            for k in range(1, 16):
                total = total + product[8 * k : 8 * k + 8]
            sums_ref[index] += total
        for k, (acc, x) in enumerate(((acc_z, z1), (acc_p, p), (acc_r, r), (acc_d, d))):
            put_columns(acc, x, j)
            put_rows(message_ref, x, 32 * j + 8 * k)
        return carry

    lax.fori_loop(0, PAIRS, body, 0)
    for k, acc in enumerate((acc_z, acc_p, acc_r, acc_d)):
        columns_to_message(acc, turned, message_ref, 8 * k, 32)


def to_normal(x, r):
    row = iota((8, 128), 0)
    return jnp.where(r == 1, jnp.where(row < 4, roll(x, 6, 0), roll(x, 64, 1)), x)


def halo_of(west, east, south, north):
    row = iota((8, 128), 0)
    side = jnp.where(row == 0, roll(west, 7, 0), roll(east, 1, 0))
    end = jnp.where(row % 2 == 0, roll(south, 7, 0), roll(north, 1, 0))
    return jnp.where(row < 2, side, jnp.where(row >= 4, end, 0.0))


def collect(count, arrival, received_ref, tiles_ref, west_ref, east_ref, south_ref, north_ref):
    outgoing = west_ref.shape[1] // 8
    for t in range(TILES):
        at = arrival[t]
        for k in range(count):
            x = received_ref[at // 2, 8 * k : 8 * k + 8, :]
            x = to_normal(x, at % 2)
            tiles_ref[t, 8 * k : 8 * k + 8, :] = x
            if k < outgoing:
                rows = slice(8 * k, 8 * k + 8)
                if t % 8 == 0:
                    west_ref[t // 8, rows, :] = x
                if t % 8 == 7:
                    east_ref[t // 8, rows, :] = x
                if t // 8 == 0:
                    south_ref[t % 8, rows, :] = x
                if t // 8 == 3:
                    north_ref[t % 8, rows, :] = x


def tile_halo(t, rows, tiles_ref, from_west, from_east, from_south, from_north):
    ty, tx = t // 8, t % 8
    return halo_of(
        tiles_ref[t - 1, rows, :] if tx > 0 else from_west[ty, rows, :],
        tiles_ref[t + 1, rows, :] if tx < 7 else from_east[ty, rows, :],
        tiles_ref[t - 8, rows, :] if ty > 0 else from_south[tx, rows, :],
        tiles_ref[t + 8, rows, :] if ty < 3 else from_north[tx, rows, :],
    )


def hand_back(arrival, t, k, halo, out_ref):
    at = arrival[t]
    r = at % 2
    row, lane = iota((8, 128), 0), iota((8, 128), 1)
    placed = jnp.where(r == 1, jnp.where(row < 4, roll(halo, 2, 0), roll(halo, 64, 1)), halo)
    mine = ((row < 4) & (row // 2 == r)) | ((row >= 4) & (lane // 64 == r))
    rows = slice(8 * k, 8 * k + 8)
    out_ref[at // 2, rows, :] += jnp.where(mine, placed, 0.0)


def first_return(arrival, tiles_ref, west, east, south, north, out_ref, face_ref):
    row, lane = iota((8, 128), 0), iota((8, 128), 1)
    along_x = jnp.where(lane < 64, KX[0], KX[1])
    along_y = jnp.where(row < 6, KY[0], KY[1])
    factor = 0.5 * jnp.where(row < 4, along_x, along_y)
    out_ref[...] = jnp.zeros(out_ref.shape, F32)
    for t in range(TILES):
        for k in range(2):
            rows = slice(8 * k, 8 * k + 8)
            halo = tile_halo(t, rows, tiles_ref, west, east, south, north)
            hand_back(arrival, t, k, halo, out_ref)
            if k == 1:
                face_ref[t] = factor * (tiles_ref[t, rows, :] + halo)


def second_return(arrival, tiles_ref, west, east, south, north, out_ref):
    out_ref[...] = jnp.zeros(out_ref.shape, F32)
    for t in range(TILES):
        halo = tile_halo(t, slice(0, 8), tiles_ref, west, east, south, north)
        hand_back(arrival, t, 0, halo, out_ref)


def edge_sums(tiles_ref, west, east, south, north, face_ref, sums_ref, out_ref):
    row, lane = iota((8, 128), 0), iota((8, 128), 1)
    valid = (row < 2) | ((row >= 4) & (lane < 64))
    total_r = jnp.zeros((8, 128), F32)
    total_d = jnp.zeros((8, 128), F32)
    total_p = jnp.zeros((8, 128), F32)
    for t in range(TILES):
        halo = tile_halo(t, slice(0, 8), tiles_ref, west, east, south, north)
        h = jnp.where(valid, -face_ref[t] * halo, 0.0)
        p, r, d = tiles_ref[t, 8:16, :], tiles_ref[t, 16:24, :], tiles_ref[t, 24:32, :]
        total_r = total_r + jnp.where(valid, h * r, 0.0)
        total_d = total_d + jnp.where(valid, h * d, 0.0)
        wide_w = jnp.broadcast_to(h[0:1], (8, 128))
        wide_e = jnp.broadcast_to(h[1:2], (8, 128))
        corner_w = jnp.where(
            row == 4, wide_w,
            jnp.where(row == 5, roll(wide_w, 65, 1), jnp.where(row == 6, roll(wide_w, 64, 1), roll(wide_w, 1, 1))),
        )
        corner_e = jnp.where(
            row == 4, roll(wide_e, 63, 1),
            jnp.where(row == 5, wide_e, jnp.where(row == 6, roll(wide_e, 127, 1), roll(wide_e, 64, 1))),
        )
        corner = jnp.where(lane == 0, corner_w, jnp.where(lane == 63, corner_e, 0.0))
        corner = jnp.where(row >= 4, corner, 0.0)
        total_p = total_p + jnp.where(valid, h * (2.0 * (p + corner) + h), 0.0)
    lane = iota((1, 128), 1)
    out = jnp.zeros((1, 128), F32)
    for index in range(6):
        total = sums_ref[index]
        if index == 3:
            total = total + total_r
        if index == 4:
            total = total + total_d
        if index == 5:
            total = total + total_p
        value = jnp.sum(jnp.sum(total, axis=0, keepdims=True), axis=1, keepdims=True)
        out = jnp.where(lane == index, value, out)
    out_ref[...] = jnp.broadcast_to(out, (128, 128))


def least_squares(magnitude, upper_first, below_first, upper_cross, upper_second, below_second):
    radius_first = jnp.sqrt(upper_first * upper_first + below_first * below_first)
    cosine_first = upper_first / radius_first
    sine_first = below_first / radius_first
    lifted_top = cosine_first * upper_cross + sine_first * upper_second
    lifted_low = cosine_first * upper_second - sine_first * upper_cross
    radius_second = jnp.sqrt(lifted_low * lifted_low + below_second * below_second)
    weight_second = -(sine_first * magnitude) * (lifted_low / radius_second) / radius_second
    weight_first = (cosine_first * magnitude - lifted_top * weight_second) / radius_first
    return (weight_first, weight_second)


def final_weights(gathered):
    total = jnp.sum(gathered, axis=0, keepdims=True)
    lane = iota((1, 128), 1)
    rr, rd, dd, re, de, ee = [
        jnp.sum(jnp.where(lane == index, total, 0.0), axis=1, keepdims=True) for index in range(6)
    ]
    square = rr + EPSILON
    magnitude = jnp.sqrt(square)
    h11 = (rr + rd) / square
    gap = -(rd - EPSILON) / square
    h21_square = jnp.maximum((dd + 2.0 * gap * rd + gap * gap * rr) / square, 0.0) + EPSILON
    h21 = jnp.sqrt(h21_square)
    unit = 1.0 / (magnitude * h21)
    h12 = (gap * rr + (1.0 + gap) * rd + re) * unit / magnitude
    h22 = (
        gap * (gap * rr + rd) + (1.0 + gap) * (gap * rd + dd) + (gap * re + de)
    ) * unit * unit
    c_r = gap * unit - h12 / magnitude - h22 * gap * unit
    c_d = (1.0 + gap - h22) * unit
    c_e = unit
    h32_square = (
        c_r * c_r * rr + c_d * c_d * dd + c_e * c_e * ee
        + 2.0 * (c_r * c_d * rd + c_r * c_e * re + c_d * c_e * de)
    )
    h32 = jnp.sqrt(jnp.maximum(h32_square, 0.0) + EPSILON)
    y1, y2 = least_squares(magnitude, h11, h21, h12, h22, h32)
    return y1 / magnitude + y2 * gap * unit, y2 * unit


def last_step(table, gathered_ref, u_ref, z0_ref, z1_ref, out_ref):
    weight0, weight1 = final_weights(gathered_ref[...])
    out_ref[...] = jnp.zeros(out_ref.shape, F32)

    def body(j, carry):
        change = weight0 * z0_ref[j] + weight1 * z1_ref[j]
        for c in range(2):
            for r, x in enumerate(split_up(change[64 * c : 64 * c + 64])):
                s = table[2 * j + r]

                @pl.when(s >= 0)
                def _():
                    rows = pl.ds(c, 32, stride=2)
                    out_ref[s, rows, :] = u_ref[s, rows, :] + x

        return carry

    lax.fori_loop(0, PAIRS, body, 0)


def call(kernel, outs, specs, scratch=()):
    return pl.pallas_call(
        kernel,
        out_shape=outs,
        in_specs=specs,
        out_specs=jax.tree.map(lambda _: vmem(), outs),
        scratch_shapes=list(scratch),
        compiler_params=params(),
    )


def square(rows=128):
    return pltpu.VMEM((rows, 128), F32)


def vector_view(x):
    return x.reshape(64, 2, 32, 128).transpose(0, 2, 1, 3).reshape(64, 64, 128)


def field_view(x):
    return x.reshape(8, 8, 32, 128).transpose(0, 2, 1, 3).reshape(8, 256, 128)


def exchange(x):
    return lax.all_to_all(x, "dev", split_axis=0, concat_axis=0, tiled=True)


def shifted(west, east, south, north):
    dev, grp = lax.axis_size("dev"), lax.axis_size("grp")
    up_dev = [(i, i + 1) for i in range(dev - 1)]
    up_grp = [(i, i + 1) for i in range(grp - 1)]
    return (
        lax.ppermute(east, "dev", up_dev),
        lax.ppermute(west, "dev", [(j, i) for i, j in up_dev]),
        lax.ppermute(north, "grp", up_grp),
        lax.ppermute(south, "grp", [(j, i) for i, j in up_grp]),
    )


def collected(received, arrival, count, outgoing):
    outs = (
        struct(TILES, 8 * count, 128),
        struct(4, 8 * outgoing, 128),
        struct(4, 8 * outgoing, 128),
        struct(8, 8 * outgoing, 128),
        struct(8, 8 * outgoing, 128),
    )

    def kernel(*refs):
        collect(count, *refs)

    tiles, west, east, south, north = call(kernel, outs, [smem(), vmem()])(arrival, received)
    return (tiles,) + shifted(west, east, south, north)


def shards(velocity, forcing, mass, coriolis, viscosity, lines, tile_source_slot, ocean_tile):
    slots = jnp.arange(SLOTS)
    occupied = ocean_tile >= 0
    target = ocean_tile // TILES % PAIRS
    earlier = (
        (target[None, :] == target[:, None])
        & (ocean_tile[None, :] < ocean_tile[:, None])
        & occupied[None, :]
    )
    position = jnp.where(
        occupied, target * 2 + jnp.sum(earlier.astype(jnp.int32), axis=1), -1
    )
    table = jnp.max(jnp.where(position[None, :] == slots[:, None], slots[None, :], -1), axis=1)
    owner = tile_source_slot // SLOTS % PAIRS
    order = jnp.arange(TILES)
    sooner = (owner[None, :] == owner[:, None]) & (order[None, :] < order[:, None])
    arrival = owner * 2 + jnp.sum(sooner.astype(jnp.int32), axis=1)

    u, b = vector_view(velocity), vector_view(forcing)
    a, f, z, p = [field_view(x) for x in (mass, coriolis, viscosity, lines)]

    message = call(
        first_edges, struct(PAIRS * 16, 128), [smem(), vmem(), vmem()], [square(), square(), square()]
    )(table, u, z)
    weight = call(
        line_weights, struct(PAIRS, 256, 256, dtype=BF16), [smem(), vmem()], [square()]
    )(table, p)
    landed = collected(exchange(message.reshape(PAIRS, 16, 128)), arrival, 2, 2)
    halo, face = call(
        first_return, (struct(PAIRS, 16, 128), struct(TILES, 8, 128)), [smem()] + [vmem()] * 5
    )(arrival, *landed)
    halo = exchange(halo).reshape(PAIRS * 16, 128)

    whole = struct(PAIRS, 128, 128)
    west, south, turn, diag, r, z0, message, rowcoef, colcoef = call(
        first_step,
        (
            whole, whole, struct(PAIRS, 64, 128), whole, whole, whole,
            struct(PAIRS * 8, 128), struct(PAIRS * 8, 128), struct(128, 128),
        ),
        [smem()] + [vmem()] * 7,
        [square(), square(), square(), square()],
    )(table, u, b, a, f, z, halo, weight)
    landed = collected(exchange(message.reshape(PAIRS, 8, 128)), arrival, 1, 1)
    halo = call(second_return, struct(PAIRS, 8, 128), [smem()] + [vmem()] * 5)(arrival, *landed)
    halo = exchange(halo).reshape(PAIRS * 8, 128)

    z1, message, sums = call(
        second_step,
        (whole, struct(PAIRS * 32, 128), struct(6, 8, 128)),
        [vmem()] * 10,
        [square() for _ in range(6)],
    )(west, south, turn, diag, r, z0, rowcoef, colcoef, halo, weight)
    landed = collected(exchange(message.reshape(PAIRS, 32, 128)), arrival, 4, 1)
    partial = call(edge_sums, struct(128, 128), [vmem()] * 7)(*landed, face, sums)
    gathered = lax.all_to_all(partial, ("grp", "dev"), split_axis=0, concat_axis=0, tiled=True)

    out = call(last_step, struct(SLOTS, 64, 128), [smem()] + [vmem()] * 4)(table, gathered, u, z0, z1)
    return out.reshape(64, 32, 2, 128).transpose(0, 2, 1, 3).reshape(64, 2, 4096)


def solution(mesh):
    return jax.shard_map(
        shards,
        mesh=mesh,
        in_specs=(
            P(("grp", "dev"), None, None),
            P(("grp", "dev"), None, None),
            P(("grp", "dev"), None),
            P(("grp", "dev"), None),
            P(("grp", "dev"), None),
            P(("grp", "dev"), None),
            P(("grp", "dev")),
            P(("grp", "dev")),
        ),
        out_specs=P(("grp", "dev"), None, None),
        check_vma=False,
    )
```

time: 871 us -> 248 us (0.28); the launches traced: 857 us -> 247 us
  blocking collectives: 334 us -> 68 us
  local copies, waits for them, and re-layouts: 179 us -> 3.28 us
  waiting for transfers between devices: 140 us -> 18.2 us
  Pallas kernels: 0 us -> 107 us
  other arithmetic: 81.1 us -> 4.46 us
  matrix products: 56.4 us -> 0 us
  starting transfers between devices: 58 us -> 46.1 us
    psum x5 -> x0, blocking collectives: 334 us -> none  [the longest x3 199 us: length(): lax.psum(jnp.sum(values * values), ('grp', 'dev')) + EPSILON]
    all_to_all x2, waiting for transfers between devices: 125 us -> 8.07 us  [exchange(): return lax.all_to_all(x, 'dev', split_axis=0, concat_axis=0, tiled=True)]
    pallas_call x0 -> x11, Pallas kernels: none -> 107 us  [the longest x1 35.1 us: shards(): call(first_step, (whole, whole, struct(PAIRS, 64, 128), whole, whole, who...]
    all_to_all x0 -> x4, blocking collectives: none -> 68 us  [the longest x3 46.9 us: exchange(): return lax.all_to_all(x, 'dev', split_axis=0, concat_axis=0, tiled=True)]
    dot_general x6 -> x0, matrix products: 56.4 us -> none  [apply_lines(): jnp.einsum('caybx,abwx->caybw', scaled, line_mats, precision=lax.Precisio...]
    reshape x16 -> x0, local copies, waits for them, and re-layouts: 53 us -> none  [the longest x6 16.7 us: apply_lines(): return output.reshape(2, TR * TILE_SIDE, TC * TILE_SIDE) * scale]
    mul x17 -> x0, other arithmetic: 35.4 us -> none  [the longest x6 15.1 us: apply_lines(): scaled = (scale * source_index).reshape(2, TR, TILE_SIDE, TC, TILE_SIDE)]
    slice x16 -> x0, local copies, waits for them, and re-layouts: 26.7 us -> none  [the longest x2 5.66 us: shards(): forcing_grid = ice_block[2:4]]
  transfers between devices with their start and end apart: 18 -> 14, of which waited for: 8 -> 4; matrix products, arithmetic and copies ran while one was open for 5% -> 0% of each run, Pallas kernels for 0% -> 4%
where the time goes in v1:
time: 248 us; the launch traced here: 247 us
  Pallas kernels  107 us (43%)
  blocking collectives  68 us (27%)
  starting transfers between devices  46.1 us (19%)
  waiting for transfers between devices  18.2 us (7%)
  other arithmetic  4.46 us (2%)
  local copies, waits for them, and re-layouts  3.28 us (1%)
    all_to_all x3, blocking collectives, exchange(): return lax.all_to_all(x, 'dev', split_axis=0, concat_axis=0, tiled=True)  46.9 us
    pallas_call x1, Pallas kernels, shards(): call(first_step, (whole, whole, struct(PAIRS, 64, 128), whole, whole, who...  35.1 us
    pallas_call x1, Pallas kernels, shards(): call(second_step, (whole, struct(PAIRS * 32, 128), struct(6, 8, 128)), [v...  32.6 us
    all_to_all x1, blocking collectives, shards(): lax.all_to_all(partial, ('grp', 'dev'), split_axis=0, concat_axis=0, tile...  21.1 us
    all_to_all x2, starting transfers between devices, exchange(): return lax.all_to_all(x, 'dev', split_axis=0, concat_axis=0, tiled=True)  16.2 us
    ppermute x3, starting transfers between devices, shifted(): lax.ppermute(north, 'grp', up_grp)  12 us
    ppermute x3, waiting for transfers between devices, shifted(): lax.ppermute(west, 'dev', [(j, i) for i, j in up_dev])  10.1 us
    pallas_call x1, Pallas kernels, shards(): call(last_step, struct(SLOTS, 64, 128), [smem()] + [vmem()] * 4)  9.4 us
  transfers between devices with their start and end apart: 14, of which 4 were waited for; matrix products, arithmetic and copies ran while one was open for 0% of the time, Pallas kernels for 4%

profile of v1, /device:TPU:1, one launch (start us, length us, event | category | flops | bytes accessed | tf_op | source)
XLA Modules:
  0.0 246.9 jit_solution(1989413156623925066)
XLA Ops:
  0.0 0.7 broadcast_compare_fusion
  0.7 0.7 and_select_fusion.2
  1.3 0.9 convert_reduce_fusion
  2.3 0.7 add_select_fusion
  2.9 0.7 select_reduce_fusion.table
  3.7 8.3 %shard_map.82 = f32[512,128]{1,0:T(8,128)} custom-call(s32[64]{0:T(128)} %select_reduce_fusion.table, f32[64,64,128]{2,1,0:T(8,128)} %bitcast.44, f32[8,256,128]{2,1,0:T(8,128)} %bitcast.47), custom_call_target="tpu_custom_call" | custom-call | tf_op jit(solution)/shard_map/pallas_call | solution.py:593
  12.0 8.6 %all-to-all-start = ((f32[32,16,128]{2,1,0:T(8,128)}), f32[32,16,128]{2,1,0:T(8,128)S(1)}, u32[]{:S(2)}, u32[]{:S(2)}) async-start(f32[32,16,128]{2,1,0:T(8,128)} %bitcast.53), calls=%async_computation | async-start | bytes 524288 | tf_op jit(solution)/shard_map/all_to_all | solution.py:541
  20.6 0.2 convert_reduce_fusion.1
  20.8 0.6 multiply_add_fusion.refs_0_.arrival
  21.4 8.1 %all-to-all-done.refs_1_ = f32[32,16,128]{2,1,0:T(8,128)S(1)} async-done(((f32[32,16,128]{2,1,0:T(8,128)}), f32[32,16,128]{2,1,0:T(8,128)S(1)}, u32[]{:S(2)}, u32[]{:S(2)}) %all-to-all-start) | async-done | bytes 262176 | tf_op jit(solution)/shard_map/all_to_all | solution.py:541
  29.5 0.7 copy-done.1
  30.2 2.0 shard_map.83
  32.2 3.5 %collective-permute-start.2 = (f32[8,16,128]{2,1,0:T(8,128)}, f32[8,16,128]{2,1,0:T(8,128)S(1)}, u32[]{:S(2)}, u32[]{:S(2)}) collective-permute-start(f32[8,16,128]{2,1,0:T(8,128)} %get-tuple-element.37), channel_id=1, source_target_pairs={{0,32},{32,64},{64,96},{1,33},{33,65},{65,97},{2,34},{34,66},{66,9... | collective-permute-start | bytes 196616 | tf_op jit(solution)/shard_map/ppermute | solution.py:551
  35.7 1.3 collective-permute-start.3
  37.0 2.6 %collective-permute-start = (f32[4,16,128]{2,1,0:T(8,128)}, f32[4,16,128]{2,1,0:T(8,128)S(1)}, u32[]{:S(2)}, u32[]{:S(2)}) collective-permute-start(f32[4,16,128]{2,1,0:T(8,128)} %get-tuple-element.35), channel_id=1, source_target_pairs={{0,1},{1,2},{2,3},{3,4},{4,5},{5,6},{6,7},{7,8},{8,9},{9,10},{10,1... | collective-permute-start | bytes 98312 | tf_op jit(solution)/shard_map/ppermute | solution.py:549
  39.6 1.9 collective-permute-start.1
  41.6 3.5 %collective-permute-done.1.east = f32[4,16,128]{2,1,0:T(8,128)S(1)} collective-permute-done((f32[4,16,128]{2,1,0:T(8,128)}, f32[4,16,128]{2,1,0:T(8,128)S(1)}, u32[]{:S(2)}, u32[]{:S(2)}) %collective-permute-start.1) | collective-permute-done | bytes 32800 | tf_op jit(solution)/shard_map/ppermute | solution.py:550
  45.1 0.6 copy-done.7
  45.7 0.1 copy-done.2
  45.8 2.0 shard_map.84
  47.7 7.6 %all-to-all-start.1 = ((f32[32,16,128]{2,1,0:T(8,128)}), f32[32,16,128]{2,1,0:T(8,128)S(1)}, u32[]{:S(2)}, u32[]{:S(2)}) async-start(f32[32,16,128]{2,1,0:T(8,128)} %get-tuple-element.39), calls=%async_computation.1 | async-start | bytes 524288 | tf_op jit(solution)/shard_map/all_to_all | solution.py:541
  55.3 9.3 %shard_map.85.weight_ref = bf16[32,256,256]{2,1,0:T(8,128)(2,1)} custom-call(s32[64]{0:T(128)} %select_reduce_fusion.table, f32[8,256,128]{2,1,0:T(8,128)} %bitcast.54), custom_call_target="tpu_custom_call" | custom-call | tf_op jit(solution)/shard_map/pallas_call | solution.py:596
  64.6 0.7 copy-done
  65.3 35.1 %shard_map.86 = (f32[32,128,128]{2,1,0:T(8,128)}, f32[32,128,128]{2,1,0:T(8,128)}, f32[32,64,128]{2,1,0:T(8,128)}, f32[32,128,128]{2,1,0:T(8,128)}, f32[32,128,1...) custom-call(s32[64]{0:T(128)} %select_reduce_fusion.table, ...), custom_call_target="tpu_custom_call" | custom-call | tf_op jit(solution)/shard_map/pallas_call | solution.py:606
  100.5 15.1 %all_to_all.36.refs_1_ = f32[32,8,128]{2,1,0:T(8,128)} all-to-all(f32[32,8,128]{2,1,0:T(8,128)} %bitcast.59), channel_id=1, replica_groups=mesh['grp'=4,'dev'=32] {'dev'}, dimensions={0} | all-to-all | bytes 262144 | tf_op jit(solution)/shard_map/all_to_all | solution.py:541
  115.6 1.8 shard_map.87
  117.4 4.3 %collective-permute-start.6 = (f32[8,8,128]{2,1,0:T(8,128)}, f32[8,8,128]{2,1,0:T(8,128)S(1)}, u32[]{:S(2)}, u32[]{:S(2)}) collective-permute-start(f32[8,8,128]{2,1,0:T(8,128)} %get-tuple-element.52), channel_id=1, source_target_pairs={{0,32},{32,64},{64,96},{1,33},{33,65},{65,97},{2,34},{34,66},{66,9... | collective-permute-start | bytes 98312 | tf_op jit(solution)/shard_map/ppermute | solution.py:551
  121.7 1.3 collective-permute-start.7
  123.0 2.8 %collective-permute-start.4 = (f32[4,8,128]{2,1,0:T(8,128)}, f32[4,8,128]{2,1,0:T(8,128)S(1)}, u32[]{:S(2)}, u32[]{:S(2)}) collective-permute-start(f32[4,8,128]{2,1,0:T(8,128)} %get-tuple-element.50), channel_id=1, source_target_pairs={{0,1},{1,2},{2,3},{3,4},{4,5},{5,6},{6,7},{7,8},{8,9},{9,10},{10,1... | collective-permute-start | bytes 49160 | tf_op jit(solution)/shard_map/ppermute | solution.py:549
  125.8 1.9 collective-permute-start.5
  127.7 3.3 %collective-permute-done.5.east = f32[4,8,128]{2,1,0:T(8,128)S(1)} collective-permute-done((f32[4,8,128]{2,1,0:T(8,128)}, f32[4,8,128]{2,1,0:T(8,128)S(1)}, u32[]{:S(2)}, u32[]{:S(2)}) %collective-permute-start.5) | collective-permute-done | bytes 16416 | tf_op jit(solution)/shard_map/ppermute | solution.py:550
  131.1 0.6 copy-done.13
  131.7 0.0 copy-done.9
  131.7 1.9 shard_map.88
  133.5 15.5 %all_to_all.37 = f32[32,8,128]{2,1,0:T(8,128)} all-to-all(f32[32,8,128]{2,1,0:T(8,128)} %shard_map.88), channel_id=1, replica_groups=mesh['grp'=4,'dev'=32] {'dev'}, dimensions={0} | all-to-all | bytes 262144 | tf_op jit(solution)/shard_map/all_to_all | solution.py:541
  149.0 32.6 %shard_map.89 = (f32[32,128,128]{2,1,0:T(8,128)}, f32[1024,128]{1,0:T(8,128)}, f32[6,8,128]{2,1,0:T(8,128)}) custom-call(f32[32,128,128]{2,1,0:T(8,128)} %get-tuple-element.40.west_ref, f32[32,128,128]{2,1,0:T(8,128)} %get-tuple-element.41.south_ref, f32[32,64,128]{2,1,0:T(8,128)} %get-tuple-element.42.turn_ref, f32[32,128,128]{2,1,0:T(8,128)} %get-tuple-element.43.diag_ref, ...), custom_call_target="tpu_custom_call" | custom-call | tf_op jit(solution)/shard_map/pallas_call | solution.py:619
  181.6 16.3 %all_to_all.38.refs_1_ = f32[32,32,128]{2,1,0:T(8,128)} all-to-all(f32[32,32,128]{2,1,0:T(8,128)} %bitcast.56), channel_id=1, replica_groups=mesh['grp'=4,'dev'=32] {'dev'}, dimensions={0} | all-to-all | bytes 1048576 | tf_op jit(solution)/shard_map/all_to_all | solution.py:541
  197.9 2.1 shard_map.90
  200.0 4.3 %collective-permute-start.10 = (f32[8,8,128]{2,1,0:T(8,128)}, f32[8,8,128]{2,1,0:T(8,128)S(1)}, u32[]{:S(2)}, u32[]{:S(2)}) collective-permute-start(f32[8,8,128]{2,1,0:T(8,128)} %get-tuple-element.58), channel_id=1, source_target_pairs={{0,32},{32,64},{64,96},{1,33},{33,65},{65,97},{2,34},{34,66},{66,9... | collective-permute-start | bytes 98312 | tf_op jit(solution)/shard_map/ppermute | solution.py:551
  204.3 1.3 collective-permute-start.11
  205.6 2.8 %collective-permute-start.8 = (f32[4,8,128]{2,1,0:T(8,128)}, f32[4,8,128]{2,1,0:T(8,128)S(1)}, u32[]{:S(2)}, u32[]{:S(2)}) collective-permute-start(f32[4,8,128]{2,1,0:T(8,128)} %get-tuple-element.56), channel_id=1, source_target_pairs={{0,1},{1,2},{2,3},{3,4},{4,5},{5,6},{6,7},{7,8},{8,9},{9,10},{10,1... | collective-permute-start | bytes 49160 | tf_op jit(solution)/shard_map/ppermute | solution.py:549
  208.4 1.9 collective-permute-start.9
  210.3 3.3 %collective-permute-done.9.east = f32[4,8,128]{2,1,0:T(8,128)S(1)} collective-permute-done((f32[4,8,128]{2,1,0:T(8,128)}, f32[4,8,128]{2,1,0:T(8,128)S(1)}, u32[]{:S(2)}, u32[]{:S(2)}) %collective-permute-start.9) | collective-permute-done | bytes 16416 | tf_op jit(solution)/shard_map/ppermute | solution.py:550
  213.7 0.6 copy-done.12
  214.2 0.0 copy-done.4
  214.3 2.1 shard_map.91
  216.4 21.1 %all_to_all.39 = f32[128,1,128]{2,1,0:T(1,128)} all-to-all(f32[128,1,128]{2,1,0:T(1,128)} %bitcast.58), channel_id=1, replica_groups=mesh['grp'=4,'dev'=32] {'grp','dev'}, dimensions={0} | all-to-all | bytes 131072 | tf_op jit(solution)/shard_map/all_to_all | solution.py:627
  237.5 9.4 %shard_map.92 = f32[64,64,128]{2,1,0:T(8,128)} custom-call(s32[64]{0:T(128)} %select_reduce_fusion.table, f32[128,128]{1,0:T(8,128)} %bitcast.57, f32[64,64,128]{2,1,0:T(8,128)} %bitcast.46, f32[32,128,128]{2,1,0:T(8,128)} %get-tuple-element.45.z0_ref, f32[32,128,128]{2,1,0:T(8,128)} %get-tuple-element.62.z1_ref), custom_call_target="tpu_custom_call" | custom-call | tf_op jit(solution)/shard_map/pallas_call | solution.py:629
  (33 shorter events, 0.1 us)
Async XLA Ops:
  0.0 20.6 %copy-start.14 = (s32[32]{0:T(128)S(1)}, s32[32]{0:T(128)}, u32[]{:S(2)}) copy-start(s32[32]{0:T(128)} %param.14) | copy-start | bytes 388
  12.0 17.5 %all-to-all-start = ((f32[32,16,128]{2,1,0:T(8,128)}), f32[32,16,128]{2,1,0:T(8,128)S(1)}, u32[]{:S(2)}, u32[]{:S(2)}) async-start(f32[32,16,128]{2,1,0:T(8,128)} %bitcast.53), calls=%async_computation | async-start | bytes 524288 | tf_op jit(solution)/shard_map/all_to_all | solution.py:541
  29.5 0.7 copy-start.1
  32.2 12.9 %collective-permute-start.2 = (f32[8,16,128]{2,1,0:T(8,128)}, f32[8,16,128]{2,1,0:T(8,128)S(1)}, u32[]{:S(2)}, u32[]{:S(2)}) collective-permute-start(f32[8,16,128]{2,1,0:T(8,128)} %get-tuple-element.37), channel_id=1, source_target_pairs={{0,32},{32,64},{64,96},{1,33},{33,65},{65,97},{2,34},{34,66},{66,9... | collective-permute-start | bytes 196616 | tf_op jit(solution)/shard_map/ppermute | solution.py:551
  35.7 9.4 %collective-permute-start.3 = (f32[8,16,128]{2,1,0:T(8,128)}, f32[8,16,128]{2,1,0:T(8,128)S(1)}, u32[]{:S(2)}, u32[]{:S(2)}) collective-permute-start(f32[8,16,128]{2,1,0:T(8,128)} %get-tuple-element.38), channel_id=1, source_target_pairs={{32,0},{64,32},{96,64},{33,1},{65,33},{97,65},{34,2},{66,34},{98,6... | collective-permute-start | bytes 196616 | tf_op jit(solution)/shard_map/ppermute | solution.py:552
  37.0 4.5 %collective-permute-start = (f32[4,16,128]{2,1,0:T(8,128)}, f32[4,16,128]{2,1,0:T(8,128)S(1)}, u32[]{:S(2)}, u32[]{:S(2)}) collective-permute-start(f32[4,16,128]{2,1,0:T(8,128)} %get-tuple-element.35), channel_id=1, source_target_pairs={{0,1},{1,2},{2,3},{3,4},{4,5},{5,6},{6,7},{7,8},{8,9},{9,10},{10,1... | collective-permute-start | bytes 98312 | tf_op jit(solution)/shard_map/ppermute | solution.py:549
  39.6 5.4 %collective-permute-start.1 = (f32[4,16,128]{2,1,0:T(8,128)}, f32[4,16,128]{2,1,0:T(8,128)S(1)}, u32[]{:S(2)}, u32[]{:S(2)}) collective-permute-start(f32[4,16,128]{2,1,0:T(8,128)} %get-tuple-element.36), channel_id=1, source_target_pairs={{1,0},{2,1},{3,2},{4,3},{5,4},{6,5},{7,6},{8,7},{9,8},{10,9},{11,1... | collective-permute-start | bytes 98312 | tf_op jit(solution)/shard_map/ppermute | solution.py:550
  41.6 3.5 %copy-start.6 = (f32[4,16,128]{2,1,0:T(8,128)}, f32[4,16,128]{2,1,0:T(8,128)S(1)}, u32[]{:S(2)}) copy-start(f32[4,16,128]{2,1,0:T(8,128)S(1)} %collective-permute-done.west) | copy-start | bytes 98308
  45.1 0.6 copy-start.7
  45.1 0.7 copy-start.2
  45.1 0.7 copy-start.3
  47.7 16.9 %all-to-all-start.1 = ((f32[32,16,128]{2,1,0:T(8,128)}), f32[32,16,128]{2,1,0:T(8,128)S(1)}, u32[]{:S(2)}, u32[]{:S(2)}) async-start(f32[32,16,128]{2,1,0:T(8,128)} %get-tuple-element.39), calls=%async_computation.1 | async-start | bytes 524288 | tf_op jit(solution)/shard_map/all_to_all | solution.py:541
  64.6 0.7 copy-start
  117.4 13.7 %collective-permute-start.6 = (f32[8,8,128]{2,1,0:T(8,128)}, f32[8,8,128]{2,1,0:T(8,128)S(1)}, u32[]{:S(2)}, u32[]{:S(2)}) collective-permute-start(f32[8,8,128]{2,1,0:T(8,128)} %get-tuple-element.52), channel_id=1, source_target_pairs={{0,32},{32,64},{64,96},{1,33},{33,65},{65,97},{2,34},{34,66},{66,9... | collective-permute-start | bytes 98312 | tf_op jit(solution)/shard_map/ppermute | solution.py:551
  121.7 9.4 %collective-permute-start.7 = (f32[8,8,128]{2,1,0:T(8,128)}, f32[8,8,128]{2,1,0:T(8,128)S(1)}, u32[]{:S(2)}, u32[]{:S(2)}) collective-permute-start(f32[8,8,128]{2,1,0:T(8,128)} %get-tuple-element.53), channel_id=1, source_target_pairs={{32,0},{64,32},{96,64},{33,1},{65,33},{97,65},{34,2},{66,34},{98,6... | collective-permute-start | bytes 98312 | tf_op jit(solution)/shard_map/ppermute | solution.py:552
  123.0 4.8 %collective-permute-start.4 = (f32[4,8,128]{2,1,0:T(8,128)}, f32[4,8,128]{2,1,0:T(8,128)S(1)}, u32[]{:S(2)}, u32[]{:S(2)}) collective-permute-start(f32[4,8,128]{2,1,0:T(8,128)} %get-tuple-element.50), channel_id=1, source_target_pairs={{0,1},{1,2},{2,3},{3,4},{4,5},{5,6},{6,7},{7,8},{8,9},{9,10},{10,1... | collective-permute-start | bytes 49160 | tf_op jit(solution)/shard_map/ppermute | solution.py:549
  125.8 5.3 %collective-permute-start.5 = (f32[4,8,128]{2,1,0:T(8,128)}, f32[4,8,128]{2,1,0:T(8,128)S(1)}, u32[]{:S(2)}, u32[]{:S(2)}) collective-permute-start(f32[4,8,128]{2,1,0:T(8,128)} %get-tuple-element.51), channel_id=1, source_target_pairs={{1,0},{2,1},{3,2},{4,3},{5,4},{6,5},{7,6},{8,7},{9,8},{10,9},{11,1... | collective-permute-start | bytes 49160 | tf_op jit(solution)/shard_map/ppermute | solution.py:550
  127.7 3.4 %copy-start.11 = (f32[4,8,128]{2,1,0:T(8,128)}, f32[4,8,128]{2,1,0:T(8,128)S(1)}, u32[]{:S(2)}) copy-start(f32[4,8,128]{2,1,0:T(8,128)S(1)} %collective-permute-done.4.west) | copy-start | bytes 49156
  131.0 0.6 copy-start.13
  131.1 0.6 copy-start.8
  131.1 0.6 copy-start.9
  200.0 13.6 %collective-permute-start.10 = (f32[8,8,128]{2,1,0:T(8,128)}, f32[8,8,128]{2,1,0:T(8,128)S(1)}, u32[]{:S(2)}, u32[]{:S(2)}) collective-permute-start(f32[8,8,128]{2,1,0:T(8,128)} %get-tuple-element.58), channel_id=1, source_target_pairs={{0,32},{32,64},{64,96},{1,33},{33,65},{65,97},{2,34},{34,66},{66,9... | collective-permute-start | bytes 98312 | tf_op jit(solution)/shard_map/ppermute | solution.py:551
  204.3 9.4 %collective-permute-start.11 = (f32[8,8,128]{2,1,0:T(8,128)}, f32[8,8,128]{2,1,0:T(8,128)S(1)}, u32[]{:S(2)}, u32[]{:S(2)}) collective-permute-start(f32[8,8,128]{2,1,0:T(8,128)} %get-tuple-element.59), channel_id=1, source_target_pairs={{32,0},{64,32},{96,64},{33,1},{65,33},{97,65},{34,2},{66,34},{98,6... | collective-permute-start | bytes 98312 | tf_op jit(solution)/shard_map/ppermute | solution.py:552
  205.6 4.7 %collective-permute-start.8 = (f32[4,8,128]{2,1,0:T(8,128)}, f32[4,8,128]{2,1,0:T(8,128)S(1)}, u32[]{:S(2)}, u32[]{:S(2)}) collective-permute-start(f32[4,8,128]{2,1,0:T(8,128)} %get-tuple-element.56), channel_id=1, source_target_pairs={{0,1},{1,2},{2,3},{3,4},{4,5},{5,6},{6,7},{7,8},{8,9},{9,10},{10,1... | collective-permute-start | bytes 49160 | tf_op jit(solution)/shard_map/ppermute | solution.py:549
  208.4 5.3 %collective-permute-start.9 = (f32[4,8,128]{2,1,0:T(8,128)}, f32[4,8,128]{2,1,0:T(8,128)S(1)}, u32[]{:S(2)}, u32[]{:S(2)}) collective-permute-start(f32[4,8,128]{2,1,0:T(8,128)} %get-tuple-element.57), channel_id=1, source_target_pairs={{1,0},{2,1},{3,2},{4,3},{5,4},{6,5},{7,6},{8,7},{9,8},{10,9},{11,1... | collective-permute-start | bytes 49160 | tf_op jit(solution)/shard_map/ppermute | solution.py:550
  210.3 3.4 %copy-start.10 = (f32[4,8,128]{2,1,0:T(8,128)}, f32[4,8,128]{2,1,0:T(8,128)S(1)}, u32[]{:S(2)}) copy-start(f32[4,8,128]{2,1,0:T(8,128)S(1)} %collective-permute-done.8.west) | copy-start | bytes 49156
  213.6 0.6 copy-start.12
  213.6 0.6 copy-start.4
  213.6 0.6 copy-start.5

commit v2 on v1

v2 whole, which is shorter than its diff:
```python
import jax
import jax.numpy as jnp
from jax import lax
from jax.experimental import pallas as pl
from jax.experimental.pallas import tpu as pltpu
from jax.sharding import PartitionSpec as P

F32 = jnp.float32
BF16 = jnp.bfloat16
SLOTS = 64
PAIRS = 32
TILES = 32
CHUNK = 4
CHUNKS = PAIRS // CHUNK
TABLE = 72
CODES = 144
STATE = 704
EPSILON = 1e-06
VMEM_LIMIT = 56 * 1024 * 1024


def params():
    return pltpu.CompilerParams(vmem_limit_bytes=VMEM_LIMIT)


def vmem():
    return pl.BlockSpec(memory_space=pltpu.VMEM)


def smem():
    return pl.BlockSpec(memory_space=pltpu.SMEM)


def struct(*shape, dtype=F32):
    return jax.ShapeDtypeStruct(shape, dtype)


def iota(shape, dim):
    return lax.broadcasted_iota(jnp.int32, shape, dim)


def roll(x, shift, axis):
    return pltpu.roll(x, shift, axis)


def pair_up(t0, t1):
    low = iota(t0.shape, 1) < 64
    return jnp.concatenate(
        [jnp.where(low, t0, roll(t1, 64, 1)), jnp.where(low, roll(t0, 64, 1), t1)], axis=0
    )


def split_up(q):
    even, odd = q[:32], q[32:]
    low = iota(even.shape, 1) < 64
    return (
        jnp.where(low, even, roll(odd, 64, 1)),
        jnp.where(low, roll(even, 64, 1), odd),
    )


def load_field(ref, table, j, empty):
    tiles = []
    for r in range(2):
        s = table[2 * j + r]
        t = jnp.maximum(s, 0)
        x = ref[t // 8, pl.ds(t % 8, 32, stride=8), :]
        tiles.append(jnp.where(s >= 0, x, empty))
    return pair_up(*tiles)


def load_vector(ref, table, j):
    parts = []
    for c in range(2):
        tiles = []
        for r in range(2):
            s = table[2 * j + r]
            x = ref[jnp.maximum(s, 0), pl.ds(c, 32, stride=2), :]
            tiles.append(jnp.where(s >= 0, x, 0.0))
        parts.append(pair_up(*tiles))
    return parts


def put_columns(acc_ref, x, j):
    mine = ((iota(x.shape, 1) % 64) // 2) == j
    acc_ref[...] = jnp.where(mine, roll(x, 2 * j + 1, 1), acc_ref[...])


def get_columns(acc, j):
    return roll(acc, 128 - (2 * j + 1), 1)


COLUMN_ROWS = (1, 64, 65, 0)


def columns_to_message(acc_ref, turned_ref, message_ref, first, stride):
    turned_ref[...] = acc_ref[...].T
    for row, source in enumerate(COLUMN_ROWS):
        message_ref[pl.ds(first + row, 32, stride=stride), :] = turned_ref[pl.ds(source, 32, stride=2), :]


def message_to_columns(message_ref, turned_ref, acc_ref, first, stride):
    for row, source in enumerate(COLUMN_ROWS):
        turned_ref[pl.ds(source, 32, stride=2), :] = message_ref[pl.ds(first + row, 32, stride=stride), :]
    acc_ref[...] = turned_ref[...].T


def put_rows(message_ref, x, base):
    for row, source in enumerate((0, 63, 64, 127)):
        message_ref[pl.ds(base + 4 + row, 1), :] = x[source : source + 1, :]


def south_of(x, halo=None):
    even, odd = x[:32], x[32:]
    below = roll(odd, 1, 0)
    if halo is not None:
        below = jnp.where(iota(below.shape, 0) == 0, halo, below)
    return jnp.concatenate([below, even], axis=0)


def north_of(x, halo=None):
    even, odd = x[:32], x[32:]
    above = roll(even, 31, 0)
    if halo is not None:
        above = jnp.where(iota(above.shape, 0) == 31, halo, above)
    return jnp.concatenate([odd, above], axis=0)


def tile_part(y, west, south, turn):
    parts = []
    for c in range(2):
        rows = slice(64 * c, 64 * c + 64)
        x, w, s = y[rows], west[rows], south[rows]
        even, odd = x[:32], x[32:]
        s_even, s_odd = s[:32], s[32:]
        across = w * roll(x, 1, 1) + roll(w * x, 127, 1)
        along = jnp.concatenate(
            [
                s_even * roll(odd, 1, 0) + s_odd * odd,
                s_odd * even + roll(s_even * even, 31, 0),
            ],
            axis=0,
        )
        other = y[64:] if c == 0 else y[:64]
        spin = turn * other
        parts.append(x - across - along - spin if c == 0 else x - across - along + spin)
    return jnp.concatenate(parts, axis=0)


def line_solve(t, weight):
    high = t.astype(BF16)
    low = (t - high.astype(F32)).astype(BF16)
    out = lax.dot_general(
        jnp.concatenate([high, low], axis=1),
        weight,
        (((1,), (0,)), ((), ())),
        preferred_element_type=F32,
    )
    return out[:, :128] + out[:, 128:]


def relax(q, weight, west, south, turn):
    y = line_solve(q, weight)
    for _ in range(2):
        y = y + line_solve(q - tile_part(y, west, south, turn), weight)
    return y


NONE = 99
CODE_W = 72


def make_tables(ocean, table, codes):
    def clear(i, carry):
        table[i] = -1
        return carry

    def clear_codes(i, carry):
        codes[i] = NONE
        return carry

    def place(s, carry):
        t = ocean[s]
        j = jnp.where(t >= 0, (t >> 5) & 31, 32)
        held = table[2 * j]
        before = ocean[jnp.maximum(held, 0)]
        keep = (held >= 0) & (before < t)
        table[2 * j] = jnp.where(keep, held, s)
        table[2 * j + 1] = jnp.where(keep, s, held)
        return carry

    def code(p, carry):
        s = table[p]
        t = ocean[jnp.maximum(s, 0)]
        column, row = t & 7, (t >> 3) & 3
        codes[p + 2] = jnp.where((s >= 0) & (column == 7), row, NONE)
        codes[CODE_W + p] = jnp.where((s >= 0) & (column == 0), row + 4, NONE)
        return carry

    lax.fori_loop(0, TABLE, clear, 0, unroll=8)
    lax.fori_loop(0, CODES, clear_codes, 0, unroll=8)
    lax.fori_loop(0, SLOTS, place, 0, unroll=4)
    lax.fori_loop(0, 2 * PAIRS, code, 0, unroll=8)


def put_extras(codes, turned, message_ref, first, stride):
    row = iota((8, 128), 0)

    def body(m, carry):
        before, after = 2 * jnp.maximum(m - 1, 0), 2 * jnp.minimum(m + 1, PAIRS - 1)
        total = jnp.zeros((8, 128), F32)
        for r in range(2):
            east = turned[pl.ds(before + (64, 0)[r], 1), :]
            west = turned[pl.ds(after + (1, 65)[r], 1), :]
            total = jnp.where(row == codes[2 * m + r], east, total)
            total = jnp.where(row == codes[CODE_W + 2 * m + 2 + r], west, total)
        message_ref[pl.ds(pl.multiple_of(m * stride + first, 8), 8), :] = total
        return carry

    lax.fori_loop(0, PAIRS, body, 0, unroll=8)


def chunk(ref, i):
    return ref.at[pl.ds(i * CHUNK, CHUNK)]


def first_edges(
    ocean, u_hbm, z_hbm,
    message_ref, table, codes, pairs_hbm,
    u_ref, z_ref, pairs, acc_v, acc_z, turned, sem_in, sem_out,
):
    copies = [
        pltpu.make_async_copy(u_hbm, u_ref, sem_in.at[0]),
        pltpu.make_async_copy(z_hbm, z_ref, sem_in.at[1]),
    ]
    for copy in copies:
        copy.start()
    make_tables(ocean, table, codes)
    for copy in copies:
        copy.wait()

    def body(i, carry):
        for k in range(CHUNK):
            j = i * CHUNK + k
            u, v = load_vector(u_ref, table, j)
            z = load_field(z_ref, table, j, 0.0)
            vector = jnp.concatenate([u, v], axis=0)
            visc = jnp.concatenate([z, z], axis=0)
            pairs[j, 0:128, :] = vector
            pairs[j, 128:192, :] = z
            put_columns(acc_v, vector, j)
            put_columns(acc_z, visc, j)
            put_rows(message_ref, vector, 32 * j)
            put_rows(message_ref, visc, 32 * j + 8)
        pltpu.make_async_copy(chunk(pairs, i), chunk(pairs_hbm, i), sem_out.at[i]).start()
        return carry

    lax.fori_loop(0, CHUNKS, body, 0)
    columns_to_message(acc_v, turned, message_ref, 0, 32)
    put_extras(codes, turned, message_ref, 16, 32)
    columns_to_message(acc_z, turned, message_ref, 8, 32)
    put_extras(codes, turned, message_ref, 24, 32)
    for i in range(CHUNKS):
        pltpu.make_async_copy(chunk(pairs, i), chunk(pairs_hbm, i), sem_out.at[i]).wait()


def pair_fields(table, b_ref, a_ref, f_ref, out_hbm, pairs, sem):
    def body(i, carry):
        for k in range(CHUNK):
            j = i * CHUNK + k
            bu, bv = load_vector(b_ref, table, j)
            pairs[j, 0:64, :] = bu
            pairs[j, 64:128, :] = bv
            pairs[j, 128:192, :] = load_field(a_ref, table, j, 1.0)
            pairs[j, 192:256, :] = load_field(f_ref, table, j, 0.0)
        pltpu.make_async_copy(chunk(pairs, i), chunk(out_hbm, i), sem.at[i]).start()
        return carry

    lax.fori_loop(0, CHUNKS, body, 0)
    for i in range(CHUNKS):
        pltpu.make_async_copy(chunk(pairs, i), chunk(out_hbm, i), sem.at[i]).wait()


def line_weights(table, p_ref, out_hbm, weight, natural, sem):
    low = iota((32, 128), 1) < 64

    def body(i, carry):
        for k in range(CHUNK):
            j = i * CHUNK + k
            tiles = []
            for r in range(2):
                s = table[2 * j + r]
                t = jnp.maximum(s, 0)
                x = p_ref[t // 8, pl.ds(t % 8, 32, stride=8), :]
                tiles.append(jnp.where(s >= 0, x, 0.0))
            t0, t1 = tiles
            natural[k, pl.ds(0, 32, stride=2), :] = jnp.where(low, t0, 0.0)
            natural[k, pl.ds(1, 32, stride=2), :] = jnp.where(low, roll(t0, 64, 1), 0.0)
            natural[k, pl.ds(64, 32, stride=2), :] = jnp.where(low, 0.0, roll(t1, 64, 1))
            natural[k, pl.ds(65, 32, stride=2), :] = jnp.where(low, 0.0, t1)
            turned = natural[k].T
            high = turned.astype(BF16)
            rest = (turned - high.astype(F32)).astype(BF16)
            both = jnp.concatenate([high, rest], axis=1)
            weight[j, 0:128, :] = both
            weight[j, 128:256, :] = both
        pltpu.make_async_copy(chunk(weight, i), chunk(out_hbm, i), sem.at[i]).start()
        return carry

    lax.fori_loop(0, CHUNKS, body, 0)
    for i in range(CHUNKS):
        pltpu.make_async_copy(chunk(weight, i), chunk(out_hbm, i), sem.at[i]).wait()


def side_masks():
    x = iota((64, 128), 1) % 64
    return x == 0, x == 63


KX = (1.25, 0.25)
KY = (0.25, 1.25)


def first_step(
    codes, halo_ref, pairs_hbm, fields_hbm, weight_hbm,
    state_hbm, message_ref, rowcoef_ref, colcoef_ref,
    pairs, fields, weight, state, acc_z, acc_r, hv, hz, turned, sem_in, sem_out,
):
    def incoming(i):
        return [
            pltpu.make_async_copy(chunk(source, i), chunk(target, i), sem_in.at[n, i])
            for n, (source, target) in enumerate(((pairs_hbm, pairs), (fields_hbm, fields), (weight_hbm, weight)))
        ]

    for i in range(CHUNKS):
        for copy in incoming(i):
            copy.start()
    message_to_columns(halo_ref, turned, hv, 0, 16)
    message_to_columns(halo_ref, turned, hz, 8, 16)
    at_west, at_east = side_masks()

    def one(j):
        u0 = pairs[j, 0:64, :], pairs[j, 64:128, :]
        z = pairs[j, 128:192, :]
        b = fields[j, 0:64, :], fields[j, 64:128, :]
        a, f = fields[j, 128:192, :], fields[j, 192:256, :]
        side_v = get_columns(hv[...], j)
        side_z = get_columns(hz[0:64, :], j)
        rows = halo_ref[pl.ds(pl.multiple_of(16 * j, 16), 16), :]
        face_w = 0.5 * (z + jnp.where(at_west, side_z, roll(z, 1, 1)))
        face_e = 0.5 * (z + jnp.where(at_east, side_z, roll(z, 127, 1)))
        face_s = 0.5 * (z + south_of(z, rows[12:13]))
        face_n = 0.5 * (z + north_of(z, rows[13:14]))
        scale, diag = [], []
        for c in range(2):
            d = a + KX[c] * (face_w + face_e) + KY[c] * (face_s + face_n)
            diag.append(d)
            scale.append(lax.rsqrt(d))
        turn = f * scale[0] * scale[1]
        rhat, west, south, column, plain = [], [], [], [], []
        for c in range(2):
            x, s = u0[c], scale[c]
            side = side_v[64 * c : 64 * c + 64]
            x_w = jnp.where(at_west, side, roll(x, 1, 1))
            x_e = jnp.where(at_east, side, roll(x, 127, 1))
            x_s = south_of(x, rows[4 + 2 * c : 5 + 2 * c])
            x_n = north_of(x, rows[5 + 2 * c : 6 + 2 * c])
            spin = -f * u0[1] if c == 0 else f * u0[0]
            applied = (
                diag[c] * x + spin
                - KX[c] * (face_w * x_w + face_e * x_e)
                - KY[c] * (face_s * x_s + face_n * x_n)
            )
            residual = b[c] - applied
            plain.append(residual)
            rhat.append(s * residual)
            k_w = KX[c] * s * face_w
            k_e = KX[c] * s * face_e
            k_s = KY[c] * s * face_s
            west.append(jnp.where(at_west, 0.0, k_w * roll(s, 1, 1)))
            south.append(k_s * south_of(s, jnp.zeros((1, 128), F32)))
            column.append(jnp.where(at_west, k_w, k_e))
            rowcoef_ref[pl.ds(8 * j + 4 + 2 * c, 1), :] = k_s[0:1]
            rowcoef_ref[pl.ds(8 * j + 5 + 2 * c, 1), :] = KY[c] * s[63:64] * face_n[63:64]
        rhat = jnp.concatenate(rhat, axis=0)
        plain = jnp.concatenate(plain, axis=0)
        west = jnp.concatenate(west, axis=0)
        south = jnp.concatenate(south, axis=0)
        put_columns(colcoef_ref, jnp.concatenate(column, axis=0), j)
        put_columns(acc_r, plain, j)
        put_rows(message_ref, plain, 24 * j + 8)
        state[j, 0:128, :] = west
        state[j, 128:256, :] = south
        state[j, 256:384, :] = jnp.concatenate(diag, axis=0)
        state[j, 384:512, :] = rhat
        state[j, 512:576, :] = turn
        y = relax(rhat, weight[j], west, south, turn)
        z0 = jnp.concatenate(scale, axis=0) * y
        state[j, 576:704, :] = z0
        put_columns(acc_z, z0, j)
        put_rows(message_ref, z0, 24 * j)

    def body(i, carry):
        for copy in incoming(i):
            copy.wait()
        for k in range(CHUNK):
            one(i * CHUNK + k)
        pltpu.make_async_copy(chunk(state, i), chunk(state_hbm, i), sem_out.at[i]).start()
        return carry

    lax.fori_loop(0, CHUNKS, body, 0)
    columns_to_message(acc_r, turned, message_ref, 8, 24)
    columns_to_message(acc_z, turned, message_ref, 0, 24)
    put_extras(codes, turned, message_ref, 16, 24)
    for i in range(CHUNKS):
        pltpu.make_async_copy(chunk(state, i), chunk(state_hbm, i), sem_out.at[i]).wait()


def second_step(
    codes, halo_ref, rowcoef_ref, colcoef_ref, state_hbm, weight_hbm,
    z1_hbm, message_ref, sums_ref,
    state, weight, z1s, acc_z, acc_p, acc_d, hv, turned, sem_in, sem_out,
):
    def incoming(i):
        return [
            pltpu.make_async_copy(chunk(source, i), chunk(target, i), sem_in.at[n, i])
            for n, (source, target) in enumerate(((state_hbm, state), (weight_hbm, weight)))
        ]

    for i in range(CHUNKS):
        for copy in incoming(i):
            copy.start()
    message_to_columns(halo_ref, turned, hv, 0, 8)
    hv[...] = hv[...] * colcoef_ref[...]
    lane = iota((128, 128), 1) % 64
    at_side = (lane == 0) | (lane == 63)
    first, last = iota((8, 128), 0) == 0, iota((8, 128), 0) == 7
    sums_ref[...] = jnp.zeros((6, 8, 128), F32)

    def one(j):
        west, south, turn = state[j, 0:128, :], state[j, 128:256, :], state[j, 512:576, :]
        diag = state[j, 256:384, :]
        rhat = state[j, 384:512, :]
        scale = lax.rsqrt(diag)
        root = diag * scale
        y0 = root * state[j, 576:704, :]
        what = tile_part(y0, west, south, turn)
        what = what - jnp.where(at_side, get_columns(hv[...], j), 0.0)
        base = pl.multiple_of(8 * j, 8)
        rows = halo_ref[pl.ds(base, 8), :] * rowcoef_ref[pl.ds(base, 8), :]
        fixed = []
        for c in range(2):
            part = what[64 * c : 64 * c + 64]
            low = part[:8] - jnp.where(first, rows[4 + 2 * c : 5 + 2 * c], 0.0)
            high = part[56:] - jnp.where(last, rows[5 + 2 * c : 6 + 2 * c], 0.0)
            fixed += [low, part[8:56], high]
        what = jnp.concatenate(fixed, axis=0)
        dhat = what - rhat
        y1 = relax(dhat, weight[j], west, south, turn)
        phat = tile_part(y1, west, south, turn) - dhat
        z1 = scale * y1
        z1s[j] = z1
        r, d, p = root * rhat, root * dhat, root * phat
        for index, (left, right) in enumerate(((r, r), (r, d), (d, d), (r, p), (d, p), (p, p))):
            product = left * right
            total = product[0:8]
            for k in range(1, 16):
                total = total + product[8 * k : 8 * k + 8]
            sums_ref[index] += total
        for k, (acc, x) in enumerate(((acc_z, z1), (acc_p, p), (acc_d, d))):
            put_columns(acc, x, j)
            put_rows(message_ref, x, 32 * j + 8 * k)

    def body(i, carry):
        for copy in incoming(i):
            copy.wait()
        for k in range(CHUNK):
            one(i * CHUNK + k)
        pltpu.make_async_copy(chunk(z1s, i), chunk(z1_hbm, i), sem_out.at[i]).start()
        return carry

    lax.fori_loop(0, CHUNKS, body, 0)
    columns_to_message(acc_p, turned, message_ref, 8, 32)
    columns_to_message(acc_d, turned, message_ref, 16, 32)
    columns_to_message(acc_z, turned, message_ref, 0, 32)
    put_extras(codes, turned, message_ref, 24, 32)
    for i in range(CHUNKS):
        pltpu.make_async_copy(chunk(z1s, i), chunk(z1_hbm, i), sem_out.at[i]).wait()


def to_normal(x, r):
    row = iota((8, 128), 0)
    return jnp.where(r == 1, jnp.where(row < 4, roll(x, 6, 0), roll(x, 64, 1)), x)


def halo_of(west, east, south, north):
    row = iota((8, 128), 0)
    side = jnp.where(row == 0, roll(west, 7, 0), roll(east, 1, 0))
    end = jnp.where(row % 2 == 0, roll(south, 7, 0), roll(north, 1, 0))
    return jnp.where(row < 2, side, jnp.where(row >= 4, end, 0.0))


def tile_block(arrival, received_ref, t, k):
    at = arrival[t]
    return to_normal(received_ref[at // 2, 8 * k : 8 * k + 8, :], at % 2)


def boundary(arrival, received_ref, south_ref, north_ref):
    for k in range(south_ref.shape[1] // 8):
        rows = slice(8 * k, 8 * k + 8)
        for x in range(8):
            south_ref[x, rows, :] = tile_block(arrival, received_ref, x, k)
            north_ref[x, rows, :] = tile_block(arrival, received_ref, 24 + x, k)


def tile_halos(arrival, received_ref, from_south, from_north, k, extra):
    group = lax.axis_index("grp")
    blocks = [tile_block(arrival, received_ref, t, k) for t in range(TILES)]
    sides = received_ref[0, 8 * extra : 8 * extra + 8, :]
    for o in range(1, PAIRS):
        sides = sides + received_ref[o, 8 * extra : 8 * extra + 8, :]
    rows = slice(8 * k, 8 * k + 8)
    last = lax.axis_size("grp") - 1
    below = [jnp.where(group > 0, from_south[x, rows, :], 0.0) for x in range(8)]
    above = [jnp.where(group < last, from_north[x, rows, :], 0.0) for x in range(8)]
    halos = []
    for t in range(TILES):
        ty, tx = t // 8, t % 8
        halos.append(
            halo_of(
                blocks[t - 1] if tx > 0 else roll(sides, (1 - ty) % 8, 0),
                blocks[t + 1] if tx < 7 else roll(sides, 4 - ty, 0),
                blocks[t - 8] if ty > 0 else below[tx],
                blocks[t + 8] if ty < 3 else above[tx],
            )
        )
    return blocks, halos


def hand_back(arrival, t, k, halo, out_ref):
    at = arrival[t]
    r = at % 2
    row, lane = iota((8, 128), 0), iota((8, 128), 1)
    placed = jnp.where(r == 1, jnp.where(row < 4, roll(halo, 2, 0), roll(halo, 64, 1)), halo)
    mine = ((row < 4) & (row // 2 == r)) | ((row >= 4) & (lane // 64 == r))
    rows = slice(8 * k, 8 * k + 8)
    out_ref[at // 2, rows, :] += jnp.where(mine, placed, 0.0)


def first_return(arrival, received_ref, south, north, out_ref, face_ref):
    row, lane = iota((8, 128), 0), iota((8, 128), 1)
    along_x = jnp.where(lane < 64, KX[0], KX[1])
    along_y = jnp.where(row < 6, KY[0], KY[1])
    factor = 0.5 * jnp.where(row < 4, along_x, along_y)
    out_ref[...] = jnp.zeros(out_ref.shape, F32)
    for k in range(2):
        blocks, halos = tile_halos(arrival, received_ref, south, north, k, 2 + k)
        for t in range(TILES):
            hand_back(arrival, t, k, halos[t], out_ref)
            if k == 1:
                face_ref[t] = factor * (blocks[t] + halos[t])


def second_return(arrival, received_ref, south, north, out_ref):
    out_ref[...] = jnp.zeros(out_ref.shape, F32)
    blocks, halos = tile_halos(arrival, received_ref, south, north, 0, 2)
    for t in range(TILES):
        hand_back(arrival, t, 0, halos[t], out_ref)


def edge_sums(arrival, received_ref, south, north, earlier_ref, face_ref, sums_ref, out_ref):
    row, lane = iota((8, 128), 0), iota((8, 128), 1)
    valid = (row < 2) | ((row >= 4) & (lane < 64))
    total_r = jnp.zeros((8, 128), F32)
    total_d = jnp.zeros((8, 128), F32)
    total_p = jnp.zeros((8, 128), F32)
    blocks, halos = tile_halos(arrival, received_ref, south, north, 0, 3)
    for t in range(TILES):
        h = jnp.where(valid, -face_ref[t] * halos[t], 0.0)
        p = tile_block(arrival, received_ref, t, 1)
        d = tile_block(arrival, received_ref, t, 2)
        r = tile_block(arrival, earlier_ref, t, 1)
        total_r = total_r + jnp.where(valid, h * r, 0.0)
        total_d = total_d + jnp.where(valid, h * d, 0.0)
        wide_w = jnp.broadcast_to(h[0:1], (8, 128))
        wide_e = jnp.broadcast_to(h[1:2], (8, 128))
        corner_w = jnp.where(
            row == 4, wide_w,
            jnp.where(row == 5, roll(wide_w, 65, 1), jnp.where(row == 6, roll(wide_w, 64, 1), roll(wide_w, 1, 1))),
        )
        corner_e = jnp.where(
            row == 4, roll(wide_e, 63, 1),
            jnp.where(row == 5, wide_e, jnp.where(row == 6, roll(wide_e, 127, 1), roll(wide_e, 64, 1))),
        )
        corner = jnp.where(lane == 0, corner_w, jnp.where(lane == 63, corner_e, 0.0))
        corner = jnp.where(row >= 4, corner, 0.0)
        total_p = total_p + jnp.where(valid, h * (2.0 * (p + corner) + h), 0.0)
    lane = iota((1, 128), 1)
    out = jnp.zeros((1, 128), F32)
    for index in range(6):
        total = sums_ref[index]
        if index == 3:
            total = total + total_r
        if index == 4:
            total = total + total_d
        if index == 5:
            total = total + total_p
        value = jnp.sum(jnp.sum(total, axis=0, keepdims=True), axis=1, keepdims=True)
        out = jnp.where(lane == index, value, out)
    out_ref[...] = jnp.broadcast_to(out, (128, 128))


def least_squares(magnitude, upper_first, below_first, upper_cross, upper_second, below_second):
    radius_first = jnp.sqrt(upper_first * upper_first + below_first * below_first)
    cosine_first = upper_first / radius_first
    sine_first = below_first / radius_first
    lifted_top = cosine_first * upper_cross + sine_first * upper_second
    lifted_low = cosine_first * upper_second - sine_first * upper_cross
    radius_second = jnp.sqrt(lifted_low * lifted_low + below_second * below_second)
    weight_second = -(sine_first * magnitude) * (lifted_low / radius_second) / radius_second
    weight_first = (cosine_first * magnitude - lifted_top * weight_second) / radius_first
    return (weight_first, weight_second)


def final_weights(gathered):
    total = jnp.sum(gathered, axis=0, keepdims=True)
    lane = iota((1, 128), 1)
    rr, rd, dd, re, de, ee = [
        jnp.sum(jnp.where(lane == index, total, 0.0), axis=1, keepdims=True) for index in range(6)
    ]
    square = rr + EPSILON
    magnitude = jnp.sqrt(square)
    h11 = (rr + rd) / square
    gap = -(rd - EPSILON) / square
    h21_square = jnp.maximum((dd + 2.0 * gap * rd + gap * gap * rr) / square, 0.0) + EPSILON
    h21 = jnp.sqrt(h21_square)
    unit = 1.0 / (magnitude * h21)
    h12 = (gap * rr + (1.0 + gap) * rd + re) * unit / magnitude
    h22 = (
        gap * (gap * rr + rd) + (1.0 + gap) * (gap * rd + dd) + (gap * re + de)
    ) * unit * unit
    c_r = gap * unit - h12 / magnitude - h22 * gap * unit
    c_d = (1.0 + gap - h22) * unit
    c_e = unit
    h32_square = (
        c_r * c_r * rr + c_d * c_d * dd + c_e * c_e * ee
        + 2.0 * (c_r * c_d * rd + c_r * c_e * re + c_d * c_e * de)
    )
    h32 = jnp.sqrt(jnp.maximum(h32_square, 0.0) + EPSILON)
    y1, y2 = least_squares(magnitude, h11, h21, h12, h22, h32)
    return y1 / magnitude + y2 * gap * unit, y2 * unit


def last_step(
    table, gathered_ref, pairs_hbm, state_hbm, z1_hbm,
    out_hbm,
    u, z0, z1, out, sem_in, sem_out,
):
    def incoming(i):
        return [
            pltpu.make_async_copy(source, chunk(target, i), sem_in.at[n, i])
            for n, (source, target) in enumerate(
                (
                    (chunk(pairs_hbm, i).at[:, pl.ds(0, 128)], u),
                    (chunk(state_hbm, i).at[:, pl.ds(576, 128)], z0),
                    (chunk(z1_hbm, i), z1),
                )
            )
        ]

    for i in range(CHUNKS):
        for copy in incoming(i):
            copy.start()
    out[...] = jnp.zeros(out.shape, F32)
    weight0, weight1 = final_weights(gathered_ref[...])

    def body(i, carry):
        for copy in incoming(i):
            copy.wait()
        for k in range(CHUNK):
            j = i * CHUNK + k
            new = u[j] + weight0 * z0[j] + weight1 * z1[j]
            slots = [jnp.where(table[2 * j + r] >= 0, table[2 * j + r], SLOTS) for r in range(2)]
            for c in range(2):
                for r, x in enumerate(split_up(new[64 * c : 64 * c + 64])):
                    out[slots[r], pl.ds(c, 32, stride=2), :] = x
        return carry

    lax.fori_loop(0, CHUNKS, body, 0)
    copy = pltpu.make_async_copy(out.at[pl.ds(0, SLOTS)], out_hbm, sem_out)
    copy.start()
    copy.wait()


def call(kernel, outs, specs, scratch=(), out_specs=None):
    return pl.pallas_call(
        kernel,
        out_shape=outs,
        in_specs=specs,
        out_specs=out_specs if out_specs is not None else jax.tree.map(lambda _: vmem(), outs),
        scratch_shapes=list(scratch),
        compiler_params=params(),
    )


def hbm():
    return pl.BlockSpec(memory_space=pl.ANY)


def square(rows=128):
    return pltpu.VMEM((rows, 128), F32)


def buffer(*shape, dtype=F32):
    return pltpu.VMEM(shape, dtype)


def sems(*shape):
    return pltpu.SemaphoreType.DMA(shape)


def vector_view(x):
    return x.reshape(64, 2, 32, 128).transpose(0, 2, 1, 3).reshape(64, 64, 128)


def field_view(x):
    return x.reshape(8, 8, 32, 128).transpose(0, 2, 1, 3).reshape(8, 256, 128)


def exchange(x):
    return lax.all_to_all(x, "dev", split_axis=0, concat_axis=0, tiled=True)


def from_groups(arrival, received, count):
    side = struct(8, 8 * count, 128)
    south, north = call(boundary, (side, side), [smem(), vmem()])(arrival, received)
    size = lax.axis_size("grp")
    ahead = [(i, (i + 1) % size) for i in range(size)]
    return lax.ppermute(north, "grp", ahead), lax.ppermute(south, "grp", [(j, i) for i, j in ahead])


def shards(velocity, forcing, mass, coriolis, viscosity, lines, tile_source_slot, ocean_tile):
    owner = tile_source_slot // SLOTS % PAIRS
    order = jnp.arange(TILES)
    sooner = (owner[None, :] == owner[:, None]) & (order[None, :] < order[:, None])
    arrival = owner * 2 + jnp.sum(sooner.astype(jnp.int32), axis=1)

    u, b = vector_view(velocity), vector_view(forcing)
    a, f, z, p = [field_view(x) for x in (mass, coriolis, viscosity, lines)]

    message, table, codes, pairs = call(
        first_edges,
        (
            struct(PAIRS * 32, 128), struct(TABLE, dtype=jnp.int32), struct(CODES, dtype=jnp.int32),
            struct(PAIRS, 192, 128),
        ),
        [smem(), hbm(), hbm()],
        [
            buffer(64, 64, 128), buffer(8, 256, 128), buffer(PAIRS, 192, 128),
            square(), square(), square(), sems(2), sems(CHUNKS),
        ],
        (vmem(), smem(), smem(), hbm()),
    )(ocean_tile, u, z)
    weight = call(
        line_weights, struct(PAIRS, 256, 256, dtype=BF16), [smem(), vmem()],
        [buffer(PAIRS, 256, 256, dtype=BF16), buffer(CHUNK, 128, 128), sems(CHUNKS)], hbm(),
    )(table, p)
    fields = call(
        pair_fields, struct(PAIRS, 256, 128), [smem(), vmem(), vmem(), vmem()],
        [buffer(PAIRS, 256, 128), sems(CHUNKS)], hbm(),
    )(table, b, a, f)

    received = exchange(message.reshape(PAIRS, 32, 128))
    halo, face = call(
        first_return, (struct(PAIRS, 16, 128), struct(TILES, 8, 128)), [smem()] + [vmem()] * 3
    )(arrival, received, *from_groups(arrival, received, 2))
    halo = exchange(halo).reshape(PAIRS * 16, 128)

    state, message, rowcoef, colcoef = call(
        first_step,
        (struct(PAIRS, STATE, 128), struct(PAIRS * 24, 128), struct(PAIRS * 8, 128), struct(128, 128)),
        [smem(), vmem(), hbm(), hbm(), hbm()],
        [
            buffer(PAIRS, 192, 128), buffer(PAIRS, 256, 128), buffer(PAIRS, 256, 256, dtype=BF16),
            buffer(PAIRS, STATE, 128), square(), square(), square(), square(), square(),
            sems(3, CHUNKS), sems(CHUNKS),
        ],
        (hbm(), vmem(), vmem(), vmem()),
    )(codes, halo, pairs, fields, weight)
    earlier = exchange(message.reshape(PAIRS, 24, 128))
    halo = call(second_return, struct(PAIRS, 8, 128), [smem()] + [vmem()] * 3)(
        arrival, earlier, *from_groups(arrival, earlier, 1)
    )
    halo = exchange(halo).reshape(PAIRS * 8, 128)

    z1, message, sums = call(
        second_step,
        (struct(PAIRS, 128, 128), struct(PAIRS * 32, 128), struct(6, 8, 128)),
        [smem(), vmem(), vmem(), vmem(), hbm(), hbm()],
        [
            buffer(PAIRS, STATE, 128), buffer(PAIRS, 256, 256, dtype=BF16), buffer(PAIRS, 128, 128),
            square(), square(), square(), square(), square(), sems(2, CHUNKS), sems(CHUNKS),
        ],
        (hbm(), vmem(), vmem()),
    )(codes, halo, rowcoef, colcoef, state, weight)
    received = exchange(message.reshape(PAIRS, 32, 128))
    partial = call(edge_sums, struct(128, 128), [smem()] + [vmem()] * 6)(
        arrival, received, *from_groups(arrival, received, 1), earlier, face, sums
    )
    gathered = lax.all_to_all(partial, ("grp", "dev"), split_axis=0, concat_axis=0, tiled=True)

    out = call(
        last_step, struct(SLOTS, 64, 128), [smem(), vmem(), hbm(), hbm(), hbm()],
        [buffer(PAIRS, 128, 128), buffer(PAIRS, 128, 128), buffer(PAIRS, 128, 128), buffer(SLOTS + 1, 64, 128),
         sems(3, CHUNKS), pltpu.SemaphoreType.DMA],
        hbm(),
    )(table, gathered, pairs, state, z1)
    return out.reshape(64, 32, 2, 128).transpose(0, 2, 1, 3).reshape(64, 2, 4096)


def solution(mesh):
    return jax.shard_map(
        shards,
        mesh=mesh,
        in_specs=(
            P(("grp", "dev"), None, None),
            P(("grp", "dev"), None, None),
            P(("grp", "dev"), None),
            P(("grp", "dev"), None),
            P(("grp", "dev"), None),
            P(("grp", "dev"), None),
            P(("grp", "dev")),
            P(("grp", "dev")),
        ),
        out_specs=P(("grp", "dev"), None, None),
        check_vma=False,
    )
```

time: 248 us -> 176 us (0.71)
  Pallas kernels: 107 us -> 67.1 us
  starting transfers between devices: 46.1 us -> 22.2 us
  other arithmetic: 4.46 us -> 0.7 us
  blocking collectives: 68 us -> 64.4 us
    pallas_call x9 -> x10, Pallas kernels: 95.4 us -> 60.3 us  [the longest x1 16.3 us: shards(): call(second_step, (struct(PAIRS, 128, 128), struct(PAIRS * 32, 128), stru...]
    ppermute x12 -> x6, starting transfers between devices: 29.9 us -> 9.12 us  [the longest x3 5.95 us: from_groups(): lax.ppermute(south, 'grp', [(j, i) for i, j in ahead])]
    pallas_call x1, Pallas kernels: 9.25 us -> 4.1 us  [shards(): call(line_weights, struct(PAIRS, 256, 256, dtype=BF16), [smem(), vmem()],...]
    ppermute x12 -> x6, waiting for transfers between devices: 10.2 us -> 5.31 us  [the longest x3 5.3 us: from_groups(): lax.ppermute(north, 'grp', ahead)]
    all_to_all x1, blocking collectives: 21.1 us -> 16.9 us  [shards(): lax.all_to_all(partial, ('grp', 'dev'), split_axis=0, concat_axis=0, tile...]
    all_to_all x2, starting transfers between devices: 16.2 us -> 13.1 us  [exchange(): return lax.all_to_all(x, 'dev', split_axis=0, concat_axis=0, tiled=True)]
    all_to_all x2, waiting for transfers between devices: 8.07 us -> 10.8 us  [exchange(): return lax.all_to_all(x, 'dev', split_axis=0, concat_axis=0, tiled=True)]
  transfers between devices with their start and end apart: 14 -> 8, of which waited for: 4 -> 4; matrix products, arithmetic and copies ran while one was open for 0% -> 0% of each run, Pallas kernels for 4% -> 5%
where the time goes in v2:
time: 176 us; the launch traced here: 175 us
  Pallas kernels  67.1 us (38%)
  blocking collectives  64.4 us (37%)
  starting transfers between devices  22.2 us (13%)
  waiting for transfers between devices  16.1 us (9%)
  local copies, waits for them, and re-layouts  4.53 us (3%)
    all_to_all x3, blocking collectives, exchange(): return lax.all_to_all(x, 'dev', split_axis=0, concat_axis=0, tiled=True)  47.5 us
    all_to_all x1, blocking collectives, shards(): lax.all_to_all(partial, ('grp', 'dev'), split_axis=0, concat_axis=0, tile...  16.9 us
    pallas_call x1, Pallas kernels, shards(): call(second_step, (struct(PAIRS, 128, 128), struct(PAIRS * 32, 128), stru...  16.3 us
    pallas_call x1, Pallas kernels, shards(): call(first_step, (struct(PAIRS, STATE, 128), struct(PAIRS * 24, 128), str...  16.3 us
    all_to_all x2, starting transfers between devices, exchange(): return lax.all_to_all(x, 'dev', split_axis=0, concat_axis=0, tiled=True)  13.1 us
    all_to_all x2, waiting for transfers between devices, exchange(): return lax.all_to_all(x, 'dev', split_axis=0, concat_axis=0, tiled=True)  10.8 us
    pallas_call x1, Pallas kernels, shards(): call(first_edges, (struct(PAIRS * 32, 128), struct(TABLE, dtype=jnp.int32...  7.2 us
    ppermute x3, starting transfers between devices, from_groups(): lax.ppermute(south, 'grp', [(j, i) for i, j in ahead])  5.95 us
  transfers between devices with their start and end apart: 8, of which 4 were waited for; matrix products, arithmetic and copies ran while one was open for 0% of the time, Pallas kernels for 5%

profile of v2, /device:TPU:1, one launch (start us, length us, event | category | flops | bytes accessed | tf_op | source)
XLA Modules:
  0.0 175.2 jit_solution(3368971221842837502)
XLA Ops:
  0.0 0.0 copy-start.8
  0.0 7.2 %shard_map.82 = (f32[1024,128]{1,0:T(8,128)}, s32[72]{0:T(128)}, s32[144]{0:T(256)}, f32[32,192,128]{2,1,0:T(8,128)}) custom-call(s32[64]{0:T(128)} %ocean.1, f32[64,64,128]{2,1,0:T(8,128)} %bitcast.44, f32[8,256,128]{2,1,0:T(8,128)} %bitcast.49), custom_call_target="tpu_custom_call" | custom-call | tf_op jit(solution)/shard_map/pallas_call | solution.py:751
  7.2 8.6 %all-to-all-start = ((f32[32,32,128]{2,1,0:T(8,128)}), f32[32,32,128]{2,1,0:T(8,128)S(1)}, u32[]{:S(2)}, u32[]{:S(2)}) async-start(f32[32,32,128]{2,1,0:T(8,128)} %bitcast.52), calls=%async_computation | async-start | bytes 1048576 | tf_op jit(solution)/shard_map/all_to_all | solution.py:731
  15.8 0.0 copy-done.8
  15.8 0.2 convert_reduce_fusion
  16.0 0.5 multiply_add_fusion.arrival
  16.5 10.8 %all-to-all-done.received_ref = f32[32,32,128]{2,1,0:T(8,128)S(1)} async-done(((f32[32,32,128]{2,1,0:T(8,128)}), f32[32,32,128]{2,1,0:T(8,128)S(1)}, u32[]{:S(2)}, u32[]{:S(2)}) %all-to-all-start) | async-done | bytes 524320 | tf_op jit(solution)/shard_map/all_to_all | solution.py:731
  27.4 0.0 copy-start
  27.4 0.8 copy-done
  28.2 1.9 %shard_map.83 = (f32[8,16,128]{2,1,0:T(8,128)}, f32[8,16,128]{2,1,0:T(8,128)}) custom-call(s32[32]{0:T(128)} %multiply_add_fusion.arrival, f32[32,32,128]{2,1,0:T(8,128)} %copy-done), custom_call_target="tpu_custom_call" | custom-call | tf_op jit(solution)/shard_map/pallas_call | solution.py:736
  30.0 1.6 collective-permute-start
  31.7 2.1 %collective-permute-start.1 = (f32[8,16,128]{2,1,0:T(8,128)}, f32[8,16,128]{2,1,0:T(8,128)S(1)}, u32[]{:S(2)}, u32[]{:S(2)}) collective-permute-start(f32[8,16,128]{2,1,0:T(8,128)} %get-tuple-element.28), channel_id=1, source_target_pairs={{32,0},{64,32},{96,64},{0,96},{33,1},{65,33},{97,65},{1,97},{34,2}... | collective-permute-start | bytes 196616 | tf_op jit(solution)/shard_map/ppermute | solution.py:739
  33.8 2.3 %collective-permute-done.south = f32[8,16,128]{2,1,0:T(8,128)S(1)} collective-permute-done((f32[8,16,128]{2,1,0:T(8,128)}, f32[8,16,128]{2,1,0:T(8,128)S(1)}, u32[]{:S(2)}, u32[]{:S(2)}) %collective-permute-start) | collective-permute-done | bytes 65568 | tf_op jit(solution)/shard_map/ppermute | solution.py:739
  36.1 0.0 copy-start.2
  36.1 0.0 collective-permute-done.1.north
  36.1 0.6 copy-done.2
  36.7 0.6 copy-done.3
  37.3 2.7 %shard_map.84 = (f32[32,16,128]{2,1,0:T(8,128)}, f32[32,8,128]{2,1,0:T(8,128)}) custom-call(s32[32]{0:T(128)} %multiply_add_fusion.arrival, f32[32,32,128]{2,1,0:T(8,128)} %copy-done, f32[8,16,128]{2,1,0:T(8,128)} %copy-done.2, f32[8,16,128]{2,1,0:T(8,128)} %copy-done.3), custom_call_target="tpu_custom_call" | custom-call | tf_op jit(solution)/shard_map/pallas_call | solution.py:774
  40.0 4.5 %all-to-all-start.1 = ((f32[32,16,128]{2,1,0:T(8,128)}), f32[32,16,128]{2,1,0:T(8,128)S(1)}, u32[]{:S(2)}, u32[]{:S(2)}) async-start(f32[32,16,128]{2,1,0:T(8,128)} %get-tuple-element.29), calls=%async_computation.1 | async-start | bytes 524288 | tf_op jit(solution)/shard_map/all_to_all | solution.py:731
  44.5 4.1 %shard_map.86.weight_hbm = bf16[32,256,256]{2,1,0:T(8,128)(2,1)} custom-call(s32[72]{0:T(128)} %get-tuple-element.24.table, f32[8,256,128]{2,1,0:T(8,128)} %bitcast.50), custom_call_target="tpu_custom_call" | custom-call | tf_op jit(solution)/shard_map/pallas_call | solution.py:764
  48.6 5.0 %shard_map.85.fields_hbm = f32[32,256,128]{2,1,0:T(8,128)} custom-call(s32[72]{0:T(128)} %get-tuple-element.24.table, f32[64,64,128]{2,1,0:T(8,128)} %bitcast.45, f32[8,256,128]{2,1,0:T(8,128)} %bitcast.46, f32[8,256,128]{2,1,0:T(8,128)} %bitcast.47), custom_call_target="tpu_custom_call" | custom-call | tf_op jit(solution)/shard_map/pallas_call | solution.py:768
  53.6 0.0 all-to-all-done.1
  53.6 0.0 copy-start.1
  53.7 0.7 copy-done.1
  54.4 16.3 %shard_map.87 = (f32[32,704,128]{2,1,0:T(8,128)}, f32[768,128]{1,0:T(8,128)}, f32[256,128]{1,0:T(8,128)}, f32[128,128]{1,0:T(8,128)}) custom-call(s32[144]{0:T(256)} %get-tuple-element.25.codes, f32[512,128]{1,0:T(8,128)} %bitcast.48, f32[32,192,128]{2,1,0:T(8,128)} %get-tuple-element.30.pairs_hbm, f32[32,256,128]{2,1,0:T(8,128)} %shard_map.85.fields_hbm, ...), custom_call_target="tpu_custom_call" | custom-call | tf_op jit(solution)/shard_map/pallas_call | solution.py:779
  70.7 17.8 %all_to_all.36.received_ref.earlier_ref = f32[32,24,128]{2,1,0:T(8,128)} all-to-all(f32[32,24,128]{2,1,0:T(8,128)} %bitcast.54), channel_id=1, replica_groups=mesh['grp'=4,'dev'=32] {'dev'}, dimensions={0} | all-to-all | bytes 786432 | tf_op jit(solution)/shard_map/all_to_all | solution.py:731
  88.4 1.8 %shard_map.88 = (f32[8,8,128]{2,1,0:T(8,128)}, f32[8,8,128]{2,1,0:T(8,128)}) custom-call(s32[32]{0:T(128)} %multiply_add_fusion.arrival, f32[32,24,128]{2,1,0:T(8,128)} %all_to_all.36.received_ref.earlier_ref), custom_call_target="tpu_custom_call" | custom-call | tf_op jit(solution)/shard_map/pallas_call | solution.py:736
  90.2 0.9 collective-permute-start.2
  91.1 1.8 %collective-permute-start.3 = (f32[8,8,128]{2,1,0:T(8,128)}, f32[8,8,128]{2,1,0:T(8,128)S(1)}, u32[]{:S(2)}, u32[]{:S(2)}) collective-permute-start(f32[8,8,128]{2,1,0:T(8,128)} %get-tuple-element.33), channel_id=1, source_target_pairs={{32,0},{64,32},{96,64},{0,96},{33,1},{65,33},{97,65},{1,97},{34,2}... | collective-permute-start | bytes 98312 | tf_op jit(solution)/shard_map/ppermute | solution.py:739
  92.9 1.5 collective-permute-done.2.south
  94.4 0.0 copy-start.6
  94.4 0.0 collective-permute-done.3.north
  94.4 0.6 copy-done.6
  95.0 0.6 copy-done.7
  95.6 2.1 %shard_map.89 = f32[32,8,128]{2,1,0:T(8,128)} custom-call(s32[32]{0:T(128)} %multiply_add_fusion.arrival, f32[32,24,128]{2,1,0:T(8,128)} %all_to_all.36.received_ref.earlier_ref, f32[8,8,128]{2,1,0:T(8,128)} %copy-done.6, f32[8,8,128]{2,1,0:T(8,128)} %copy-done.7), custom_call_target="tpu_custom_call" | custom-call | tf_op jit(solution)/shard_map/pallas_call | solution.py:791
  97.7 13.4 %all_to_all.37 = f32[32,8,128]{2,1,0:T(8,128)} all-to-all(f32[32,8,128]{2,1,0:T(8,128)} %shard_map.89), channel_id=1, replica_groups=mesh['grp'=4,'dev'=32] {'dev'}, dimensions={0} | all-to-all | bytes 262144 | tf_op jit(solution)/shard_map/all_to_all | solution.py:731
  111.2 16.3 %shard_map.90 = (f32[32,128,128]{2,1,0:T(8,128)}, f32[1024,128]{1,0:T(8,128)}, f32[6,8,128]{2,1,0:T(8,128)}) custom-call(s32[144]{0:T(256)} %get-tuple-element.25.codes, f32[256,128]{1,0:T(8,128)} %bitcast.51, f32[256,128]{1,0:T(8,128)} %get-tuple-element.34.rowcoef_ref, f32[128,128]{1,0:T(8,128)} %get-tuple-element.35.colcoef_ref, ...), custom_call_target="tpu_custom_call" | custom-call | tf_op jit(solution)/shard_map/pallas_call | solution.py:796
  127.5 16.3 %all_to_all.38.received_ref = f32[32,32,128]{2,1,0:T(8,128)} all-to-all(f32[32,32,128]{2,1,0:T(8,128)} %bitcast.53), channel_id=1, replica_groups=mesh['grp'=4,'dev'=32] {'dev'}, dimensions={0} | all-to-all | bytes 1048576 | tf_op jit(solution)/shard_map/all_to_all | solution.py:731
  143.8 1.8 %shard_map.91 = (f32[8,8,128]{2,1,0:T(8,128)}, f32[8,8,128]{2,1,0:T(8,128)}) custom-call(s32[32]{0:T(128)} %multiply_add_fusion.arrival, f32[32,32,128]{2,1,0:T(8,128)} %all_to_all.38.received_ref), custom_call_target="tpu_custom_call" | custom-call | tf_op jit(solution)/shard_map/pallas_call | solution.py:736
  145.7 0.7 collective-permute-start.4
  146.3 2.0 %collective-permute-start.5 = (f32[8,8,128]{2,1,0:T(8,128)}, f32[8,8,128]{2,1,0:T(8,128)S(1)}, u32[]{:S(2)}, u32[]{:S(2)}) collective-permute-start(f32[8,8,128]{2,1,0:T(8,128)} %get-tuple-element.39), channel_id=1, source_target_pairs={{32,0},{64,32},{96,64},{0,96},{33,1},{65,33},{97,65},{1,97},{34,2}... | collective-permute-start | bytes 98312 | tf_op jit(solution)/shard_map/ppermute | solution.py:739
  148.3 1.5 collective-permute-done.4.south
  149.9 0.0 collective-permute-done.5.north
  149.9 0.6 copy-done.4
  150.5 0.0 copy-done.5
  150.5 2.6 %shard_map.92 = f32[128,128]{1,0:T(8,128)} custom-call(s32[32]{0:T(128)} %multiply_add_fusion.arrival, f32[32,32,128]{2,1,0:T(8,128)} %all_to_all.38.received_ref, f32[8,8,128]{2,1,0:T(8,128)} %copy-done.4, f32[8,8,128]{2,1,0:T(8,128)} %copy-done.5, f32[32,24,128]{2,1,0:T(8,128)} %all_to_all.36.received_ref.earlier_ref, ...), custom_call_target="tpu_custom_call" | custom-call | tf_op jit(solution)/shard_map/pallas_call | solution.py:807
  153.0 16.9 %all_to_all.39 = f32[128,1,128]{2,1,0:T(1,128)} all-to-all(f32[128,1,128]{2,1,0:T(1,128)} %bitcast.56), channel_id=1, replica_groups=mesh['grp'=4,'dev'=32] {'grp','dev'}, dimensions={0} | all-to-all | bytes 131072 | tf_op jit(solution)/shard_map/all_to_all | solution.py:810
  169.9 5.3 %shard_map.93 = f32[64,64,128]{2,1,0:T(8,128)} custom-call(s32[72]{0:T(128)} %get-tuple-element.24.table, f32[128,128]{1,0:T(8,128)} %bitcast.55, f32[32,192,128]{2,1,0:T(8,128)} %get-tuple-element.30.pairs_hbm, f32[32,704,128]{2,1,0:T(8,128)} %get-tuple-element.36.state_hbm, f32[32,128,128]{2,1,0:T(8,128)} %get-tuple-element.42.z1_hbm), custom_call_target="tpu_custom_call" | custom-call | tf_op jit(solution)/shard_map/pallas_call | solution.py:812
  (5 shorter events, 0.0 us)
Async XLA Ops:
  0.0 15.8 %copy-start.8 = (s32[32]{0:T(128)S(1)}, s32[32]{0:T(128)}, u32[]{:S(2)}) copy-start(s32[32]{0:T(128)} %param.14) | copy-start | bytes 388
  7.2 20.2 %all-to-all-start = ((f32[32,32,128]{2,1,0:T(8,128)}), f32[32,32,128]{2,1,0:T(8,128)S(1)}, u32[]{:S(2)}, u32[]{:S(2)}) async-start(f32[32,32,128]{2,1,0:T(8,128)} %bitcast.52), calls=%async_computation | async-start | bytes 1048576 | tf_op jit(solution)/shard_map/all_to_all | solution.py:731
  27.4 0.8 copy-start
  30.0 6.0 %collective-permute-start = (f32[8,16,128]{2,1,0:T(8,128)}, f32[8,16,128]{2,1,0:T(8,128)S(1)}, u32[]{:S(2)}, u32[]{:S(2)}) collective-permute-start(f32[8,16,128]{2,1,0:T(8,128)} %get-tuple-element.27), channel_id=1, source_target_pairs={{0,32},{32,64},{64,96},{96,0},{1,33},{33,65},{65,97},{97,1},{2,34}... | collective-permute-start | bytes 196616 | tf_op jit(solution)/shard_map/ppermute | solution.py:739
  31.7 4.4 %collective-permute-start.1 = (f32[8,16,128]{2,1,0:T(8,128)}, f32[8,16,128]{2,1,0:T(8,128)S(1)}, u32[]{:S(2)}, u32[]{:S(2)}) collective-permute-start(f32[8,16,128]{2,1,0:T(8,128)} %get-tuple-element.28), channel_id=1, source_target_pairs={{32,0},{64,32},{96,64},{0,96},{33,1},{65,33},{97,65},{1,97},{34,2}... | collective-permute-start | bytes 196616 | tf_op jit(solution)/shard_map/ppermute | solution.py:739
  36.1 0.6 copy-start.2
  36.7 0.6 copy-start.3
  40.0 13.6 %all-to-all-start.1 = ((f32[32,16,128]{2,1,0:T(8,128)}), f32[32,16,128]{2,1,0:T(8,128)S(1)}, u32[]{:S(2)}, u32[]{:S(2)}) async-start(f32[32,16,128]{2,1,0:T(8,128)} %get-tuple-element.29), calls=%async_computation.1 | async-start | bytes 524288 | tf_op jit(solution)/shard_map/all_to_all | solution.py:731
  53.6 0.7 copy-start.1
  90.2 4.2 %collective-permute-start.2 = (f32[8,8,128]{2,1,0:T(8,128)}, f32[8,8,128]{2,1,0:T(8,128)S(1)}, u32[]{:S(2)}, u32[]{:S(2)}) collective-permute-start(f32[8,8,128]{2,1,0:T(8,128)} %get-tuple-element.32), channel_id=1, source_target_pairs={{0,32},{32,64},{64,96},{96,0},{1,33},{33,65},{65,97},{97,1},{2,34}... | collective-permute-start | bytes 98312 | tf_op jit(solution)/shard_map/ppermute | solution.py:739
  91.1 3.3 %collective-permute-start.3 = (f32[8,8,128]{2,1,0:T(8,128)}, f32[8,8,128]{2,1,0:T(8,128)S(1)}, u32[]{:S(2)}, u32[]{:S(2)}) collective-permute-start(f32[8,8,128]{2,1,0:T(8,128)} %get-tuple-element.33), channel_id=1, source_target_pairs={{32,0},{64,32},{96,64},{0,96},{33,1},{65,33},{97,65},{1,97},{34,2}... | collective-permute-start | bytes 98312 | tf_op jit(solution)/shard_map/ppermute | solution.py:739
  94.4 0.6 copy-start.6
  95.0 0.6 copy-start.7
  145.7 4.2 %collective-permute-start.4 = (f32[8,8,128]{2,1,0:T(8,128)}, f32[8,8,128]{2,1,0:T(8,128)S(1)}, u32[]{:S(2)}, u32[]{:S(2)}) collective-permute-start(f32[8,8,128]{2,1,0:T(8,128)} %get-tuple-element.38), channel_id=1, source_target_pairs={{0,32},{32,64},{64,96},{96,0},{1,33},{33,65},{65,97},{97,1},{2,34}... | collective-permute-start | bytes 98312 | tf_op jit(solution)/shard_map/ppermute | solution.py:739
  146.3 3.5 %collective-permute-start.5 = (f32[8,8,128]{2,1,0:T(8,128)}, f32[8,8,128]{2,1,0:T(8,128)S(1)}, u32[]{:S(2)}, u32[]{:S(2)}) collective-permute-start(f32[8,8,128]{2,1,0:T(8,128)} %get-tuple-element.39), channel_id=1, source_target_pairs={{32,0},{64,32},{96,64},{0,96},{33,1},{65,33},{97,65},{1,97},{34,2}... | collective-permute-start | bytes 98312 | tf_op jit(solution)/shard_map/ppermute | solution.py:739
  149.9 0.6 copy-start.4
  149.9 0.6 copy-start.5

commit v3 on v2

--- a/solution.py
+++ b/solution.py
@@ -10,17 +10,16 @@
 SLOTS = 64
 PAIRS = 32
 TILES = 32
-CHUNK = 4
+CHUNK = 8
 CHUNKS = PAIRS // CHUNK
 TABLE = 72
 CODES = 144
 STATE = 704
 EPSILON = 1e-06
-VMEM_LIMIT = 56 * 1024 * 1024
-
-
-def params():
-    return pltpu.CompilerParams(vmem_limit_bytes=VMEM_LIMIT)
+
+
+def params(mebibytes):
+    return pltpu.CompilerParams(vmem_limit_bytes=mebibytes * 1024 * 1024)
 
 
 def vmem():
@@ -35,6 +34,22 @@
     return jax.ShapeDtypeStruct(shape, dtype)
 
 
+def resident(*shape, dtype=F32):
+    return pltpu.VMEM(shape, dtype)
+
+
+def held(x):
+    return pltpu.with_memory_space_constraint(x, pltpu.VMEM)
+
+
+def stored(*shape, dtype=F32):
+    return pltpu.HBM(shape, dtype)
+
+
+def kept(x):
+    return pltpu.with_memory_space_constraint(x, pltpu.HBM)
+
+
 def iota(shape, dim):
     return lax.broadcasted_iota(jnp.int32, shape, dim)
 
@@ -45,18 +60,20 @@
 
 def pair_up(t0, t1):
     low = iota(t0.shape, 1) < 64
-    return jnp.concatenate(
-        [jnp.where(low, t0, roll(t1, 64, 1)), jnp.where(low, roll(t0, 64, 1), t1)], axis=0
-    )
+    crossed = roll(jnp.where(low, t1, t0), 64, 1)
+    return jnp.concatenate([jnp.where(low, t0, crossed), jnp.where(low, crossed, t1)], axis=0)
 
 
 def split_up(q):
     even, odd = q[:32], q[32:]
     low = iota(even.shape, 1) < 64
-    return (
-        jnp.where(low, even, roll(odd, 64, 1)),
-        jnp.where(low, roll(even, 64, 1), odd),
-    )
+    crossed = roll(jnp.where(low, odd, even), 64, 1)
+    return jnp.where(low, even, crossed), jnp.where(low, crossed, odd)
+
+
+def load_tile(ref, index, offset, step):
+    rows = [ref[index, pl.ds(offset + step * q, 8, stride=4 * step), :] for q in range(4)]
+    return jnp.concatenate(rows, axis=0)
 
 
 def load_field(ref, table, j, empty):
@@ -64,8 +81,7 @@
     for r in range(2):
         s = table[2 * j + r]
         t = jnp.maximum(s, 0)
-        x = ref[t // 8, pl.ds(t % 8, 32, stride=8), :]
-        tiles.append(jnp.where(s >= 0, x, empty))
+        tiles.append(jnp.where(s >= 0, load_tile(ref, t // 8, t % 8, 8), empty))
     return pair_up(*tiles)
 
 
@@ -75,15 +91,15 @@
         tiles = []
         for r in range(2):
             s = table[2 * j + r]
-            x = ref[jnp.maximum(s, 0), pl.ds(c, 32, stride=2), :]
-            tiles.append(jnp.where(s >= 0, x, 0.0))
+            tiles.append(jnp.where(s >= 0, load_tile(ref, jnp.maximum(s, 0), c, 2), 0.0))
         parts.append(pair_up(*tiles))
     return parts
 
 
 def put_columns(acc_ref, x, j):
     mine = ((iota(x.shape, 1) % 64) // 2) == j
-    acc_ref[...] = jnp.where(mine, roll(x, 2 * j + 1, 1), acc_ref[...])
+    rows = slice(0, x.shape[0])
+    acc_ref[rows, :] = jnp.where(mine, roll(x, 2 * j + 1, 1), acc_ref[rows, :])
 
 
 def get_columns(acc, j):
@@ -112,18 +128,18 @@
 
 def south_of(x, halo=None):
     even, odd = x[:32], x[32:]
-    below = roll(odd, 1, 0)
+    below = roll(odd[24:], 1, 0)
     if halo is not None:
         below = jnp.where(iota(below.shape, 0) == 0, halo, below)
-    return jnp.concatenate([below, even], axis=0)
+    return jnp.concatenate([below, odd[:24], even], axis=0)
 
 
 def north_of(x, halo=None):
     even, odd = x[:32], x[32:]
-    above = roll(even, 31, 0)
+    above = roll(even[:8], 7, 0)
     if halo is not None:
-        above = jnp.where(iota(above.shape, 0) == 31, halo, above)
-    return jnp.concatenate([odd, above], axis=0)
+        above = jnp.where(iota(above.shape, 0) == 7, halo, above)
+    return jnp.concatenate([odd, even[8:], above], axis=0)
 
 
 def tile_part(y, west, south, turn):
@@ -134,10 +150,13 @@
         even, odd = x[:32], x[32:]
         s_even, s_odd = s[:32], s[32:]
         across = w * roll(x, 1, 1) + roll(w * x, 127, 1)
+        up = s_even * even
         along = jnp.concatenate(
             [
-                s_even * roll(odd, 1, 0) + s_odd * odd,
-                s_odd * even + roll(s_even * even, 31, 0),
+                s_even[:8] * roll(odd[24:], 1, 0) + s_odd[:8] * odd[:8],
+                s_even[8:] * odd[:24] + s_odd[8:] * odd[8:],
+                s_odd[:24] * even[:24] + up[8:],
+                s_odd[24:] * even[24:] + roll(up[:8], 7, 0),
             ],
             axis=0,
         )
@@ -224,10 +243,14 @@
     return ref.at[pl.ds(i * CHUNK, CHUNK)]
 
 
+def outgoing(source, target, sem, i):
+    return pltpu.make_async_copy(chunk(source, i), chunk(target, i), sem.at[i])
+
+
 def first_edges(
     ocean, u_hbm, z_hbm,
-    message_ref, table, codes, pairs_hbm,
-    u_ref, z_ref, pairs, acc_v, acc_z, turned, sem_in, sem_out,
+    message_ref, table, codes, pairs,
+    u_ref, z_ref, acc_v, acc_z, turned, sem_in,
 ):
     copies = [
         pltpu.make_async_copy(u_hbm, u_ref, sem_in.at[0]),
@@ -245,26 +268,32 @@
             u, v = load_vector(u_ref, table, j)
             z = load_field(z_ref, table, j, 0.0)
             vector = jnp.concatenate([u, v], axis=0)
-            visc = jnp.concatenate([z, z], axis=0)
             pairs[j, 0:128, :] = vector
             pairs[j, 128:192, :] = z
             put_columns(acc_v, vector, j)
-            put_columns(acc_z, visc, j)
+            put_columns(acc_z, z, j)
             put_rows(message_ref, vector, 32 * j)
-            put_rows(message_ref, visc, 32 * j + 8)
-        pltpu.make_async_copy(chunk(pairs, i), chunk(pairs_hbm, i), sem_out.at[i]).start()
+            put_rows(message_ref, jnp.concatenate([z, z], axis=0), 32 * j + 8)
         return carry
 
     lax.fori_loop(0, CHUNKS, body, 0)
     columns_to_message(acc_v, turned, message_ref, 0, 32)
     put_extras(codes, turned, message_ref, 16, 32)
+    acc_z[64:128, :] = acc_z[0:64, :]
     columns_to_message(acc_z, turned, message_ref, 8, 32)
     put_extras(codes, turned, message_ref, 24, 32)
-    for i in range(CHUNKS):
-        pltpu.make_async_copy(chunk(pairs, i), chunk(pairs_hbm, i), sem_out.at[i]).wait()
-
-
-def pair_fields(table, b_ref, a_ref, f_ref, out_hbm, pairs, sem):
+
+
+def pair_fields(table, b_hbm, a_hbm, f_hbm, out_hbm, b_ref, a_ref, f_ref, pairs, sem_in, sem_out):
+    copies = [
+        pltpu.make_async_copy(source, target, sem_in.at[n])
+        for n, (source, target) in enumerate(((b_hbm, b_ref), (a_hbm, a_ref), (f_hbm, f_ref)))
+    ]
+    for copy in copies:
+        copy.start()
+    for copy in copies:
+        copy.wait()
+
     def body(i, carry):
         for k in range(CHUNK):
             j = i * CHUNK + k
@@ -273,15 +302,18 @@
             pairs[j, 64:128, :] = bv
             pairs[j, 128:192, :] = load_field(a_ref, table, j, 1.0)
             pairs[j, 192:256, :] = load_field(f_ref, table, j, 0.0)
-        pltpu.make_async_copy(chunk(pairs, i), chunk(out_hbm, i), sem.at[i]).start()
+        outgoing(pairs, out_hbm, sem_out, i).start()
         return carry
 
     lax.fori_loop(0, CHUNKS, body, 0)
     for i in range(CHUNKS):
-        pltpu.make_async_copy(chunk(pairs, i), chunk(out_hbm, i), sem.at[i]).wait()
-
-
-def line_weights(table, p_ref, out_hbm, weight, natural, sem):
+        outgoing(pairs, out_hbm, sem_out, i).wait()
+
+
+def line_weights(table, p_hbm, out_hbm, p_ref, weight, natural, sem_in, sem_out):
+    copy = pltpu.make_async_copy(p_hbm, p_ref, sem_in)
+    copy.start()
+    copy.wait()
     low = iota((32, 128), 1) < 64
 
     def body(i, carry):
@@ -304,12 +336,12 @@
             both = jnp.concatenate([high, rest], axis=1)
             weight[j, 0:128, :] = both
             weight[j, 128:256, :] = both
-        pltpu.make_async_copy(chunk(weight, i), chunk(out_hbm, i), sem.at[i]).start()
+        outgoing(weight, out_hbm, sem_out, i).start()
         return carry
 
     lax.fori_loop(0, CHUNKS, body, 0)
     for i in range(CHUNKS):
-        pltpu.make_async_copy(chunk(weight, i), chunk(out_hbm, i), sem.at[i]).wait()
+        outgoing(weight, out_hbm, sem_out, i).wait()
 
 
 def side_masks():
@@ -322,14 +354,14 @@
 
 
 def first_step(
-    codes, halo_ref, pairs_hbm, fields_hbm, weight_hbm,
-    state_hbm, message_ref, rowcoef_ref, colcoef_ref,
-    pairs, fields, weight, state, acc_z, acc_r, hv, hz, turned, sem_in, sem_out,
+    codes, halo_ref, pairs, fields_hbm, weight_hbm,
+    state, weight, message_ref, edges_ref, rowcoef_ref, colcoef_ref,
+    fields, acc_z, acc_r, hv, hz, turned, sem,
 ):
     def incoming(i):
         return [
-            pltpu.make_async_copy(chunk(source, i), chunk(target, i), sem_in.at[n, i])
-            for n, (source, target) in enumerate(((pairs_hbm, pairs), (fields_hbm, fields), (weight_hbm, weight)))
+            pltpu.make_async_copy(chunk(source, i), chunk(target, i), sem.at[n, i])
+            for n, (source, target) in enumerate(((fields_hbm, fields), (weight_hbm, weight)))
         ]
 
     for i in range(CHUNKS):
@@ -388,7 +420,7 @@
         south = jnp.concatenate(south, axis=0)
         put_columns(colcoef_ref, jnp.concatenate(column, axis=0), j)
         put_columns(acc_r, plain, j)
-        put_rows(message_ref, plain, 24 * j + 8)
+        put_rows(edges_ref, plain, 8 * j)
         state[j, 0:128, :] = west
         state[j, 128:256, :] = south
         state[j, 256:384, :] = jnp.concatenate(diag, axis=0)
@@ -398,39 +430,27 @@
         z0 = jnp.concatenate(scale, axis=0) * y
         state[j, 576:704, :] = z0
         put_columns(acc_z, z0, j)
-        put_rows(message_ref, z0, 24 * j)
+        put_rows(message_ref, z0, 16 * j)
 
     def body(i, carry):
         for copy in incoming(i):
             copy.wait()
         for k in range(CHUNK):
             one(i * CHUNK + k)
-        pltpu.make_async_copy(chunk(state, i), chunk(state_hbm, i), sem_out.at[i]).start()
         return carry
 
     lax.fori_loop(0, CHUNKS, body, 0)
-    columns_to_message(acc_r, turned, message_ref, 8, 24)
-    columns_to_message(acc_z, turned, message_ref, 0, 24)
-    put_extras(codes, turned, message_ref, 16, 24)
-    for i in range(CHUNKS):
-        pltpu.make_async_copy(chunk(state, i), chunk(state_hbm, i), sem_out.at[i]).wait()
+    columns_to_message(acc_r, turned, edges_ref, 0, 8)
+    columns_to_message(acc_z, turned, message_ref, 0, 16)
+    put_extras(codes, turned, message_ref, 8, 16)
 
 
 def second_step(
-    codes, halo_ref, rowcoef_ref, colcoef_ref, state_hbm, weight_hbm,
-    z1_hbm, message_ref, sums_ref,
-    state, weight, z1s, acc_z, acc_p, acc_d, hv, turned, sem_in, sem_out,
+    codes, halo_ref, rowcoef_ref, colcoef_ref, state, weight,
+    z1s, message_ref, sums_ref,
+    acc_z, acc_p, acc_d, hv, turned,
 ):
-    def incoming(i):
-        return [
-            pltpu.make_async_copy(chunk(source, i), chunk(target, i), sem_in.at[n, i])
-            for n, (source, target) in enumerate(((state_hbm, state), (weight_hbm, weight)))
-        ]
-
-    for i in range(CHUNKS):
-        for copy in incoming(i):
-            copy.start()
-    message_to_columns(halo_ref, turned, hv, 0, 8)
+    message_to_columns(halo_ref, turned, hv, 0, 16)
     hv[...] = hv[...] * colcoef_ref[...]
     lane = iota((128, 128), 1) % 64
     at_side = (lane == 0) | (lane == 63)
@@ -447,7 +467,7 @@
         what = tile_part(y0, west, south, turn)
         what = what - jnp.where(at_side, get_columns(hv[...], j), 0.0)
         base = pl.multiple_of(8 * j, 8)
-        rows = halo_ref[pl.ds(base, 8), :] * rowcoef_ref[pl.ds(base, 8), :]
+        rows = halo_ref[pl.ds(pl.multiple_of(16 * j, 16), 8), :] * rowcoef_ref[pl.ds(base, 8), :]
         fixed = []
         for c in range(2):
             part = what[64 * c : 64 * c + 64]
@@ -472,11 +492,8 @@
             put_rows(message_ref, x, 32 * j + 8 * k)
 
     def body(i, carry):
-        for copy in incoming(i):
-            copy.wait()
         for k in range(CHUNK):
             one(i * CHUNK + k)
-        pltpu.make_async_copy(chunk(z1s, i), chunk(z1_hbm, i), sem_out.at[i]).start()
         return carry
 
     lax.fori_loop(0, CHUNKS, body, 0)
@@ -484,8 +501,6 @@
     columns_to_message(acc_d, turned, message_ref, 16, 32)
     columns_to_message(acc_z, turned, message_ref, 0, 32)
     put_extras(codes, turned, message_ref, 24, 32)
-    for i in range(CHUNKS):
-        pltpu.make_async_copy(chunk(z1s, i), chunk(z1_hbm, i), sem_out.at[i]).wait()
 
 
 def to_normal(x, r):
@@ -561,9 +576,10 @@
                 face_ref[t] = factor * (blocks[t] + halos[t])
 
 
-def second_return(arrival, received_ref, south, north, out_ref):
-    out_ref[...] = jnp.zeros(out_ref.shape, F32)
-    blocks, halos = tile_halos(arrival, received_ref, south, north, 0, 2)
+def second_return(arrival, received_ref, south, north, edges_ref, out_ref):
+    out_ref[:, 0:8, :] = jnp.zeros((PAIRS, 8, 128), F32)
+    out_ref[:, 8:16, :] = edges_ref[...]
+    blocks, halos = tile_halos(arrival, received_ref, south, north, 0, 1)
     for t in range(TILES):
         hand_back(arrival, t, 0, halos[t], out_ref)
 
@@ -652,38 +668,22 @@
 
 
 def last_step(
-    table, gathered_ref, pairs_hbm, state_hbm, z1_hbm,
+    table, gathered_ref, pairs, state, z1,
     out_hbm,
-    u, z0, z1, out, sem_in, sem_out,
+    out, sem_out,
 ):
-    def incoming(i):
-        return [
-            pltpu.make_async_copy(source, chunk(target, i), sem_in.at[n, i])
-            for n, (source, target) in enumerate(
-                (
-                    (chunk(pairs_hbm, i).at[:, pl.ds(0, 128)], u),
-                    (chunk(state_hbm, i).at[:, pl.ds(576, 128)], z0),
-                    (chunk(z1_hbm, i), z1),
-                )
-            )
-        ]
-
-    for i in range(CHUNKS):
-        for copy in incoming(i):
-            copy.start()
     out[...] = jnp.zeros(out.shape, F32)
     weight0, weight1 = final_weights(gathered_ref[...])
 
     def body(i, carry):
-        for copy in incoming(i):
-            copy.wait()
         for k in range(CHUNK):
             j = i * CHUNK + k
-            new = u[j] + weight0 * z0[j] + weight1 * z1[j]
+            new = pairs[j, 0:128, :] + weight0 * state[j, 576:704, :] + weight1 * z1[j]
             slots = [jnp.where(table[2 * j + r] >= 0, table[2 * j + r], SLOTS) for r in range(2)]
             for c in range(2):
                 for r, x in enumerate(split_up(new[64 * c : 64 * c + 64])):
-                    out[slots[r], pl.ds(c, 32, stride=2), :] = x
+                    for q in range(4):
+                        out[slots[r], pl.ds(c + 2 * q, 8, stride=8), :] = x[8 * q : 8 * q + 8]
         return carry
 
     lax.fori_loop(0, CHUNKS, body, 0)
@@ -692,14 +692,14 @@
     copy.wait()
 
 
-def call(kernel, outs, specs, scratch=(), out_specs=None):
+def call(kernel, outs, specs, scratch=(), out_specs=None, mebibytes=4):
     return pl.pallas_call(
         kernel,
         out_shape=outs,
         in_specs=specs,
         out_specs=out_specs if out_specs is not None else jax.tree.map(lambda _: vmem(), outs),
         scratch_shapes=list(scratch),
-        compiler_params=params(),
+        compiler_params=params(mebibytes),
     )
 
 
@@ -752,57 +752,62 @@
         first_edges,
         (
             struct(PAIRS * 32, 128), struct(TABLE, dtype=jnp.int32), struct(CODES, dtype=jnp.int32),
-            struct(PAIRS, 192, 128),
+            resident(PAIRS, 192, 128),
         ),
         [smem(), hbm(), hbm()],
+        [buffer(64, 64, 128), buffer(8, 256, 128), square(), square(), square(), sems(2)],
+        (vmem(), smem(), smem(), vmem()),
+        8,
+    )(kept(ocean_tile), kept(u), kept(z))
+    weight = call(
+        line_weights, stored(PAIRS, 256, 256, dtype=BF16), [smem(), hbm()],
         [
-            buffer(64, 64, 128), buffer(8, 256, 128), buffer(PAIRS, 192, 128),
-            square(), square(), square(), sems(2), sems(CHUNKS),
+            buffer(8, 256, 128), buffer(PAIRS, 256, 256, dtype=BF16), buffer(CHUNK, 128, 128),
+            pltpu.SemaphoreType.DMA, sems(CHUNKS),
         ],
-        (vmem(), smem(), smem(), hbm()),
-    )(ocean_tile, u, z)
-    weight = call(
-        line_weights, struct(PAIRS, 256, 256, dtype=BF16), [smem(), vmem()],
-        [buffer(PAIRS, 256, 256, dtype=BF16), buffer(CHUNK, 128, 128), sems(CHUNKS)], hbm(),
-    )(table, p)
+        hbm(), 8,
+    )(table, kept(p))
     fields = call(
-        pair_fields, struct(PAIRS, 256, 128), [smem(), vmem(), vmem(), vmem()],
-        [buffer(PAIRS, 256, 128), sems(CHUNKS)], hbm(),
-    )(table, b, a, f)
+        pair_fields, stored(PAIRS, 256, 128), [smem(), hbm(), hbm(), hbm()],
+        [
+            buffer(64, 64, 128), buffer(8, 256, 128), buffer(8, 256, 128), buffer(PAIRS, 256, 128),
+            sems(3), sems(CHUNKS),
+        ],
+        hbm(), 12,
+    )(table, kept(b), kept(a), kept(f))
 
     received = exchange(message.reshape(PAIRS, 32, 128))
+    received, weight = lax.optimization_barrier((received, weight))
     halo, face = call(
         first_return, (struct(PAIRS, 16, 128), struct(TILES, 8, 128)), [smem()] + [vmem()] * 3
     )(arrival, received, *from_groups(arrival, received, 2))
     halo = exchange(halo).reshape(PAIRS * 16, 128)
 
-    state, message, rowcoef, colcoef = call(
+    state, weight, message, edges, rowcoef, colcoef = call(
         first_step,
-        (struct(PAIRS, STATE, 128), struct(PAIRS * 24, 128), struct(PAIRS * 8, 128), struct(128, 128)),
-        [smem(), vmem(), hbm(), hbm(), hbm()],
-        [
-            buffer(PAIRS, 192, 128), buffer(PAIRS, 256, 128), buffer(PAIRS, 256, 256, dtype=BF16),
-            buffer(PAIRS, STATE, 128), square(), square(), square(), square(), square(),
-            sems(3, CHUNKS), sems(CHUNKS),
-        ],
-        (hbm(), vmem(), vmem(), vmem()),
-    )(codes, halo, pairs, fields, weight)
-    earlier = exchange(message.reshape(PAIRS, 24, 128))
-    halo = call(second_return, struct(PAIRS, 8, 128), [smem()] + [vmem()] * 3)(
-        arrival, earlier, *from_groups(arrival, earlier, 1)
+        (
+            resident(PAIRS, STATE, 128), resident(PAIRS, 256, 256, dtype=BF16), struct(PAIRS * 16, 128), struct(PAIRS * 8, 128),
+            struct(PAIRS * 8, 128), struct(128, 128),
+        ),
+        [smem(), vmem(), vmem(), hbm(), hbm()],
+        [buffer(PAIRS, 256, 128)] + [square()] * 5 + [sems(2, CHUNKS)],
+        [vmem()] * 6,
+        mebibytes=16,
+    )(codes, halo, held(pairs), kept(fields), kept(weight))
+    received = exchange(message.reshape(PAIRS, 16, 128))
+    halo = call(second_return, struct(PAIRS, 16, 128), [smem()] + [vmem()] * 4)(
+        arrival, received, *from_groups(arrival, received, 1), edges.reshape(PAIRS, 8, 128)
     )
-    halo = exchange(halo).reshape(PAIRS * 8, 128)
+    earlier = exchange(halo)
+    halo = earlier.reshape(PAIRS * 16, 128)
 
     z1, message, sums = call(
         second_step,
-        (struct(PAIRS, 128, 128), struct(PAIRS * 32, 128), struct(6, 8, 128)),
-        [smem(), vmem(), vmem(), vmem(), hbm(), hbm()],
-        [
-            buffer(PAIRS, STATE, 128), buffer(PAIRS, 256, 256, dtype=BF16), buffer(PAIRS, 128, 128),
-            square(), square(), square(), square(), square(), sems(2, CHUNKS), sems(CHUNKS),
-        ],
-        (hbm(), vmem(), vmem()),
-    )(codes, halo, rowcoef, colcoef, state, weight)
+        (resident(PAIRS, 128, 128), struct(PAIRS * 32, 128), struct(6, 8, 128)),
+        [smem()] + [vmem()] * 5,
+        [square()] * 5,
+        mebibytes=8,
+    )(codes, halo, rowcoef, colcoef, held(state), held(weight))
     received = exchange(message.reshape(PAIRS, 32, 128))
     partial = call(edge_sums, struct(128, 128), [smem()] + [vmem()] * 6)(
         arrival, received, *from_groups(arrival, received, 1), earlier, face, sums
@@ -810,11 +815,11 @@
     gathered = lax.all_to_all(partial, ("grp", "dev"), split_axis=0, concat_axis=0, tiled=True)
 
     out = call(
-        last_step, struct(SLOTS, 64, 128), [smem(), vmem(), hbm(), hbm(), hbm()],
-        [buffer(PAIRS, 128, 128), buffer(PAIRS, 128, 128), buffer(PAIRS, 128, 128), buffer(SLOTS + 1, 64, 128),
-         sems(3, CHUNKS), pltpu.SemaphoreType.DMA],
+        last_step, struct(SLOTS, 64, 128), [smem()] + [vmem()] * 4,
+        [buffer(SLOTS + 1, 64, 128), pltpu.SemaphoreType.DMA],
         hbm(),
-    )(table, gathered, pairs, state, z1)
+        8,
+    )(table, gathered, held(pairs), held(state), held(z1))
     return out.reshape(64, 32, 2, 128).transpose(0, 2, 1, 3).reshape(64, 2, 4096)
 
 

time: 176 us -> 148 us (0.84)
  Pallas kernels: 67.1 us -> 49.4 us
  blocking collectives: 64.4 us -> 58.3 us
  local copies, waits for them, and re-layouts: 4.53 us -> 1.49 us
    pallas_call x6, Pallas kernels: 49.1 us -> 37.2 us  [the longest x1 12.2 us: shards(): call(first_step, (resident(PAIRS, STATE, 128), resident(PAIRS, 256, 256,...]
    all_to_all x3, blocking collectives: 47.5 us -> 41.9 us  [exchange(): return lax.all_to_all(x, 'dev', split_axis=0, concat_axis=0, tiled=True)]
    unnamed x18 -> x6, local copies, waits for them, and re-layouts: 4.53 us -> 1.49 us
    pallas_call x3, Pallas kernels: 5.48 us -> 2.61 us  [from_groups(): call(boundary, (side, side), [smem(), vmem()])(arrival, received)]
  transfers between devices with their start and end apart: 8 -> 8, of which waited for: 4 -> 7; matrix products, arithmetic and copies ran while one was open for 0% -> 0% of each run, Pallas kernels for 5% -> 7%
where the time goes in v3:
time: 148 us
  blocking collectives  58.3 us (39%)
  Pallas kernels  49.4 us (33%)
  starting transfers between devices  23 us (16%)
  waiting for transfers between devices  15.2 us (10%)
  local copies, waits for them, and re-layouts  1.49 us (1%)
    all_to_all x3, blocking collectives, exchange(): return lax.all_to_all(x, 'dev', split_axis=0, concat_axis=0, tiled=True)  41.9 us
    all_to_all x1, blocking collectives, shards(): lax.all_to_all(partial, ('grp', 'dev'), split_axis=0, concat_axis=0, tile...  16.4 us
    all_to_all x2, starting transfers between devices, exchange(): return lax.all_to_all(x, 'dev', split_axis=0, concat_axis=0, tiled=True)  13.3 us
    pallas_call x1, Pallas kernels, shards(): call(first_step, (resident(PAIRS, STATE, 128), resident(PAIRS, 256, 256,...  12.2 us
    pallas_call x1, Pallas kernels, shards(): call(second_step, (resident(PAIRS, 128, 128), struct(PAIRS * 32, 128), st...  11.2 us
    all_to_all x2, waiting for transfers between devices, exchange(): return lax.all_to_all(x, 'dev', split_axis=0, concat_axis=0, tiled=True)  10.2 us
    pallas_call x1, Pallas kernels, shards(): call(first_edges, (struct(PAIRS * 32, 128), struct(TABLE, dtype=jnp.int32...  6.38 us
    pallas_call x1, Pallas kernels, shards(): call(pair_fields, stored(PAIRS, 256, 128), [smem(), hbm(), hbm(), hbm()],...  5.96 us
  transfers between devices with their start and end apart: 8, of which 7 were waited for; matrix products, arithmetic and copies ran while one was open for 0% of the time, Pallas kernels for 7%

profile of v3, /device:TPU:1, one launch (start us, length us, event | category | flops | bytes accessed | tf_op | source)
XLA Modules:
  0.0 147.8 jit_solution(14227757456034903440)
XLA Ops:
  0.0 6.4 %shard_map.82 = (f32[1024,128]{1,0:T(8,128)S(1)}, s32[72]{0:T(128)S(1)}, s32[144]{0:T(256)S(1)}, f32[32,192,128]{2,1,0:T(8,128)S(1)}) custom-call(s32[64]{0:T(128)} %ocean.1, f32[64,64,128]{2,1,0:T(8,128)} %bitcast.53, f32[8,256,128]{2,1,0:T(8,128)} %bitcast.57), custom_call_target="tpu_custom_call" | custom-call | tf_op jit(solution)/shard_map/pallas_call | solution.py:751
  6.4 0.0 copy-start
  6.4 0.8 copy-done
  7.2 0.0 copy-start.2
  7.2 8.8 %all-to-all-start = ((f32[32,32,128]{2,1,0:T(8,128)}), f32[32,32,128]{2,1,0:T(8,128)}, u32[]{:S(2)}, u32[]{:S(2)}) async-start(f32[32,32,128]{2,1,0:T(8,128)} %bitcast.47), calls=%async_computation | async-start | bytes 1048576 | tf_op jit(solution)/shard_map/all_to_all | solution.py:731
  16.0 4.2 %shard_map.83.weight_hbm = bf16[32,256,256]{2,1,0:T(8,128)(2,1)} custom-call(s32[72]{0:T(128)S(1)} %get-tuple-element.28.table, f32[8,256,128]{2,1,0:T(8,128)} %bitcast.58), custom_call_target="tpu_custom_call" | custom-call | tf_op jit(solution)/shard_map/pallas_call | solution.py:762
  20.1 0.0 copy-done.2
  20.2 0.2 convert_reduce_fusion
  20.4 7.2 %all-to-all-done.received_ref = f32[32,32,128]{2,1,0:T(8,128)} async-done(((f32[32,32,128]{2,1,0:T(8,128)}), f32[32,32,128]{2,1,0:T(8,128)}, u32[]{:S(2)}, u32[]{:S(2)}) %all-to-all-start) | async-done | bytes 524320 | tf_op jit(solution)/shard_map/all_to_all | solution.py:731
  27.6 1.2 shard_map.84
  28.8 1.7 %collective-permute-start = (f32[8,16,128]{2,1,0:T(8,128)S(1)}, f32[8,16,128]{2,1,0:T(8,128)S(1)}, u32[]{:S(2)}, u32[]{:S(2)}) collective-permute-start(f32[8,16,128]{2,1,0:T(8,128)S(1)} %get-tuple-element.32), channel_id=1, source_target_pairs={{0,32},{32,64},{64,96},{96,0},{1,33},{33,65},{65,97},{97,1},{2,34}... | collective-permute-start | bytes 196616 | tf_op jit(solution)/shard_map/ppermute | solution.py:739
  30.5 2.2 %collective-permute-start.1 = (f32[8,16,128]{2,1,0:T(8,128)S(1)}, f32[8,16,128]{2,1,0:T(8,128)S(1)}, u32[]{:S(2)}, u32[]{:S(2)}) collective-permute-start(f32[8,16,128]{2,1,0:T(8,128)S(1)} %get-tuple-element.33), channel_id=1, source_target_pairs={{32,0},{64,32},{96,64},{0,96},{33,1},{65,33},{97,65},{1,97},{34,2}... | collective-permute-start | bytes 196616 | tf_op jit(solution)/shard_map/ppermute | solution.py:739
  32.7 2.0 %collective-permute-done.south = f32[8,16,128]{2,1,0:T(8,128)S(1)} collective-permute-done((f32[8,16,128]{2,1,0:T(8,128)S(1)}, f32[8,16,128]{2,1,0:T(8,128)S(1)}, u32[]{:S(2)}, u32[]{:S(2)}) %collective-permute-start) | collective-permute-done | bytes 65568 | tf_op jit(solution)/shard_map/ppermute | solution.py:739
  34.7 0.0 collective-permute-done.1.north
  34.7 1.9 %shard_map.85 = (f32[32,16,128]{2,1,0:T(8,128)S(1)}, f32[32,8,128]{2,1,0:T(8,128)S(1)}) custom-call(s32[32]{0:T(128)S(1)} %multiply_add_fusion.arrival, f32[32,32,128]{2,1,0:T(8,128)} %all-to-all-done.received_ref, f32[8,16,128]{2,1,0:T(8,128)S(1)} %collective-permute-done.south, f32[8,16,128]{2,1,0:T(8,128)S(1)} %collective-permute-done.1.north), custom_call_target="tpu_custom_call" | custom-call | tf_op jit(solution)/shard_map/pallas_call | solution.py:781
  36.6 0.0 copy-start.1
  36.7 0.7 copy-done.1
  37.3 4.5 %all-to-all-start.1 = ((f32[32,16,128]{2,1,0:T(8,128)}), f32[32,16,128]{2,1,0:T(8,128)S(1)}, u32[]{:S(2)}, u32[]{:S(2)}) async-start(f32[32,16,128]{2,1,0:T(8,128)} %copy-done.1), calls=%async_computation.1 | async-start | bytes 524288 | tf_op jit(solution)/shard_map/all_to_all | solution.py:731
  41.8 6.0 %shard_map.86.fields_hbm = f32[32,256,128]{2,1,0:T(8,128)} custom-call(s32[72]{0:T(128)S(1)} %get-tuple-element.28.table, f32[64,64,128]{2,1,0:T(8,128)} %bitcast.54, f32[8,256,128]{2,1,0:T(8,128)} %bitcast.55, f32[8,256,128]{2,1,0:T(8,128)} %bitcast.56), custom_call_target="tpu_custom_call" | custom-call | tf_op jit(solution)/shard_map/pallas_call | solution.py:770
  47.8 3.0 %all-to-all-done.1 = f32[32,16,128]{2,1,0:T(8,128)S(1)} async-done(((f32[32,16,128]{2,1,0:T(8,128)}), f32[32,16,128]{2,1,0:T(8,128)S(1)}, u32[]{:S(2)}, u32[]{:S(2)}) %all-to-all-start.1) | async-done | bytes 262176 | tf_op jit(solution)/shard_map/all_to_all | solution.py:731
  50.9 12.2 %shard_map.87 = (f32[32,704,128]{2,1,0:T(8,128)S(1)}, bf16[32,256,256]{2,1,0:T(8,128)(2,1)S(1)}, f32[512,128]{1,0:T(8,128)S(1)}, f32[256,128]{1,0:T(8,128)S(1)},...) custom-call(s32[144]{0:T(256)S(1)} %get-tuple-element.29.codes, f32[512,128]{1,0:T(8,128)S(1)} %bitcast.46, ...), custom_call_target="tpu_custom_call" | custom-call | tf_op jit(solution)/shard_map/pallas_call | solution.py:786
  63.1 13.2 %all_to_all.36.received_ref = f32[32,16,128]{2,1,0:T(8,128)S(1)} all-to-all(f32[32,16,128]{2,1,0:T(8,128)S(1)} %bitcast.50), channel_id=1, replica_groups=mesh['grp'=4,'dev'=32] {'dev'}, dimensions={0} | all-to-all | bytes 524288 | tf_op jit(solution)/shard_map/all_to_all | solution.py:731
  76.3 0.7 shard_map.88
  77.0 1.5 %collective-permute-start.2 = (f32[8,8,128]{2,1,0:T(8,128)S(1)}, f32[8,8,128]{2,1,0:T(8,128)S(1)}, u32[]{:S(2)}, u32[]{:S(2)}) collective-permute-start(f32[8,8,128]{2,1,0:T(8,128)S(1)} %get-tuple-element.38), channel_id=1, source_target_pairs={{0,32},{32,64},{64,96},{96,0},{1,33},{33,65},{65,97},{97,1},{2,34}... | collective-permute-start | bytes 98312 | tf_op jit(solution)/shard_map/ppermute | solution.py:739
  78.5 1.6 %collective-permute-start.3 = (f32[8,8,128]{2,1,0:T(8,128)S(1)}, f32[8,8,128]{2,1,0:T(8,128)S(1)}, u32[]{:S(2)}, u32[]{:S(2)}) collective-permute-start(f32[8,8,128]{2,1,0:T(8,128)S(1)} %get-tuple-element.39), channel_id=1, source_target_pairs={{32,0},{64,32},{96,64},{0,96},{33,1},{65,33},{97,65},{1,97},{34,2}... | collective-permute-start | bytes 98312 | tf_op jit(solution)/shard_map/ppermute | solution.py:739
  80.0 1.2 collective-permute-done.2.south
  81.3 0.3 collective-permute-done.3.north
  81.5 1.0 shard_map.89
  82.5 13.6 %all_to_all.37.earlier_ref = f32[32,16,128]{2,1,0:T(8,128)S(1)} all-to-all(f32[32,16,128]{2,1,0:T(8,128)S(1)} %shard_map.89), channel_id=1, replica_groups=mesh['grp'=4,'dev'=32] {'dev'}, dimensions={0} | all-to-all | bytes 524288 | tf_op jit(solution)/shard_map/all_to_all | solution.py:731
  96.1 11.2 %shard_map.90 = (f32[32,128,128]{2,1,0:T(8,128)S(1)}, f32[1024,128]{1,0:T(8,128)S(1)}, f32[6,8,128]{2,1,0:T(8,128)S(1)}) custom-call(s32[144]{0:T(256)S(1)} %get-tuple-element.29.codes, f32[512,128]{1,0:T(8,128)S(1)} %bitcast.45, f32[256,128]{1,0:T(8,128)S(1)} %get-tuple-element.41.rowcoef_ref, f32[128,128]{1,0:T(8,128)S(1)} %get-tuple-element.42.colcoef_ref, ...), custom_call_target="tpu_custom_call" | custom-call | tf_op jit(solution)/shard_map/pallas_call | solution.py:804
  107.3 15.1 %all_to_all.38.received_ref = f32[32,32,128]{2,1,0:T(8,128)S(1)} all-to-all(f32[32,32,128]{2,1,0:T(8,128)S(1)} %bitcast.48), channel_id=1, replica_groups=mesh['grp'=4,'dev'=32] {'dev'}, dimensions={0} | all-to-all | bytes 1048576 | tf_op jit(solution)/shard_map/all_to_all | solution.py:731
  122.4 0.7 shard_map.91
  123.1 1.4 collective-permute-start.4
  124.5 1.3 collective-permute-start.5
  125.9 1.3 collective-permute-done.4.south
  127.2 0.1 collective-permute-done.5.north
  127.3 1.2 shard_map.92
  128.5 16.4 %all_to_all.39 = f32[128,1,128]{2,1,0:T(1,128)S(1)} all-to-all(f32[128,1,128]{2,1,0:T(1,128)S(1)} %bitcast.51), channel_id=1, replica_groups=mesh['grp'=4,'dev'=32] {'grp','dev'}, dimensions={0} | all-to-all | bytes 131072 | tf_op jit(solution)/shard_map/all_to_all | solution.py:815
  145.0 2.7 %shard_map.93 = f32[64,64,128]{2,1,0:T(8,128)} custom-call(s32[72]{0:T(128)S(1)} %get-tuple-element.28.table, f32[128,128]{1,0:T(8,128)S(1)} %bitcast.49, f32[32,192,128]{2,1,0:T(8,128)S(1)} %get-tuple-element.35.pairs, f32[32,704,128]{2,1,0:T(8,128)S(1)} %get-tuple-element.43.state, f32[32,128,128]{2,1,0:T(8,128)S(1)} %get-tuple-element.50.z1), custom_call_target="tpu_custom_call" | custom-call | tf_op jit(solution)/shard_map/pallas_call | solution.py:817
  (2 shorter events, 0.0 us)
Async XLA Ops:
  6.4 0.8 copy-start
  7.2 13.0 %copy-start.2 = (s32[32]{0:T(128)S(1)}, s32[32]{0:T(128)}, u32[]{:S(2)}) copy-start(s32[32]{0:T(128)} %param.14) | copy-start | bytes 388
  7.2 20.4 %all-to-all-start = ((f32[32,32,128]{2,1,0:T(8,128)}), f32[32,32,128]{2,1,0:T(8,128)}, u32[]{:S(2)}, u32[]{:S(2)}) async-start(f32[32,32,128]{2,1,0:T(8,128)} %bitcast.47), calls=%async_computation | async-start | bytes 1048576 | tf_op jit(solution)/shard_map/all_to_all | solution.py:731
  28.8 5.9 %collective-permute-start = (f32[8,16,128]{2,1,0:T(8,128)S(1)}, f32[8,16,128]{2,1,0:T(8,128)S(1)}, u32[]{:S(2)}, u32[]{:S(2)}) collective-permute-start(f32[8,16,128]{2,1,0:T(8,128)S(1)} %get-tuple-element.32), channel_id=1, source_target_pairs={{0,32},{32,64},{64,96},{96,0},{1,33},{33,65},{65,97},{97,1},{2,34}... | collective-permute-start | bytes 196616 | tf_op jit(solution)/shard_map/ppermute | solution.py:739
  30.5 4.2 %collective-permute-start.1 = (f32[8,16,128]{2,1,0:T(8,128)S(1)}, f32[8,16,128]{2,1,0:T(8,128)S(1)}, u32[]{:S(2)}, u32[]{:S(2)}) collective-permute-start(f32[8,16,128]{2,1,0:T(8,128)S(1)} %get-tuple-element.33), channel_id=1, source_target_pairs={{32,0},{64,32},{96,64},{0,96},{33,1},{65,33},{97,65},{1,97},{34,2}... | collective-permute-start | bytes 196616 | tf_op jit(solution)/shard_map/ppermute | solution.py:739
  36.6 0.7 copy-start.1
  37.3 13.5 %all-to-all-start.1 = ((f32[32,16,128]{2,1,0:T(8,128)}), f32[32,16,128]{2,1,0:T(8,128)S(1)}, u32[]{:S(2)}, u32[]{:S(2)}) async-start(f32[32,16,128]{2,1,0:T(8,128)} %copy-done.1), calls=%async_computation.1 | async-start | bytes 524288 | tf_op jit(solution)/shard_map/all_to_all | solution.py:731
  77.0 4.3 %collective-permute-start.2 = (f32[8,8,128]{2,1,0:T(8,128)S(1)}, f32[8,8,128]{2,1,0:T(8,128)S(1)}, u32[]{:S(2)}, u32[]{:S(2)}) collective-permute-start(f32[8,8,128]{2,1,0:T(8,128)S(1)} %get-tuple-element.38), channel_id=1, source_target_pairs={{0,32},{32,64},{64,96},{96,0},{1,33},{33,65},{65,97},{97,1},{2,34}... | collective-permute-start | bytes 98312 | tf_op jit(solution)/shard_map/ppermute | solution.py:739
  78.5 3.1 %collective-permute-start.3 = (f32[8,8,128]{2,1,0:T(8,128)S(1)}, f32[8,8,128]{2,1,0:T(8,128)S(1)}, u32[]{:S(2)}, u32[]{:S(2)}) collective-permute-start(f32[8,8,128]{2,1,0:T(8,128)S(1)} %get-tuple-element.39), channel_id=1, source_target_pairs={{32,0},{64,32},{96,64},{0,96},{33,1},{65,33},{97,65},{1,97},{34,2}... | collective-permute-start | bytes 98312 | tf_op jit(solution)/shard_map/ppermute | solution.py:739
  123.1 4.0 %collective-permute-start.4 = (f32[8,8,128]{2,1,0:T(8,128)S(1)}, f32[8,8,128]{2,1,0:T(8,128)S(1)}, u32[]{:S(2)}, u32[]{:S(2)}) collective-permute-start(f32[8,8,128]{2,1,0:T(8,128)S(1)} %get-tuple-element.46), channel_id=1, source_target_pairs={{0,32},{32,64},{64,96},{96,0},{1,33},{33,65},{65,97},{97,1},{2,34}... | collective-permute-start | bytes 98312 | tf_op jit(solution)/shard_map/ppermute | solution.py:739
  124.5 2.8 %collective-permute-start.5 = (f32[8,8,128]{2,1,0:T(8,128)S(1)}, f32[8,8,128]{2,1,0:T(8,128)S(1)}, u32[]{:S(2)}, u32[]{:S(2)}) collective-permute-start(f32[8,8,128]{2,1,0:T(8,128)S(1)} %get-tuple-element.47), channel_id=1, source_target_pairs={{32,0},{64,32},{96,64},{0,96},{33,1},{65,33},{97,65},{1,97},{34,2}... | collective-permute-start | bytes 98312 | tf_op jit(solution)/shard_map/ppermute | solution.py:739

commit v4 on v3

--- a/solution.py
+++ b/solution.py
@@ -11,6 +11,7 @@
 PAIRS = 32
 TILES = 32
 CHUNK = 8
+LONG = 16
 CHUNKS = PAIRS // CHUNK
 TABLE = 72
 CODES = 144
@@ -40,10 +41,6 @@
 
 def held(x):
     return pltpu.with_memory_space_constraint(x, pltpu.VMEM)
-
-
-def stored(*shape, dtype=F32):
-    return pltpu.HBM(shape, dtype)
 
 
 def kept(x):
@@ -171,7 +168,7 @@
     low = (t - high.astype(F32)).astype(BF16)
     out = lax.dot_general(
         jnp.concatenate([high, low], axis=1),
-        weight,
+        jnp.concatenate([weight, weight], axis=0),
         (((1,), (0,)), ((), ())),
         preferred_element_type=F32,
     )
@@ -189,37 +186,47 @@
 CODE_W = 72
 
 
-def make_tables(ocean, table, codes):
+def make_table(ocean, table, count):
     def clear(i, carry):
         table[i] = -1
         return carry
 
-    def clear_codes(i, carry):
-        codes[i] = NONE
+    def clear_count(i, carry):
+        count[i] = 0
         return carry
 
     def place(s, carry):
         t = ocean[s]
-        j = jnp.where(t >= 0, (t >> 5) & 31, 32)
-        held = table[2 * j]
-        before = ocean[jnp.maximum(held, 0)]
-        keep = (held >= 0) & (before < t)
-        table[2 * j] = jnp.where(keep, held, s)
-        table[2 * j + 1] = jnp.where(keep, s, held)
-        return carry
-
-    def code(p, carry):
+        j = jnp.where(t >= 0, (t >> 5) & 31, PAIRS)
+        held = count[j] & 1
+        table[2 * j + held] = s
+        count[j] = held + 1
+        return carry
+
+    lax.fori_loop(0, TABLE, clear, 0, unroll=8)
+    lax.fori_loop(0, PAIRS + 8, clear_count, 0, unroll=8)
+    lax.fori_loop(0, SLOTS, place, 0, unroll=8)
+
+
+def column_codes(ocean, table, codes, j):
+    for r in range(2):
+        p = 2 * j + r
         s = table[p]
         t = ocean[jnp.maximum(s, 0)]
         column, row = t & 7, (t >> 3) & 3
         codes[p + 2] = jnp.where((s >= 0) & (column == 7), row, NONE)
         codes[CODE_W + p] = jnp.where((s >= 0) & (column == 0), row + 4, NONE)
-        return carry
-
-    lax.fori_loop(0, TABLE, clear, 0, unroll=8)
-    lax.fori_loop(0, CODES, clear_codes, 0, unroll=8)
-    lax.fori_loop(0, SLOTS, place, 0, unroll=4)
-    lax.fori_loop(0, 2 * PAIRS, code, 0, unroll=8)
+
+
+def land(source, arrival, first, t):
+    slot = source[t]
+    owner = (slot >> 6) & 31
+    held = first[owner]
+    later = (held >= 0) & (source[jnp.maximum(held, 0)] < slot)
+    arrival[t] = 2 * owner + later.astype(jnp.int32)
+    other = jnp.where(held >= 0, held, TILES)
+    arrival[other] = 2 * owner + 1 - later.astype(jnp.int32)
+    first[owner] = t
 
 
 def put_extras(codes, turned, message_ref, first, stride):
@@ -239,44 +246,46 @@
     lax.fori_loop(0, PAIRS, body, 0, unroll=8)
 
 
-def chunk(ref, i):
-    return ref.at[pl.ds(i * CHUNK, CHUNK)]
-
-
-def outgoing(source, target, sem, i):
-    return pltpu.make_async_copy(chunk(source, i), chunk(target, i), sem.at[i])
-
-
 def first_edges(
-    ocean, u_hbm, z_hbm,
-    message_ref, table, codes, pairs,
-    u_ref, z_ref, acc_v, acc_z, turned, sem_in,
+    ocean, source, u_hbm, z_hbm,
+    message_ref, table, codes, arrival, pairs,
+    u_ref, z_ref, acc_v, acc_z, turned, count, landed, sem_in,
 ):
-    copies = [
-        pltpu.make_async_copy(u_hbm, u_ref, sem_in.at[0]),
-        pltpu.make_async_copy(z_hbm, z_ref, sem_in.at[1]),
-    ]
-    for copy in copies:
-        copy.start()
-    make_tables(ocean, table, codes)
-    for copy in copies:
-        copy.wait()
-
-    def body(i, carry):
+    z_copy = pltpu.make_async_copy(z_hbm, z_ref, sem_in.at[0])
+    u_copy = pltpu.make_async_copy(u_hbm, u_ref, sem_in.at[1])
+    z_copy.start()
+    u_copy.start()
+    make_table(ocean, table, count)
+    for i in (0, 1, CODE_W + 64, CODE_W + 65):
+        codes[i] = NONE
+    for i in range(PAIRS):
+        landed[i] = -1
+    z_copy.wait()
+
+    def scalars(i, carry):
+        for k in range(CHUNK):
+            j = i * CHUNK + k
+            z = load_field(z_ref, table, j, 0.0)
+            pairs[j, 128:192, :] = z
+            put_columns(acc_z, z, j)
+            put_rows(message_ref, jnp.concatenate([z, z], axis=0), 32 * j + 8)
+            column_codes(ocean, table, codes, j)
+        return carry
+
+    def vectors(i, carry):
         for k in range(CHUNK):
             j = i * CHUNK + k
             u, v = load_vector(u_ref, table, j)
-            z = load_field(z_ref, table, j, 0.0)
             vector = jnp.concatenate([u, v], axis=0)
             pairs[j, 0:128, :] = vector
-            pairs[j, 128:192, :] = z
             put_columns(acc_v, vector, j)
-            put_columns(acc_z, z, j)
             put_rows(message_ref, vector, 32 * j)
-            put_rows(message_ref, jnp.concatenate([z, z], axis=0), 32 * j + 8)
-        return carry
-
-    lax.fori_loop(0, CHUNKS, body, 0)
+            land(source, arrival, landed, j)
+        return carry
+
+    lax.fori_loop(0, CHUNKS, scalars, 0)
+    u_copy.wait()
+    lax.fori_loop(0, CHUNKS, vectors, 0)
     columns_to_message(acc_v, turned, message_ref, 0, 32)
     put_extras(codes, turned, message_ref, 16, 32)
     acc_z[64:128, :] = acc_z[0:64, :]
@@ -284,39 +293,22 @@
     put_extras(codes, turned, message_ref, 24, 32)
 
 
-def pair_fields(table, b_hbm, a_hbm, f_hbm, out_hbm, b_ref, a_ref, f_ref, pairs, sem_in, sem_out):
+def prepare(
+    table, p_hbm, b_hbm, a_hbm, f_hbm,
+    weight, b_ref, a_ref, f_ref,
+    p_ref, natural, sem,
+):
     copies = [
-        pltpu.make_async_copy(source, target, sem_in.at[n])
-        for n, (source, target) in enumerate(((b_hbm, b_ref), (a_hbm, a_ref), (f_hbm, f_ref)))
+        pltpu.make_async_copy(source, target, sem.at[n])
+        for n, (source, target) in enumerate(
+            ((p_hbm, p_ref), (b_hbm, b_ref), (a_hbm, a_ref), (f_hbm, f_ref))
+        )
     ]
     for copy in copies:
         copy.start()
-    for copy in copies:
-        copy.wait()
-
-    def body(i, carry):
-        for k in range(CHUNK):
-            j = i * CHUNK + k
-            bu, bv = load_vector(b_ref, table, j)
-            pairs[j, 0:64, :] = bu
-            pairs[j, 64:128, :] = bv
-            pairs[j, 128:192, :] = load_field(a_ref, table, j, 1.0)
-            pairs[j, 192:256, :] = load_field(f_ref, table, j, 0.0)
-        outgoing(pairs, out_hbm, sem_out, i).start()
-        return carry
-
-    lax.fori_loop(0, CHUNKS, body, 0)
-    for i in range(CHUNKS):
-        outgoing(pairs, out_hbm, sem_out, i).wait()
-
-
-def line_weights(table, p_hbm, out_hbm, p_ref, weight, natural, sem_in, sem_out):
-    copy = pltpu.make_async_copy(p_hbm, p_ref, sem_in)
-    copy.start()
-    copy.wait()
     low = iota((32, 128), 1) < 64
 
-    def body(i, carry):
+    def lines(i, carry):
         for k in range(CHUNK):
             j = i * CHUNK + k
             tiles = []
@@ -326,22 +318,21 @@
                 x = p_ref[t // 8, pl.ds(t % 8, 32, stride=8), :]
                 tiles.append(jnp.where(s >= 0, x, 0.0))
             t0, t1 = tiles
+            crossed = roll(jnp.where(low, t1, t0), 64, 1)
             natural[k, pl.ds(0, 32, stride=2), :] = jnp.where(low, t0, 0.0)
-            natural[k, pl.ds(1, 32, stride=2), :] = jnp.where(low, roll(t0, 64, 1), 0.0)
-            natural[k, pl.ds(64, 32, stride=2), :] = jnp.where(low, 0.0, roll(t1, 64, 1))
+            natural[k, pl.ds(1, 32, stride=2), :] = jnp.where(low, crossed, 0.0)
+            natural[k, pl.ds(64, 32, stride=2), :] = jnp.where(low, 0.0, crossed)
             natural[k, pl.ds(65, 32, stride=2), :] = jnp.where(low, 0.0, t1)
             turned = natural[k].T
             high = turned.astype(BF16)
-            rest = (turned - high.astype(F32)).astype(BF16)
-            both = jnp.concatenate([high, rest], axis=1)
-            weight[j, 0:128, :] = both
-            weight[j, 128:256, :] = both
-        outgoing(weight, out_hbm, sem_out, i).start()
-        return carry
-
-    lax.fori_loop(0, CHUNKS, body, 0)
-    for i in range(CHUNKS):
-        outgoing(weight, out_hbm, sem_out, i).wait()
+            weight[j, :, 0:128] = high
+            weight[j, :, 128:256] = (turned - high.astype(F32)).astype(BF16)
+        return carry
+
+    copies[0].wait()
+    lax.fori_loop(0, CHUNKS, lines, 0)
+    for copy in copies[1:]:
+        copy.wait()
 
 
 def side_masks():
@@ -354,19 +345,10 @@
 
 
 def first_step(
-    codes, halo_ref, pairs, fields_hbm, weight_hbm,
-    state, weight, message_ref, edges_ref, rowcoef_ref, colcoef_ref,
-    fields, acc_z, acc_r, hv, hz, turned, sem,
+    table, codes, halo_ref, pairs, b_ref, a_ref, f_ref, weight,
+    state, message_ref, edges_ref,
+    acc_z, acc_r, hv, hz, turned,
 ):
-    def incoming(i):
-        return [
-            pltpu.make_async_copy(chunk(source, i), chunk(target, i), sem.at[n, i])
-            for n, (source, target) in enumerate(((fields_hbm, fields), (weight_hbm, weight)))
-        ]
-
-    for i in range(CHUNKS):
-        for copy in incoming(i):
-            copy.start()
     message_to_columns(halo_ref, turned, hv, 0, 16)
     message_to_columns(halo_ref, turned, hz, 8, 16)
     at_west, at_east = side_masks()
@@ -374,8 +356,9 @@
     def one(j):
         u0 = pairs[j, 0:64, :], pairs[j, 64:128, :]
         z = pairs[j, 128:192, :]
-        b = fields[j, 0:64, :], fields[j, 64:128, :]
-        a, f = fields[j, 128:192, :], fields[j, 192:256, :]
+        b = load_vector(b_ref, table, j)
+        a = load_field(a_ref, table, j, 1.0)
+        f = load_field(f_ref, table, j, 0.0)
         side_v = get_columns(hv[...], j)
         side_z = get_columns(hz[0:64, :], j)
         rows = halo_ref[pl.ds(pl.multiple_of(16 * j, 16), 16), :]
@@ -389,7 +372,7 @@
             diag.append(d)
             scale.append(lax.rsqrt(d))
         turn = f * scale[0] * scale[1]
-        rhat, west, south, column, plain = [], [], [], [], []
+        rhat, west, south, plain = [], [], [], []
         for c in range(2):
             x, s = u0[c], scale[c]
             side = side_v[64 * c : 64 * c + 64]
@@ -407,18 +390,13 @@
             plain.append(residual)
             rhat.append(s * residual)
             k_w = KX[c] * s * face_w
-            k_e = KX[c] * s * face_e
             k_s = KY[c] * s * face_s
             west.append(jnp.where(at_west, 0.0, k_w * roll(s, 1, 1)))
             south.append(k_s * south_of(s, jnp.zeros((1, 128), F32)))
-            column.append(jnp.where(at_west, k_w, k_e))
-            rowcoef_ref[pl.ds(8 * j + 4 + 2 * c, 1), :] = k_s[0:1]
-            rowcoef_ref[pl.ds(8 * j + 5 + 2 * c, 1), :] = KY[c] * s[63:64] * face_n[63:64]
         rhat = jnp.concatenate(rhat, axis=0)
         plain = jnp.concatenate(plain, axis=0)
         west = jnp.concatenate(west, axis=0)
         south = jnp.concatenate(south, axis=0)
-        put_columns(colcoef_ref, jnp.concatenate(column, axis=0), j)
         put_columns(acc_r, plain, j)
         put_rows(edges_ref, plain, 8 * j)
         state[j, 0:128, :] = west
@@ -433,25 +411,22 @@
         put_rows(message_ref, z0, 16 * j)
 
     def body(i, carry):
-        for copy in incoming(i):
-            copy.wait()
-        for k in range(CHUNK):
-            one(i * CHUNK + k)
-        return carry
-
-    lax.fori_loop(0, CHUNKS, body, 0)
+        for k in range(LONG):
+            one(i * LONG + k)
+        return carry
+
+    lax.fori_loop(0, PAIRS // LONG, body, 0)
     columns_to_message(acc_r, turned, edges_ref, 0, 8)
     columns_to_message(acc_z, turned, message_ref, 0, 16)
     put_extras(codes, turned, message_ref, 8, 16)
 
 
 def second_step(
-    codes, halo_ref, rowcoef_ref, colcoef_ref, state, weight,
+    codes, halo_ref, state, weight,
     z1s, message_ref, sums_ref,
     acc_z, acc_p, acc_d, hv, turned,
 ):
     message_to_columns(halo_ref, turned, hv, 0, 16)
-    hv[...] = hv[...] * colcoef_ref[...]
     lane = iota((128, 128), 1) % 64
     at_side = (lane == 0) | (lane == 63)
     first, last = iota((8, 128), 0) == 0, iota((8, 128), 0) == 7
@@ -465,14 +440,14 @@
         root = diag * scale
         y0 = root * state[j, 576:704, :]
         what = tile_part(y0, west, south, turn)
-        what = what - jnp.where(at_side, get_columns(hv[...], j), 0.0)
-        base = pl.multiple_of(8 * j, 8)
-        rows = halo_ref[pl.ds(pl.multiple_of(16 * j, 16), 8), :] * rowcoef_ref[pl.ds(base, 8), :]
+        what = what - jnp.where(at_side, scale * get_columns(hv[...], j), 0.0)
+        rows = halo_ref[pl.ds(pl.multiple_of(16 * j, 16), 8), :]
         fixed = []
         for c in range(2):
             part = what[64 * c : 64 * c + 64]
-            low = part[:8] - jnp.where(first, rows[4 + 2 * c : 5 + 2 * c], 0.0)
-            high = part[56:] - jnp.where(last, rows[5 + 2 * c : 6 + 2 * c], 0.0)
+            s = scale[64 * c : 64 * c + 64]
+            low = part[:8] - jnp.where(first, s[:8] * rows[4 + 2 * c : 5 + 2 * c], 0.0)
+            high = part[56:] - jnp.where(last, s[56:] * rows[5 + 2 * c : 6 + 2 * c], 0.0)
             fixed += [low, part[8:56], high]
         what = jnp.concatenate(fixed, axis=0)
         dhat = what - rhat
@@ -492,11 +467,11 @@
             put_rows(message_ref, x, 32 * j + 8 * k)
 
     def body(i, carry):
-        for k in range(CHUNK):
-            one(i * CHUNK + k)
-        return carry
-
-    lax.fori_loop(0, CHUNKS, body, 0)
+        for k in range(LONG):
+            one(i * LONG + k)
+        return carry
+
+    lax.fori_loop(0, PAIRS // LONG, body, 0)
     columns_to_message(acc_p, turned, message_ref, 8, 32)
     columns_to_message(acc_d, turned, message_ref, 16, 32)
     columns_to_message(acc_z, turned, message_ref, 0, 32)
@@ -576,12 +551,12 @@
                 face_ref[t] = factor * (blocks[t] + halos[t])
 
 
-def second_return(arrival, received_ref, south, north, edges_ref, out_ref):
+def second_return(arrival, received_ref, south, north, edges_ref, face_ref, out_ref):
     out_ref[:, 0:8, :] = jnp.zeros((PAIRS, 8, 128), F32)
     out_ref[:, 8:16, :] = edges_ref[...]
     blocks, halos = tile_halos(arrival, received_ref, south, north, 0, 1)
     for t in range(TILES):
-        hand_back(arrival, t, 0, halos[t], out_ref)
+        hand_back(arrival, t, 0, face_ref[t] * halos[t], out_ref)
 
 
 def edge_sums(arrival, received_ref, south, north, earlier_ref, face_ref, sums_ref, out_ref):
@@ -731,72 +706,66 @@
     return lax.all_to_all(x, "dev", split_axis=0, concat_axis=0, tiled=True)
 
 
-def from_groups(arrival, received, count):
+def boundaries(arrival, received, count):
     side = struct(8, 8 * count, 128)
-    south, north = call(boundary, (side, side), [smem(), vmem()])(arrival, received)
+    return call(boundary, (side, side), [smem(), vmem()])(arrival, received)
+
+
+def from_groups(south, north):
     size = lax.axis_size("grp")
     ahead = [(i, (i + 1) % size) for i in range(size)]
     return lax.ppermute(north, "grp", ahead), lax.ppermute(south, "grp", [(j, i) for i, j in ahead])
 
 
 def shards(velocity, forcing, mass, coriolis, viscosity, lines, tile_source_slot, ocean_tile):
-    owner = tile_source_slot // SLOTS % PAIRS
-    order = jnp.arange(TILES)
-    sooner = (owner[None, :] == owner[:, None]) & (order[None, :] < order[:, None])
-    arrival = owner * 2 + jnp.sum(sooner.astype(jnp.int32), axis=1)
-
     u, b = vector_view(velocity), vector_view(forcing)
     a, f, z, p = [field_view(x) for x in (mass, coriolis, viscosity, lines)]
 
-    message, table, codes, pairs = call(
+    message, table, codes, arrival, pairs = call(
         first_edges,
         (
             struct(PAIRS * 32, 128), struct(TABLE, dtype=jnp.int32), struct(CODES, dtype=jnp.int32),
-            resident(PAIRS, 192, 128),
+            struct(TILES + 8, dtype=jnp.int32), resident(PAIRS, 192, 128),
         ),
-        [smem(), hbm(), hbm()],
-        [buffer(64, 64, 128), buffer(8, 256, 128), square(), square(), square(), sems(2)],
-        (vmem(), smem(), smem(), vmem()),
+        [smem(), smem(), hbm(), hbm()],
+        [
+            buffer(64, 64, 128), buffer(8, 256, 128), square(), square(), square(),
+            pltpu.SMEM((PAIRS + 8,), jnp.int32), pltpu.SMEM((PAIRS,), jnp.int32), sems(2),
+        ],
+        (vmem(), smem(), smem(), smem(), vmem()),
         8,
-    )(kept(ocean_tile), kept(u), kept(z))
-    weight = call(
-        line_weights, stored(PAIRS, 256, 256, dtype=BF16), [smem(), hbm()],
-        [
-            buffer(8, 256, 128), buffer(PAIRS, 256, 256, dtype=BF16), buffer(CHUNK, 128, 128),
-            pltpu.SemaphoreType.DMA, sems(CHUNKS),
-        ],
-        hbm(), 8,
-    )(table, kept(p))
-    fields = call(
-        pair_fields, stored(PAIRS, 256, 128), [smem(), hbm(), hbm(), hbm()],
-        [
-            buffer(64, 64, 128), buffer(8, 256, 128), buffer(8, 256, 128), buffer(PAIRS, 256, 128),
-            sems(3), sems(CHUNKS),
-        ],
-        hbm(), 12,
-    )(table, kept(b), kept(a), kept(f))
+    )(kept(ocean_tile), kept(tile_source_slot), kept(u), kept(z))
 
     received = exchange(message.reshape(PAIRS, 32, 128))
-    received, weight = lax.optimization_barrier((received, weight))
+    south, north = boundaries(arrival, received, 2)
+    south, north, later = lax.optimization_barrier((south, north, table))
+    weight, b, a, f = call(
+        prepare,
+        (
+            resident(PAIRS, 128, 256, dtype=BF16), resident(64, 64, 128),
+            resident(8, 256, 128), resident(8, 256, 128),
+        ),
+        [smem()] + [hbm()] * 4,
+        [buffer(8, 256, 128), buffer(CHUNK, 128, 128), sems(4)],
+        [vmem()] * 4,
+        4,
+    )(later, kept(p), kept(b), kept(a), kept(f))
     halo, face = call(
         first_return, (struct(PAIRS, 16, 128), struct(TILES, 8, 128)), [smem()] + [vmem()] * 3
-    )(arrival, received, *from_groups(arrival, received, 2))
+    )(arrival, received, *from_groups(south, north))
+    halo, weight, b, a, f = lax.optimization_barrier((halo, weight, b, a, f))
     halo = exchange(halo).reshape(PAIRS * 16, 128)
 
-    state, weight, message, edges, rowcoef, colcoef = call(
+    state, message, edges = call(
         first_step,
-        (
-            resident(PAIRS, STATE, 128), resident(PAIRS, 256, 256, dtype=BF16), struct(PAIRS * 16, 128), struct(PAIRS * 8, 128),
-            struct(PAIRS * 8, 128), struct(128, 128),
-        ),
-        [smem(), vmem(), vmem(), hbm(), hbm()],
-        [buffer(PAIRS, 256, 128)] + [square()] * 5 + [sems(2, CHUNKS)],
-        [vmem()] * 6,
-        mebibytes=16,
-    )(codes, halo, held(pairs), kept(fields), kept(weight))
+        (resident(PAIRS, STATE, 128), struct(PAIRS * 16, 128), struct(PAIRS * 8, 128)),
+        [smem()] * 2 + [vmem()] * 6,
+        [square()] * 5,
+        mebibytes=8,
+    )(table, codes, halo, held(pairs), held(b), held(a), held(f), held(weight))
     received = exchange(message.reshape(PAIRS, 16, 128))
-    halo = call(second_return, struct(PAIRS, 16, 128), [smem()] + [vmem()] * 4)(
-        arrival, received, *from_groups(arrival, received, 1), edges.reshape(PAIRS, 8, 128)
+    halo = call(second_return, struct(PAIRS, 16, 128), [smem()] + [vmem()] * 5)(
+        arrival, received, *from_groups(*boundaries(arrival, received, 1)), edges.reshape(PAIRS, 8, 128), face
     )
     earlier = exchange(halo)
     halo = earlier.reshape(PAIRS * 16, 128)
@@ -804,13 +773,13 @@
     z1, message, sums = call(
         second_step,
         (resident(PAIRS, 128, 128), struct(PAIRS * 32, 128), struct(6, 8, 128)),
-        [smem()] + [vmem()] * 5,
+        [smem()] + [vmem()] * 3,
         [square()] * 5,
         mebibytes=8,
-    )(codes, halo, rowcoef, colcoef, held(state), held(weight))
+    )(codes, halo, held(state), held(weight))
     received = exchange(message.reshape(PAIRS, 32, 128))
     partial = call(edge_sums, struct(128, 128), [smem()] + [vmem()] * 6)(
-        arrival, received, *from_groups(arrival, received, 1), earlier, face, sums
+        arrival, received, *from_groups(*boundaries(arrival, received, 1)), earlier, face, sums
     )
     gathered = lax.all_to_all(partial, ("grp", "dev"), split_axis=0, concat_axis=0, tiled=True)
 

time: 148 us -> 144 us (0.973)
  blocking collectives: 58.3 us -> 90.5 us
  starting transfers between devices: 23 us -> 9.74 us
  waiting for transfers between devices: 15.2 us -> 2.53 us
  Pallas kernels: 49.4 us -> 41.2 us
  local copies, waits for them, and re-layouts: 1.49 us -> 0 us
    all_to_all x3 -> x5, blocking collectives: 41.9 us -> 74 us  [exchange(): return lax.all_to_all(x, 'dev', split_axis=0, concat_axis=0, tiled=True)]
    all_to_all x2 -> x0, starting transfers between devices: 13.3 us -> none  [exchange(): return lax.all_to_all(x, 'dev', split_axis=0, concat_axis=0, tiled=True)]
    all_to_all x2 -> x0, waiting for transfers between devices: 10.2 us -> none  [exchange(): return lax.all_to_all(x, 'dev', split_axis=0, concat_axis=0, tiled=True)]
    pallas_call x7 -> x6, Pallas kernels: 26 us -> 17.8 us  [the longest x1 11.6 us: shards(): call(first_step, (resident(PAIRS, STATE, 128), struct(PAIRS * 16, 128), s...]
    ppermute x3, waiting for transfers between devices: 4.52 us -> 2.52 us  [from_groups(): lax.ppermute(north, 'grp', ahead)]
    unnamed x6 -> x0, local copies, waits for them, and re-layouts: 1.49 us -> none
  transfers between devices with their start and end apart: 8 -> 6, of which waited for: 7 -> 2; matrix products, arithmetic and copies ran while one was open for 0% -> 0% of each run, Pallas kernels for 7% -> 2%
where the time goes in v4:
time: 144 us
  blocking collectives  90.5 us (63%)
  Pallas kernels  41.2 us (29%)
  starting transfers between devices  9.74 us (7%)
  waiting for transfers between devices  2.53 us (2%)
    all_to_all x5, blocking collectives, exchange(): return lax.all_to_all(x, 'dev', split_axis=0, concat_axis=0, tiled=True)  74 us
    all_to_all x1, blocking collectives, shards(): lax.all_to_all(partial, ('grp', 'dev'), split_axis=0, concat_axis=0, tile...  16.5 us
    pallas_call x1, Pallas kernels, shards(): call(first_step, (resident(PAIRS, STATE, 128), struct(PAIRS * 16, 128), s...  11.6 us
    pallas_call x1, Pallas kernels, shards(): call(second_step, (resident(PAIRS, 128, 128), struct(PAIRS * 32, 128), st...  11.4 us
    pallas_call x1, Pallas kernels, shards(): call(first_edges, (struct(PAIRS * 32, 128), struct(TABLE, dtype=jnp.int32...  6.5 us
    ppermute x3, starting transfers between devices, from_groups(): lax.ppermute(south, 'grp', [(j, i) for i, j in ahead])  6.42 us
    ppermute x3, starting transfers between devices, from_groups(): lax.ppermute(north, 'grp', ahead)  3.32 us
    pallas_call x1, Pallas kernels, shards(): call(prepare, (resident(PAIRS, 128, 256, dtype=BF16), resident(64, 64, 12...  3.13 us
  transfers between devices with their start and end apart: 6, of which 2 were waited for; matrix products, arithmetic and copies ran while one was open for 0% of the time, Pallas kernels for 2%

profile of v4, /device:TPU:1, one launch (start us, length us, event | category | flops | bytes accessed | tf_op | source)
XLA Modules:
  0.0 144.2 jit_solution(7814501866996948941)
XLA Ops:
  0.0 6.5 %shard_map.82 = (f32[1024,128]{1,0:T(8,128)S(1)}, s32[72]{0:T(128)S(1)}, s32[144]{0:T(256)S(1)}, s32[40]{0:T(128)S(1)}, f32[32,192,128]{2,1,0:T(8,128)S(1)}) custom-call(s32[64]{0:T(128)} %ocean.1, s32[32]{0:T(128)} %source.1, f32[64,64,128]{2,1,0:T(8,128)} %bitcast.53, f32[8,256,128]{2,1,0:T(8,128)} %bitcast.55), custom_call_target="tpu_custom_call" | custom-call | tf_op jit(solution)/shard_map/pallas_call | solution.py:724
  6.5 19.9 %all_to_all.36.received_ref = f32[32,32,128]{2,1,0:T(8,128)S(1)} all-to-all(f32[32,32,128]{2,1,0:T(8,128)S(1)} %bitcast.47), channel_id=1, replica_groups=mesh['grp'=4,'dev'=32] {'dev'}, dimensions={0} | all-to-all | bytes 1048576 | tf_op jit(solution)/shard_map/all_to_all | solution.py:706
  26.4 0.7 shard_map.83
  27.2 1.7 %collective-permute-start = (f32[8,16,128]{2,1,0:T(8,128)S(1)}, f32[8,16,128]{2,1,0:T(8,128)S(1)}, u32[]{:S(2)}, u32[]{:S(2)}) collective-permute-start(f32[8,16,128]{2,1,0:T(8,128)S(1)} %get-tuple-element.42), channel_id=1, source_target_pairs={{0,32},{32,64},{64,96},{96,0},{1,33},{33,65},{65,97},{97,1},{2,34}... | collective-permute-start | bytes 196616 | tf_op jit(solution)/shard_map/ppermute | solution.py:717
  28.9 2.2 %collective-permute-start.1 = (f32[8,16,128]{2,1,0:T(8,128)S(1)}, f32[8,16,128]{2,1,0:T(8,128)S(1)}, u32[]{:S(2)}, u32[]{:S(2)}) collective-permute-start(f32[8,16,128]{2,1,0:T(8,128)S(1)} %get-tuple-element.43), channel_id=1, source_target_pairs={{32,0},{64,32},{96,64},{0,96},{33,1},{65,33},{97,65},{1,97},{34,2}... | collective-permute-start | bytes 196616 | tf_op jit(solution)/shard_map/ppermute | solution.py:717
  31.1 3.1 %shard_map.85 = (bf16[32,128,256]{2,1,0:T(8,128)(2,1)S(1)}, f32[64,64,128]{2,1,0:T(8,128)S(1)}, f32[8,256,128]{2,1,0:T(8,128)S(1)}, f32[8,256,128]{2,1,0:T(8,128)S(1)}) custom-call(s32[72]{0:T(128)S(1)} %get-tuple-element.45.table, f32[8,256,128]{2,1,0:T(8,128)} %bitcast.56, f32[64,64,128]{2,1,0:T(8,128)} %bitcast.54, f32[8,256,128]{2,1,0:T(8,128)} %bitcast.57, ...), custom_call_target="tpu_custom_call" | custom-call | tf_op jit(solution)/shard_map/pallas_call | solution.py:742
  34.2 0.0 collective-permute-done.south
  34.2 0.0 collective-permute-done.1.north
  34.2 1.4 shard_map.84
  35.7 12.8 %all_to_all.37 = f32[32,16,128]{2,1,0:T(8,128)S(1)} all-to-all(f32[32,16,128]{2,1,0:T(8,128)S(1)} %get-tuple-element.50), channel_id=1, replica_groups=mesh['grp'=4,'dev'=32] {'dev'}, dimensions={0} | all-to-all | bytes 524288 | tf_op jit(solution)/shard_map/all_to_all | solution.py:706
  48.5 11.6 %shard_map.86 = (f32[32,704,128]{2,1,0:T(8,128)S(1)}, f32[512,128]{1,0:T(8,128)S(1)}, f32[256,128]{1,0:T(8,128)S(1)}) custom-call(s32[72]{0:T(128)S(1)} %get-tuple-element.45.table, s32[144]{0:T(256)S(1)} %get-tuple-element.38.codes, f32[512,128]{1,0:T(8,128)S(1)} %bitcast.46, f32[32,192,128]{2,1,0:T(8,128)S(1)} %get-tuple-element.51.pairs, ...), custom_call_target="tpu_custom_call" | custom-call | tf_op jit(solution)/shard_map/pallas_call | solution.py:759
  60.1 12.5 %all_to_all.38.received_ref = f32[32,16,128]{2,1,0:T(8,128)S(1)} all-to-all(f32[32,16,128]{2,1,0:T(8,128)S(1)} %bitcast.50), channel_id=1, replica_groups=mesh['grp'=4,'dev'=32] {'dev'}, dimensions={0} | all-to-all | bytes 524288 | tf_op jit(solution)/shard_map/all_to_all | solution.py:706
  72.5 0.7 shard_map.87
  73.2 0.6 collective-permute-start.2
  73.8 2.1 %collective-permute-start.3 = (f32[8,8,128]{2,1,0:T(8,128)S(1)}, f32[8,8,128]{2,1,0:T(8,128)S(1)}, u32[]{:S(2)}, u32[]{:S(2)}) collective-permute-start(f32[8,8,128]{2,1,0:T(8,128)S(1)} %get-tuple-element.58), channel_id=1, source_target_pairs={{32,0},{64,32},{96,64},{0,96},{33,1},{65,33},{97,65},{1,97},{34,2}... | collective-permute-start | bytes 98312 | tf_op jit(solution)/shard_map/ppermute | solution.py:717
  76.0 1.3 collective-permute-done.2.south
  77.3 0.0 collective-permute-done.3.north
  77.3 1.0 shard_map.88
  78.3 13.6 %all_to_all.39.earlier_ref = f32[32,16,128]{2,1,0:T(8,128)S(1)} all-to-all(f32[32,16,128]{2,1,0:T(8,128)S(1)} %shard_map.88), channel_id=1, replica_groups=mesh['grp'=4,'dev'=32] {'dev'}, dimensions={0} | all-to-all | bytes 524288 | tf_op jit(solution)/shard_map/all_to_all | solution.py:706
  91.9 11.4 %shard_map.89 = (f32[32,128,128]{2,1,0:T(8,128)S(1)}, f32[1024,128]{1,0:T(8,128)S(1)}, f32[6,8,128]{2,1,0:T(8,128)S(1)}) custom-call(s32[144]{0:T(256)S(1)} %get-tuple-element.38.codes, f32[512,128]{1,0:T(8,128)S(1)} %bitcast.45, f32[32,704,128]{2,1,0:T(8,128)S(1)} %get-tuple-element.61.state, bf16[32,128,256]{2,1,0:T(8,128)(2,1)S(1)} %get-tuple-element.55.weight), custom_call_target="tpu_custom_call" | custom-call | tf_op jit(solution)/shard_map/pallas_call | solution.py:773
  103.3 15.1 %all_to_all.40.received_ref = f32[32,32,128]{2,1,0:T(8,128)S(1)} all-to-all(f32[32,32,128]{2,1,0:T(8,128)S(1)} %bitcast.48), channel_id=1, replica_groups=mesh['grp'=4,'dev'=32] {'dev'}, dimensions={0} | all-to-all | bytes 1048576 | tf_op jit(solution)/shard_map/all_to_all | solution.py:706
  118.4 0.7 shard_map.90
  119.1 1.0 collective-permute-start.4
  120.1 2.1 %collective-permute-start.5 = (f32[8,8,128]{2,1,0:T(8,128)S(1)}, f32[8,8,128]{2,1,0:T(8,128)S(1)}, u32[]{:S(2)}, u32[]{:S(2)}) collective-permute-start(f32[8,8,128]{2,1,0:T(8,128)S(1)} %get-tuple-element.64), channel_id=1, source_target_pairs={{32,0},{64,32},{96,64},{0,96},{33,1},{65,33},{97,65},{1,97},{34,2}... | collective-permute-start | bytes 98312 | tf_op jit(solution)/shard_map/ppermute | solution.py:717
  122.2 1.2 collective-permute-done.4.south
  123.4 0.0 collective-permute-done.5.north
  123.4 1.2 shard_map.91
  124.6 16.5 %all_to_all.41 = f32[128,1,128]{2,1,0:T(1,128)S(1)} all-to-all(f32[128,1,128]{2,1,0:T(1,128)S(1)} %bitcast.51), channel_id=1, replica_groups=mesh['grp'=4,'dev'=32] {'grp','dev'}, dimensions={0} | all-to-all | bytes 131072 | tf_op jit(solution)/shard_map/all_to_all | solution.py:784
  141.1 2.8 %shard_map.92 = f32[64,64,128]{2,1,0:T(8,128)} custom-call(s32[72]{0:T(128)S(1)} %get-tuple-element.45.table, f32[128,128]{1,0:T(8,128)S(1)} %bitcast.49, f32[32,192,128]{2,1,0:T(8,128)S(1)} %get-tuple-element.51.pairs, f32[32,704,128]{2,1,0:T(8,128)S(1)} %get-tuple-element.61.state, f32[32,128,128]{2,1,0:T(8,128)S(1)} %get-tuple-element.66.z1), custom_call_target="tpu_custom_call" | custom-call | tf_op jit(solution)/shard_map/pallas_call | solution.py:786
Async XLA Ops:
  27.2 7.0 %collective-permute-start = (f32[8,16,128]{2,1,0:T(8,128)S(1)}, f32[8,16,128]{2,1,0:T(8,128)S(1)}, u32[]{:S(2)}, u32[]{:S(2)}) collective-permute-start(f32[8,16,128]{2,1,0:T(8,128)S(1)} %get-tuple-element.42), channel_id=1, source_target_pairs={{0,32},{32,64},{64,96},{96,0},{1,33},{33,65},{65,97},{97,1},{2,34}... | collective-permute-start | bytes 196616 | tf_op jit(solution)/shard_map/ppermute | solution.py:717
  28.9 5.4 %collective-permute-start.1 = (f32[8,16,128]{2,1,0:T(8,128)S(1)}, f32[8,16,128]{2,1,0:T(8,128)S(1)}, u32[]{:S(2)}, u32[]{:S(2)}) collective-permute-start(f32[8,16,128]{2,1,0:T(8,128)S(1)} %get-tuple-element.43), channel_id=1, source_target_pairs={{32,0},{64,32},{96,64},{0,96},{33,1},{65,33},{97,65},{1,97},{34,2}... | collective-permute-start | bytes 196616 | tf_op jit(solution)/shard_map/ppermute | solution.py:717
  73.2 4.0 %collective-permute-start.2 = (f32[8,8,128]{2,1,0:T(8,128)S(1)}, f32[8,8,128]{2,1,0:T(8,128)S(1)}, u32[]{:S(2)}, u32[]{:S(2)}) collective-permute-start(f32[8,8,128]{2,1,0:T(8,128)S(1)} %get-tuple-element.57), channel_id=1, source_target_pairs={{0,32},{32,64},{64,96},{96,0},{1,33},{33,65},{65,97},{97,1},{2,34}... | collective-permute-start | bytes 98312 | tf_op jit(solution)/shard_map/ppermute | solution.py:717
  73.8 3.4 %collective-permute-start.3 = (f32[8,8,128]{2,1,0:T(8,128)S(1)}, f32[8,8,128]{2,1,0:T(8,128)S(1)}, u32[]{:S(2)}, u32[]{:S(2)}) collective-permute-start(f32[8,8,128]{2,1,0:T(8,128)S(1)} %get-tuple-element.58), channel_id=1, source_target_pairs={{32,0},{64,32},{96,64},{0,96},{33,1},{65,33},{97,65},{1,97},{34,2}... | collective-permute-start | bytes 98312 | tf_op jit(solution)/shard_map/ppermute | solution.py:717
  119.1 4.3 %collective-permute-start.4 = (f32[8,8,128]{2,1,0:T(8,128)S(1)}, f32[8,8,128]{2,1,0:T(8,128)S(1)}, u32[]{:S(2)}, u32[]{:S(2)}) collective-permute-start(f32[8,8,128]{2,1,0:T(8,128)S(1)} %get-tuple-element.63), channel_id=1, source_target_pairs={{0,32},{32,64},{64,96},{96,0},{1,33},{33,65},{65,97},{97,1},{2,34}... | collective-permute-start | bytes 98312 | tf_op jit(solution)/shard_map/ppermute | solution.py:717
  120.1 3.3 %collective-permute-start.5 = (f32[8,8,128]{2,1,0:T(8,128)S(1)}, f32[8,8,128]{2,1,0:T(8,128)S(1)}, u32[]{:S(2)}, u32[]{:S(2)}) collective-permute-start(f32[8,8,128]{2,1,0:T(8,128)S(1)} %get-tuple-element.64), channel_id=1, source_target_pairs={{32,0},{64,32},{96,64},{0,96},{33,1},{65,33},{97,65},{1,97},{34,2}... | collective-permute-start | bytes 98312 | tf_op jit(solution)/shard_map/ppermute | solution.py:717

commit v5 on v4

--- a/solution.py
+++ b/solution.py
@@ -11,7 +11,7 @@
 PAIRS = 32
 TILES = 32
 CHUNK = 8
-LONG = 16
+LONG = 32
 CHUNKS = PAIRS // CHUNK
 TABLE = 72
 CODES = 144
@@ -95,8 +95,7 @@
 
 def put_columns(acc_ref, x, j):
     mine = ((iota(x.shape, 1) % 64) // 2) == j
-    rows = slice(0, x.shape[0])
-    acc_ref[rows, :] = jnp.where(mine, roll(x, 2 * j + 1, 1), acc_ref[rows, :])
+    pltpu.store(acc_ref.at[pl.ds(0, x.shape[0])], roll(x, 2 * j + 1, 1), mask=mine)
 
 
 def get_columns(acc, j):
@@ -421,26 +420,55 @@
     put_extras(codes, turned, message_ref, 8, 16)
 
 
+def local_part(state, local):
+    def body(i, carry):
+        for k in range(CHUNK):
+            j = i * CHUNK + k
+            diag = state[j, 256:384, :]
+            y0 = diag * lax.rsqrt(diag) * state[j, 576:704, :]
+            value = tile_part(y0, state[j, 0:128, :], state[j, 128:256, :], state[j, 512:576, :])
+            local[j] = value - state[j, 384:512, :]
+        return carry
+
+    lax.fori_loop(0, CHUNKS, body, 0)
+
+
+def owner_sums(state, d_ref, p_ref, sums_ref):
+    def body(i, carry):
+        totals = [jnp.zeros((8, 128), F32) for _ in range(6)]
+        for k in range(CHUNK):
+            j = i * CHUNK + k
+            diag = state[j, 256:384, :]
+            r = diag * lax.rsqrt(diag) * state[j, 384:512, :]
+            d, p = d_ref[j], p_ref[j]
+            for index, (left, right) in enumerate(((r, r), (r, d), (d, d), (r, p), (d, p), (p, p))):
+                product = left * right
+                for n in range(16):
+                    totals[index] = totals[index] + product[8 * n : 8 * n + 8]
+        for index in range(6):
+            sums_ref[index] += totals[index]
+        return carry
+
+    sums_ref[...] = jnp.zeros((6, 8, 128), F32)
+    lax.fori_loop(0, CHUNKS, body, 0)
+
+
 def second_step(
-    codes, halo_ref, state, weight,
-    z1s, message_ref, sums_ref,
+    codes, halo_ref, state, local, weight,
+    z1s, d_ref, p_ref, message_ref,
     acc_z, acc_p, acc_d, hv, turned,
 ):
     message_to_columns(halo_ref, turned, hv, 0, 16)
     lane = iota((128, 128), 1) % 64
     at_side = (lane == 0) | (lane == 63)
     first, last = iota((8, 128), 0) == 0, iota((8, 128), 0) == 7
-    sums_ref[...] = jnp.zeros((6, 8, 128), F32)
 
     def one(j):
         west, south, turn = state[j, 0:128, :], state[j, 128:256, :], state[j, 512:576, :]
         diag = state[j, 256:384, :]
-        rhat = state[j, 384:512, :]
         scale = lax.rsqrt(diag)
         root = diag * scale
-        y0 = root * state[j, 576:704, :]
-        what = tile_part(y0, west, south, turn)
-        what = what - jnp.where(at_side, scale * get_columns(hv[...], j), 0.0)
+        what = local[j] - jnp.where(at_side, scale * get_columns(hv[...], j), 0.0)
         rows = halo_ref[pl.ds(pl.multiple_of(16 * j, 16), 8), :]
         fixed = []
         for c in range(2):
@@ -449,19 +477,14 @@
             low = part[:8] - jnp.where(first, s[:8] * rows[4 + 2 * c : 5 + 2 * c], 0.0)
             high = part[56:] - jnp.where(last, s[56:] * rows[5 + 2 * c : 6 + 2 * c], 0.0)
             fixed += [low, part[8:56], high]
-        what = jnp.concatenate(fixed, axis=0)
-        dhat = what - rhat
+        dhat = jnp.concatenate(fixed, axis=0)
         y1 = relax(dhat, weight[j], west, south, turn)
         phat = tile_part(y1, west, south, turn) - dhat
         z1 = scale * y1
         z1s[j] = z1
-        r, d, p = root * rhat, root * dhat, root * phat
-        for index, (left, right) in enumerate(((r, r), (r, d), (d, d), (r, p), (d, p), (p, p))):
-            product = left * right
-            total = product[0:8]
-            for k in range(1, 16):
-                total = total + product[8 * k : 8 * k + 8]
-            sums_ref[index] += total
+        d, p = root * dhat, root * phat
+        d_ref[j] = d
+        p_ref[j] = p
         for k, (acc, x) in enumerate(((acc_z, z1), (acc_p, p), (acc_d, d))):
             put_columns(acc, x, j)
             put_rows(message_ref, x, 32 * j + 8 * k)
@@ -764,22 +787,30 @@
         mebibytes=8,
     )(table, codes, halo, held(pairs), held(b), held(a), held(f), held(weight))
     received = exchange(message.reshape(PAIRS, 16, 128))
+    south, north = boundaries(arrival, received, 1)
+    south, north, state = lax.optimization_barrier((south, north, state))
+    whole = resident(PAIRS, 128, 128)
+    local = call(local_part, whole, [vmem()], (), vmem())(held(state))
     halo = call(second_return, struct(PAIRS, 16, 128), [smem()] + [vmem()] * 5)(
-        arrival, received, *from_groups(*boundaries(arrival, received, 1)), edges.reshape(PAIRS, 8, 128), face
+        arrival, received, *from_groups(south, north), edges.reshape(PAIRS, 8, 128), face
     )
+    halo, local = lax.optimization_barrier((halo, local))
     earlier = exchange(halo)
     halo = earlier.reshape(PAIRS * 16, 128)
 
-    z1, message, sums = call(
+    z1, d, p, message = call(
         second_step,
-        (resident(PAIRS, 128, 128), struct(PAIRS * 32, 128), struct(6, 8, 128)),
-        [smem()] + [vmem()] * 3,
+        (whole, whole, whole, struct(PAIRS * 32, 128)),
+        [smem()] + [vmem()] * 4,
         [square()] * 5,
         mebibytes=8,
-    )(codes, halo, held(state), held(weight))
+    )(codes, halo, held(state), held(local), held(weight))
     received = exchange(message.reshape(PAIRS, 32, 128))
+    south, north = boundaries(arrival, received, 1)
+    south, north, d = lax.optimization_barrier((south, north, d))
+    sums = call(owner_sums, struct(6, 8, 128), [vmem()] * 3)(held(state), held(d), held(p))
     partial = call(edge_sums, struct(128, 128), [smem()] + [vmem()] * 6)(
-        arrival, received, *from_groups(*boundaries(arrival, received, 1)), earlier, face, sums
+        arrival, received, *from_groups(south, north), earlier, face, sums
     )
     gathered = lax.all_to_all(partial, ("grp", "dev"), split_axis=0, concat_axis=0, tiled=True)
 

time: 144 us -> 143 us (level)
  waiting for transfers between devices: 2.53 us -> 0.02 us
    ppermute x3, waiting for transfers between devices: 2.52 us -> 0.01 us  [from_groups(): lax.ppermute(north, 'grp', ahead)]
    pallas_call x1 -> x3, Pallas kernels: 11.4 us -> 12.9 us  [the longest x1 9.89 us: shards(): call(second_step, (whole, whole, whole, struct(PAIRS * 32, 128)), [smem()...]
  transfers between devices with their start and end apart: 6 -> 6, of which waited for: 2 -> 0; matrix products, arithmetic and copies ran while one was open for 0% -> 0% of each run, Pallas kernels for 2% -> 4%
where the time goes in v5:
time: 143 us
  blocking collectives  90.2 us (63%)
  Pallas kernels  42.6 us (30%)
  starting transfers between devices  9.74 us (7%)
    all_to_all x5, blocking collectives, exchange(): return lax.all_to_all(x, 'dev', split_axis=0, concat_axis=0, tiled=True)  73.9 us
    all_to_all x1, blocking collectives, shards(): lax.all_to_all(partial, ('grp', 'dev'), split_axis=0, concat_axis=0, tile...  16.2 us
    pallas_call x1, Pallas kernels, shards(): call(first_step, (resident(PAIRS, STATE, 128), struct(PAIRS * 16, 128), s...  11.4 us
    pallas_call x1, Pallas kernels, shards(): call(second_step, (whole, whole, whole, struct(PAIRS * 32, 128)), [smem()...  9.89 us
    pallas_call x1, Pallas kernels, shards(): call(first_edges, (struct(PAIRS * 32, 128), struct(TABLE, dtype=jnp.int32...  6.5 us
    ppermute x3, starting transfers between devices, from_groups(): lax.ppermute(south, 'grp', [(j, i) for i, j in ahead])  6.42 us
    ppermute x3, starting transfers between devices, from_groups(): lax.ppermute(north, 'grp', ahead)  3.32 us
    pallas_call x1, Pallas kernels, shards(): call(prepare, (resident(PAIRS, 128, 256, dtype=BF16), resident(64, 64, 12...  3.13 us
  transfers between devices with their start and end apart: 6, of which 0 were waited for; matrix products, arithmetic and copies ran while one was open for 0% of the time, Pallas kernels for 4%

profile of v5, /device:TPU:1, one launch (start us, length us, event | category | flops | bytes accessed | tf_op | source)
XLA Modules:
  0.0 142.8 jit_solution(15349352376808741298)
XLA Ops:
  0.0 6.5 %shard_map.82 = (f32[1024,128]{1,0:T(8,128)S(1)}, s32[72]{0:T(128)S(1)}, s32[144]{0:T(256)S(1)}, s32[40]{0:T(128)S(1)}, f32[32,192,128]{2,1,0:T(8,128)S(1)}) custom-call(s32[64]{0:T(128)} %ocean.1, s32[32]{0:T(128)} %source.1, f32[64,64,128]{2,1,0:T(8,128)} %bitcast.53, f32[8,256,128]{2,1,0:T(8,128)} %bitcast.55), custom_call_target="tpu_custom_call" | custom-call | tf_op jit(solution)/shard_map/pallas_call | solution.py:747
  6.5 19.9 %all_to_all.36.received_ref = f32[32,32,128]{2,1,0:T(8,128)S(1)} all-to-all(f32[32,32,128]{2,1,0:T(8,128)S(1)} %bitcast.48), channel_id=1, replica_groups=mesh['grp'=4,'dev'=32] {'dev'}, dimensions={0} | all-to-all | bytes 1048576 | tf_op jit(solution)/shard_map/all_to_all | solution.py:729
  26.5 0.7 shard_map.83
  27.2 1.7 %collective-permute-start = (f32[8,16,128]{2,1,0:T(8,128)S(1)}, f32[8,16,128]{2,1,0:T(8,128)S(1)}, u32[]{:S(2)}, u32[]{:S(2)}) collective-permute-start(f32[8,16,128]{2,1,0:T(8,128)S(1)} %get-tuple-element.51), channel_id=1, source_target_pairs={{0,32},{32,64},{64,96},{96,0},{1,33},{33,65},{65,97},{97,1},{2,34}... | collective-permute-start | bytes 196616 | tf_op jit(solution)/shard_map/ppermute | solution.py:740
  28.9 2.2 %collective-permute-start.1 = (f32[8,16,128]{2,1,0:T(8,128)S(1)}, f32[8,16,128]{2,1,0:T(8,128)S(1)}, u32[]{:S(2)}, u32[]{:S(2)}) collective-permute-start(f32[8,16,128]{2,1,0:T(8,128)S(1)} %get-tuple-element.52), channel_id=1, source_target_pairs={{32,0},{64,32},{96,64},{0,96},{33,1},{65,33},{97,65},{1,97},{34,2}... | collective-permute-start | bytes 196616 | tf_op jit(solution)/shard_map/ppermute | solution.py:740
  31.1 3.1 %shard_map.85 = (bf16[32,128,256]{2,1,0:T(8,128)(2,1)S(1)}, f32[64,64,128]{2,1,0:T(8,128)S(1)}, f32[8,256,128]{2,1,0:T(8,128)S(1)}, f32[8,256,128]{2,1,0:T(8,128)S(1)}) custom-call(s32[72]{0:T(128)S(1)} %get-tuple-element.54.table, f32[8,256,128]{2,1,0:T(8,128)} %bitcast.56, f32[64,64,128]{2,1,0:T(8,128)} %bitcast.54, f32[8,256,128]{2,1,0:T(8,128)} %bitcast.57, ...), custom_call_target="tpu_custom_call" | custom-call | tf_op jit(solution)/shard_map/pallas_call | solution.py:765
  34.2 0.0 collective-permute-done.south
  34.2 0.0 collective-permute-done.1.north
  34.2 1.4 %shard_map.84 = (f32[32,16,128]{2,1,0:T(8,128)S(1)}, f32[32,8,128]{2,1,0:T(8,128)S(1)}) custom-call(s32[40]{0:T(128)S(1)} %get-tuple-element.46.arrival, f32[32,32,128]{2,1,0:T(8,128)S(1)} %all_to_all.36.received_ref, f32[8,16,128]{2,1,0:T(8,128)S(1)} %collective-permute-done.south, f32[8,16,128]{2,1,0:T(8,128)S(1)} %collective-permute-done.1.north), custom_call_target="tpu_custom_call" | custom-call | tf_op jit(solution)/shard_map/pallas_call | solution.py:776
  35.7 12.8 %all_to_all.37 = f32[32,16,128]{2,1,0:T(8,128)S(1)} all-to-all(f32[32,16,128]{2,1,0:T(8,128)S(1)} %get-tuple-element.59), channel_id=1, replica_groups=mesh['grp'=4,'dev'=32] {'dev'}, dimensions={0} | all-to-all | bytes 524288 | tf_op jit(solution)/shard_map/all_to_all | solution.py:729
  48.5 11.4 %shard_map.86 = (f32[32,704,128]{2,1,0:T(8,128)S(1)}, f32[512,128]{1,0:T(8,128)S(1)}, f32[256,128]{1,0:T(8,128)S(1)}) custom-call(s32[72]{0:T(128)S(1)} %get-tuple-element.54.table, s32[144]{0:T(256)S(1)} %get-tuple-element.47.codes, f32[512,128]{1,0:T(8,128)S(1)} %bitcast.46, f32[32,192,128]{2,1,0:T(8,128)S(1)} %get-tuple-element.60.pairs, ...), custom_call_target="tpu_custom_call" | custom-call | tf_op jit(solution)/shard_map/pallas_call | solution.py:782
  60.0 12.5 %all_to_all.38.received_ref = f32[32,16,128]{2,1,0:T(8,128)S(1)} all-to-all(f32[32,16,128]{2,1,0:T(8,128)S(1)} %bitcast.50), channel_id=1, replica_groups=mesh['grp'=4,'dev'=32] {'dev'}, dimensions={0} | all-to-all | bytes 524288 | tf_op jit(solution)/shard_map/all_to_all | solution.py:729
  72.4 0.7 shard_map.87
  73.1 0.6 collective-permute-start.2
  73.7 2.1 %collective-permute-start.3 = (f32[8,8,128]{2,1,0:T(8,128)S(1)}, f32[8,8,128]{2,1,0:T(8,128)S(1)}, u32[]{:S(2)}, u32[]{:S(2)}) collective-permute-start(f32[8,8,128]{2,1,0:T(8,128)S(1)} %get-tuple-element.70), channel_id=1, source_target_pairs={{32,0},{64,32},{96,64},{0,96},{33,1},{65,33},{97,65},{1,97},{34,2}... | collective-permute-start | bytes 98312 | tf_op jit(solution)/shard_map/ppermute | solution.py:740
  75.9 1.5 %shard_map.89.local = f32[32,128,128]{2,1,0:T(8,128)S(1)} custom-call(f32[32,704,128]{2,1,0:T(8,128)S(1)} %get-tuple-element.73.state), custom_call_target="tpu_custom_call" | custom-call | tf_op jit(solution)/shard_map/pallas_call | solution.py:793
  77.4 0.0 collective-permute-done.2.south
  77.4 0.0 collective-permute-done.3.north
  77.4 1.0 shard_map.88
  78.4 13.6 %all_to_all.39.earlier_ref = f32[32,16,128]{2,1,0:T(8,128)S(1)} all-to-all(f32[32,16,128]{2,1,0:T(8,128)S(1)} %shard_map.88), channel_id=1, replica_groups=mesh['grp'=4,'dev'=32] {'dev'}, dimensions={0} | all-to-all | bytes 524288 | tf_op jit(solution)/shard_map/all_to_all | solution.py:729
  92.0 9.9 %shard_map.90 = (f32[32,128,128]{2,1,0:T(8,128)S(1)}, f32[32,128,128]{2,1,0:T(8,128)S(1)}, f32[32,128,128]{2,1,0:T(8,128)S(1)}, f32[1024,128]{1,0:T(8,128)S(1)}) custom-call(s32[144]{0:T(256)S(1)} %get-tuple-element.47.codes, f32[512,128]{1,0:T(8,128)S(1)} %bitcast.45, f32[32,704,128]{2,1,0:T(8,128)S(1)} %get-tuple-element.73.state, ...), custom_call_target="tpu_custom_call" | custom-call | tf_op jit(solution)/shard_map/pallas_call | solution.py:801
  101.9 15.1 %all_to_all.40.received_ref = f32[32,32,128]{2,1,0:T(8,128)S(1)} all-to-all(f32[32,32,128]{2,1,0:T(8,128)S(1)} %bitcast.47), channel_id=1, replica_groups=mesh['grp'=4,'dev'=32] {'dev'}, dimensions={0} | all-to-all | bytes 1048576 | tf_op jit(solution)/shard_map/all_to_all | solution.py:729
  117.0 0.7 shard_map.91
  117.7 1.0 collective-permute-start.4
  118.7 2.1 %collective-permute-start.5 = (f32[8,8,128]{2,1,0:T(8,128)S(1)}, f32[8,8,128]{2,1,0:T(8,128)S(1)}, u32[]{:S(2)}, u32[]{:S(2)}) collective-permute-start(f32[8,8,128]{2,1,0:T(8,128)S(1)} %get-tuple-element.81), channel_id=1, source_target_pairs={{32,0},{64,32},{96,64},{0,96},{33,1},{65,33},{97,65},{1,97},{34,2}... | collective-permute-start | bytes 98312 | tf_op jit(solution)/shard_map/ppermute | solution.py:740
  120.8 1.5 %shard_map.92.sums_ref = f32[6,8,128]{2,1,0:T(8,128)S(1)} custom-call(f32[32,704,128]{2,1,0:T(8,128)S(1)} %get-tuple-element.73.state, f32[32,128,128]{2,1,0:T(8,128)S(1)} %get-tuple-element.82.d_ref, f32[32,128,128]{2,1,0:T(8,128)S(1)} %get-tuple-element.83.p_ref), custom_call_target="tpu_custom_call" | custom-call | tf_op jit(solution)/shard_map/pallas_call | solution.py:811
  122.3 0.0 collective-permute-done.4.south
  122.3 0.0 collective-permute-done.5.north
  122.3 1.3 shard_map.93
  123.6 16.2 %all_to_all.41 = f32[128,1,128]{2,1,0:T(1,128)S(1)} all-to-all(f32[128,1,128]{2,1,0:T(1,128)S(1)} %bitcast.51), channel_id=1, replica_groups=mesh['grp'=4,'dev'=32] {'grp','dev'}, dimensions={0} | all-to-all | bytes 131072 | tf_op jit(solution)/shard_map/all_to_all | solution.py:815
  139.8 2.8 %shard_map.94 = f32[64,64,128]{2,1,0:T(8,128)} custom-call(s32[72]{0:T(128)S(1)} %get-tuple-element.54.table, f32[128,128]{1,0:T(8,128)S(1)} %bitcast.49, f32[32,192,128]{2,1,0:T(8,128)S(1)} %get-tuple-element.60.pairs, f32[32,704,128]{2,1,0:T(8,128)S(1)} %get-tuple-element.73.state, f32[32,128,128]{2,1,0:T(8,128)S(1)} %get-tuple-element.84.z1), custom_call_target="tpu_custom_call" | custom-call | tf_op jit(solution)/shard_map/pallas_call | solution.py:817
Async XLA Ops:
  27.2 7.0 %collective-permute-start = (f32[8,16,128]{2,1,0:T(8,128)S(1)}, f32[8,16,128]{2,1,0:T(8,128)S(1)}, u32[]{:S(2)}, u32[]{:S(2)}) collective-permute-start(f32[8,16,128]{2,1,0:T(8,128)S(1)} %get-tuple-element.51), channel_id=1, source_target_pairs={{0,32},{32,64},{64,96},{96,0},{1,33},{33,65},{65,97},{97,1},{2,34}... | collective-permute-start | bytes 196616 | tf_op jit(solution)/shard_map/ppermute | solution.py:740
  28.9 5.4 %collective-permute-start.1 = (f32[8,16,128]{2,1,0:T(8,128)S(1)}, f32[8,16,128]{2,1,0:T(8,128)S(1)}, u32[]{:S(2)}, u32[]{:S(2)}) collective-permute-start(f32[8,16,128]{2,1,0:T(8,128)S(1)} %get-tuple-element.52), channel_id=1, source_target_pairs={{32,0},{64,32},{96,64},{0,96},{33,1},{65,33},{97,65},{1,97},{34,2}... | collective-permute-start | bytes 196616 | tf_op jit(solution)/shard_map/ppermute | solution.py:740
  73.1 4.3 %collective-permute-start.2 = (f32[8,8,128]{2,1,0:T(8,128)S(1)}, f32[8,8,128]{2,1,0:T(8,128)S(1)}, u32[]{:S(2)}, u32[]{:S(2)}) collective-permute-start(f32[8,8,128]{2,1,0:T(8,128)S(1)} %get-tuple-element.69), channel_id=1, source_target_pairs={{0,32},{32,64},{64,96},{96,0},{1,33},{33,65},{65,97},{97,1},{2,34}... | collective-permute-start | bytes 98312 | tf_op jit(solution)/shard_map/ppermute | solution.py:740
  73.7 3.7 %collective-permute-start.3 = (f32[8,8,128]{2,1,0:T(8,128)S(1)}, f32[8,8,128]{2,1,0:T(8,128)S(1)}, u32[]{:S(2)}, u32[]{:S(2)}) collective-permute-start(f32[8,8,128]{2,1,0:T(8,128)S(1)} %get-tuple-element.70), channel_id=1, source_target_pairs={{32,0},{64,32},{96,64},{0,96},{33,1},{65,33},{97,65},{1,97},{34,2}... | collective-permute-start | bytes 98312 | tf_op jit(solution)/shard_map/ppermute | solution.py:740
  117.7 4.6 %collective-permute-start.4 = (f32[8,8,128]{2,1,0:T(8,128)S(1)}, f32[8,8,128]{2,1,0:T(8,128)S(1)}, u32[]{:S(2)}, u32[]{:S(2)}) collective-permute-start(f32[8,8,128]{2,1,0:T(8,128)S(1)} %get-tuple-element.80), channel_id=1, source_target_pairs={{0,32},{32,64},{64,96},{96,0},{1,33},{33,65},{65,97},{97,1},{2,34}... | collective-permute-start | bytes 98312 | tf_op jit(solution)/shard_map/ppermute | solution.py:740
  118.7 3.6 %collective-permute-start.5 = (f32[8,8,128]{2,1,0:T(8,128)S(1)}, f32[8,8,128]{2,1,0:T(8,128)S(1)}, u32[]{:S(2)}, u32[]{:S(2)}) collective-permute-start(f32[8,8,128]{2,1,0:T(8,128)S(1)} %get-tuple-element.81), channel_id=1, source_target_pairs={{32,0},{64,32},{96,64},{0,96},{33,1},{65,33},{97,65},{1,97},{34,2}... | collective-permute-start | bytes 98312 | tf_op jit(solution)/shard_map/ppermute | solution.py:740

commit v6 on v5

--- a/solution.py
+++ b/solution.py
@@ -246,8 +246,8 @@
 
 
 def first_edges(
-    ocean, source, u_hbm, z_hbm,
-    message_ref, table, codes, arrival, pairs,
+    ocean, source, u_hbm, z_hbm, p_hbm, b_hbm, a_hbm, f_hbm,
+    message_ref, table, codes, arrival, pairs, p_ref, b_ref, a_ref, f_ref,
     u_ref, z_ref, acc_v, acc_z, turned, count, landed, sem_in,
 ):
     z_copy = pltpu.make_async_copy(z_hbm, z_ref, sem_in.at[0])
@@ -284,27 +284,25 @@
 
     lax.fori_loop(0, CHUNKS, scalars, 0)
     u_copy.wait()
+    later = [
+        pltpu.make_async_copy(origin, target, sem_in.at[2 + n])
+        for n, (origin, target) in enumerate(
+            ((p_hbm, p_ref), (b_hbm, b_ref), (a_hbm, a_ref), (f_hbm, f_ref))
+        )
+    ]
+    for copy in later:
+        copy.start()
     lax.fori_loop(0, CHUNKS, vectors, 0)
     columns_to_message(acc_v, turned, message_ref, 0, 32)
     put_extras(codes, turned, message_ref, 16, 32)
     acc_z[64:128, :] = acc_z[0:64, :]
     columns_to_message(acc_z, turned, message_ref, 8, 32)
     put_extras(codes, turned, message_ref, 24, 32)
-
-
-def prepare(
-    table, p_hbm, b_hbm, a_hbm, f_hbm,
-    weight, b_ref, a_ref, f_ref,
-    p_ref, natural, sem,
-):
-    copies = [
-        pltpu.make_async_copy(source, target, sem.at[n])
-        for n, (source, target) in enumerate(
-            ((p_hbm, p_ref), (b_hbm, b_ref), (a_hbm, a_ref), (f_hbm, f_ref))
-        )
-    ]
-    for copy in copies:
-        copy.start()
+    for copy in later:
+        copy.wait()
+
+
+def prepare(table, p_ref, weight, natural):
     low = iota((32, 128), 1) < 64
 
     def lines(i, carry):
@@ -328,10 +326,7 @@
             weight[j, :, 128:256] = (turned - high.astype(F32)).astype(BF16)
         return carry
 
-    copies[0].wait()
     lax.fori_loop(0, CHUNKS, lines, 0)
-    for copy in copies[1:]:
-        copy.wait()
 
 
 def side_masks():
@@ -345,8 +340,8 @@
 
 def first_step(
     table, codes, halo_ref, pairs, b_ref, a_ref, f_ref, weight,
-    state, message_ref, edges_ref,
-    acc_z, acc_r, hv, hz, turned,
+    state, message_ref,
+    acc_z, hv, hz, turned,
 ):
     message_to_columns(halo_ref, turned, hv, 0, 16)
     message_to_columns(halo_ref, turned, hz, 8, 16)
@@ -371,7 +366,7 @@
             diag.append(d)
             scale.append(lax.rsqrt(d))
         turn = f * scale[0] * scale[1]
-        rhat, west, south, plain = [], [], [], []
+        rhat, west, south = [], [], []
         for c in range(2):
             x, s = u0[c], scale[c]
             side = side_v[64 * c : 64 * c + 64]
@@ -385,19 +380,14 @@
                 - KX[c] * (face_w * x_w + face_e * x_e)
                 - KY[c] * (face_s * x_s + face_n * x_n)
             )
-            residual = b[c] - applied
-            plain.append(residual)
-            rhat.append(s * residual)
+            rhat.append(s * (b[c] - applied))
             k_w = KX[c] * s * face_w
             k_s = KY[c] * s * face_s
             west.append(jnp.where(at_west, 0.0, k_w * roll(s, 1, 1)))
             south.append(k_s * south_of(s, jnp.zeros((1, 128), F32)))
         rhat = jnp.concatenate(rhat, axis=0)
-        plain = jnp.concatenate(plain, axis=0)
         west = jnp.concatenate(west, axis=0)
         south = jnp.concatenate(south, axis=0)
-        put_columns(acc_r, plain, j)
-        put_rows(edges_ref, plain, 8 * j)
         state[j, 0:128, :] = west
         state[j, 128:256, :] = south
         state[j, 256:384, :] = jnp.concatenate(diag, axis=0)
@@ -415,22 +405,26 @@
         return carry
 
     lax.fori_loop(0, PAIRS // LONG, body, 0)
-    columns_to_message(acc_r, turned, edges_ref, 0, 8)
     columns_to_message(acc_z, turned, message_ref, 0, 16)
     put_extras(codes, turned, message_ref, 8, 16)
 
 
-def local_part(state, local):
+def local_part(state, local, edges_ref, acc, turned):
     def body(i, carry):
         for k in range(CHUNK):
             j = i * CHUNK + k
             diag = state[j, 256:384, :]
-            y0 = diag * lax.rsqrt(diag) * state[j, 576:704, :]
-            value = tile_part(y0, state[j, 0:128, :], state[j, 128:256, :], state[j, 512:576, :])
-            local[j] = value - state[j, 384:512, :]
+            root = diag * lax.rsqrt(diag)
+            rhat = state[j, 384:512, :]
+            y0 = root * state[j, 576:704, :]
+            local[j] = tile_part(y0, state[j, 0:128, :], state[j, 128:256, :], state[j, 512:576, :]) - rhat
+            r = root * rhat
+            put_columns(acc, r, j)
+            put_rows(edges_ref, r, 8 * j)
         return carry
 
     lax.fori_loop(0, CHUNKS, body, 0)
+    columns_to_message(acc, turned, edges_ref, 0, 8)
 
 
 def owner_sums(state, d_ref, p_ref, sums_ref):
@@ -744,53 +738,49 @@
     u, b = vector_view(velocity), vector_view(forcing)
     a, f, z, p = [field_view(x) for x in (mass, coriolis, viscosity, lines)]
 
-    message, table, codes, arrival, pairs = call(
+    tiles, vectors = resident(8, 256, 128), resident(64, 64, 128)
+    message, table, codes, arrival, pairs, p, b, a, f = call(
         first_edges,
         (
             struct(PAIRS * 32, 128), struct(TABLE, dtype=jnp.int32), struct(CODES, dtype=jnp.int32),
-            struct(TILES + 8, dtype=jnp.int32), resident(PAIRS, 192, 128),
+            struct(TILES + 8, dtype=jnp.int32), resident(PAIRS, 192, 128), tiles, vectors, tiles, tiles,
         ),
-        [smem(), smem(), hbm(), hbm()],
+        [smem(), smem()] + [hbm()] * 6,
         [
             buffer(64, 64, 128), buffer(8, 256, 128), square(), square(), square(),
-            pltpu.SMEM((PAIRS + 8,), jnp.int32), pltpu.SMEM((PAIRS,), jnp.int32), sems(2),
+            pltpu.SMEM((PAIRS + 8,), jnp.int32), pltpu.SMEM((PAIRS,), jnp.int32), sems(6),
         ],
-        (vmem(), smem(), smem(), smem(), vmem()),
+        (vmem(), smem(), smem(), smem()) + (vmem(),) * 5,
         8,
-    )(kept(ocean_tile), kept(tile_source_slot), kept(u), kept(z))
+    )(*[kept(x) for x in (ocean_tile, tile_source_slot, u, z, p, b, a, f)])
 
     received = exchange(message.reshape(PAIRS, 32, 128))
     south, north = boundaries(arrival, received, 2)
-    south, north, later = lax.optimization_barrier((south, north, table))
-    weight, b, a, f = call(
-        prepare,
-        (
-            resident(PAIRS, 128, 256, dtype=BF16), resident(64, 64, 128),
-            resident(8, 256, 128), resident(8, 256, 128),
-        ),
-        [smem()] + [hbm()] * 4,
-        [buffer(8, 256, 128), buffer(CHUNK, 128, 128), sems(4)],
-        [vmem()] * 4,
-        4,
-    )(later, kept(p), kept(b), kept(a), kept(f))
+    south, north, p = lax.optimization_barrier((south, north, p))
+    weight = call(
+        prepare, resident(PAIRS, 128, 256, dtype=BF16), [smem(), vmem()],
+        [buffer(CHUNK, 128, 128)], vmem(),
+    )(table, held(p))
     halo, face = call(
         first_return, (struct(PAIRS, 16, 128), struct(TILES, 8, 128)), [smem()] + [vmem()] * 3
     )(arrival, received, *from_groups(south, north))
-    halo, weight, b, a, f = lax.optimization_barrier((halo, weight, b, a, f))
+    halo, weight = lax.optimization_barrier((halo, weight))
     halo = exchange(halo).reshape(PAIRS * 16, 128)
 
-    state, message, edges = call(
+    state, message = call(
         first_step,
-        (resident(PAIRS, STATE, 128), struct(PAIRS * 16, 128), struct(PAIRS * 8, 128)),
+        (resident(PAIRS, STATE, 128), struct(PAIRS * 16, 128)),
         [smem()] * 2 + [vmem()] * 6,
-        [square()] * 5,
+        [square()] * 4,
         mebibytes=8,
     )(table, codes, halo, held(pairs), held(b), held(a), held(f), held(weight))
     received = exchange(message.reshape(PAIRS, 16, 128))
     south, north = boundaries(arrival, received, 1)
     south, north, state = lax.optimization_barrier((south, north, state))
     whole = resident(PAIRS, 128, 128)
-    local = call(local_part, whole, [vmem()], (), vmem())(held(state))
+    local, edges = call(
+        local_part, (whole, struct(PAIRS * 8, 128)), [vmem()], [square(), square()]
+    )(held(state))
     halo = call(second_return, struct(PAIRS, 16, 128), [smem()] + [vmem()] * 5)(
         arrival, received, *from_groups(south, north), edges.reshape(PAIRS, 8, 128), face
     )

time: 143 us -> 142 us (level)
  transfers between devices with their start and end apart: 6 -> 6, of which waited for: 0 -> 1; matrix products, arithmetic and copies ran while one was open for 0% -> 0% of each run, Pallas kernels for 4% -> 4%
where the time goes in v6:
time: 142 us
  blocking collectives  89.7 us (63%)
  Pallas kernels  41.6 us (29%)
  starting transfers between devices  9.82 us (7%)
    all_to_all x5, blocking collectives, exchange(): return lax.all_to_all(x, 'dev', split_axis=0, concat_axis=0, tiled=True)  73.4 us
    all_to_all x1, blocking collectives, shards(): lax.all_to_all(partial, ('grp', 'dev'), split_axis=0, concat_axis=0, tile...  16.3 us
    pallas_call x1, Pallas kernels, shards(): call(first_step, (resident(PAIRS, STATE, 128), struct(PAIRS * 16, 128)),...  11 us
    pallas_call x1, Pallas kernels, shards(): call(second_step, (whole, whole, whole, struct(PAIRS * 32, 128)), [smem()...  9.99 us
    pallas_call x1, Pallas kernels, shards(): call(first_edges, (struct(PAIRS * 32, 128), struct(TABLE, dtype=jnp.int32...  6.56 us
    ppermute x3, starting transfers between devices, from_groups(): lax.ppermute(south, 'grp', [(j, i) for i, j in ahead])  5.1 us
    ppermute x3, starting transfers between devices, from_groups(): lax.ppermute(north, 'grp', ahead)  4.71 us
  transfers between devices with their start and end apart: 6, of which 1 were waited for; matrix products, arithmetic and copies ran while one was open for 0% of the time, Pallas kernels for 4%

profile of v6, /device:TPU:1, one launch (start us, length us, event | category | flops | bytes accessed | tf_op | source)
XLA Modules:
  0.0 141.5 jit_solution(10386819426857827815)
XLA Ops:
  0.0 6.6 %shard_map.82 = (f32[1024,128]{1,0:T(8,128)S(1)}, s32[72]{0:T(128)S(1)}, s32[144]{0:T(256)S(1)}, s32[40]{0:T(128)S(1)}, f32[32,192,128]{2,1,0:T(8,128)S(1)}, /*i...) custom-call(s32[64]{0:T(128)} %ocean.1, ...), custom_call_target="tpu_custom_call" | custom-call | tf_op jit(solution)/shard_map/pallas_call | solution.py:742
  6.6 19.9 %all_to_all.36.received_ref = f32[32,32,128]{2,1,0:T(8,128)S(1)} all-to-all(f32[32,32,128]{2,1,0:T(8,128)S(1)} %bitcast.47), channel_id=1, replica_groups=mesh['grp'=4,'dev'=32] {'dev'}, dimensions={0} | all-to-all | bytes 1048576 | tf_op jit(solution)/shard_map/all_to_all | solution.py:723
  26.5 0.7 shard_map.83
  27.2 1.7 %collective-permute-start = (f32[8,16,128]{2,1,0:T(8,128)S(1)}, f32[8,16,128]{2,1,0:T(8,128)S(1)}, u32[]{:S(2)}, u32[]{:S(2)}) collective-permute-start(f32[8,16,128]{2,1,0:T(8,128)S(1)} %get-tuple-element.50), channel_id=1, source_target_pairs={{0,32},{32,64},{64,96},{96,0},{1,33},{33,65},{65,97},{97,1},{2,34}... | collective-permute-start | bytes 196616 | tf_op jit(solution)/shard_map/ppermute | solution.py:734
  28.9 2.2 %collective-permute-start.1 = (f32[8,16,128]{2,1,0:T(8,128)S(1)}, f32[8,16,128]{2,1,0:T(8,128)S(1)}, u32[]{:S(2)}, u32[]{:S(2)}) collective-permute-start(f32[8,16,128]{2,1,0:T(8,128)S(1)} %get-tuple-element.51), channel_id=1, source_target_pairs={{32,0},{64,32},{96,64},{0,96},{33,1},{65,33},{97,65},{1,97},{34,2}... | collective-permute-start | bytes 196616 | tf_op jit(solution)/shard_map/ppermute | solution.py:734
  31.1 1.9 %shard_map.85.weight = bf16[32,128,256]{2,1,0:T(8,128)(2,1)S(1)} custom-call(s32[72]{0:T(128)S(1)} %get-tuple-element.43.table, f32[8,256,128]{2,1,0:T(8,128)S(1)} %get-tuple-element.53.p_ref), custom_call_target="tpu_custom_call" | custom-call | tf_op jit(solution)/shard_map/pallas_call | solution.py:760
  33.0 0.1 collective-permute-done.south
  33.1 0.0 collective-permute-done.1.north
  33.1 1.4 %shard_map.84 = (f32[32,16,128]{2,1,0:T(8,128)S(1)}, f32[32,8,128]{2,1,0:T(8,128)S(1)}) custom-call(s32[40]{0:T(128)S(1)} %get-tuple-element.44.arrival, f32[32,32,128]{2,1,0:T(8,128)S(1)} %all_to_all.36.received_ref, f32[8,16,128]{2,1,0:T(8,128)S(1)} %collective-permute-done.south, f32[8,16,128]{2,1,0:T(8,128)S(1)} %collective-permute-done.1.north), custom_call_target="tpu_custom_call" | custom-call | tf_op jit(solution)/shard_map/pallas_call | solution.py:764
  34.6 13.0 %all_to_all.37 = f32[32,16,128]{2,1,0:T(8,128)S(1)} all-to-all(f32[32,16,128]{2,1,0:T(8,128)S(1)} %get-tuple-element.54), channel_id=1, replica_groups=mesh['grp'=4,'dev'=32] {'dev'}, dimensions={0} | all-to-all | bytes 524288 | tf_op jit(solution)/shard_map/all_to_all | solution.py:723
  47.6 11.0 %shard_map.86 = (f32[32,704,128]{2,1,0:T(8,128)S(1)}, f32[512,128]{1,0:T(8,128)S(1)}) custom-call(s32[72]{0:T(128)S(1)} %get-tuple-element.43.table, s32[144]{0:T(256)S(1)} %get-tuple-element.45.codes, f32[512,128]{1,0:T(8,128)S(1)} %bitcast.46, f32[32,192,128]{2,1,0:T(8,128)S(1)} %get-tuple-element.55.pairs, f32[64,64,128]{2,1,0:T(8,128)S(1)} %get-tuple-element.56.b_ref, ...), custom_call_target="tpu_custom_call" | custom-call | tf_op jit(solution)/shard_map/pallas_call | solution.py:770
  58.6 12.5 %all_to_all.38.received_ref = f32[32,16,128]{2,1,0:T(8,128)S(1)} all-to-all(f32[32,16,128]{2,1,0:T(8,128)S(1)} %bitcast.50), channel_id=1, replica_groups=mesh['grp'=4,'dev'=32] {'dev'}, dimensions={0} | all-to-all | bytes 524288 | tf_op jit(solution)/shard_map/all_to_all | solution.py:723
  71.1 0.7 shard_map.87
  71.7 1.6 %collective-permute-start.2 = (f32[8,8,128]{2,1,0:T(8,128)S(1)}, f32[8,8,128]{2,1,0:T(8,128)S(1)}, u32[]{:S(2)}, u32[]{:S(2)}) collective-permute-start(f32[8,8,128]{2,1,0:T(8,128)S(1)} %get-tuple-element.64), channel_id=1, source_target_pairs={{0,32},{32,64},{64,96},{96,0},{1,33},{33,65},{65,97},{97,1},{2,34}... | collective-permute-start | bytes 98312 | tf_op jit(solution)/shard_map/ppermute | solution.py:734
  73.3 1.6 %collective-permute-start.3 = (f32[8,8,128]{2,1,0:T(8,128)S(1)}, f32[8,8,128]{2,1,0:T(8,128)S(1)}, u32[]{:S(2)}, u32[]{:S(2)}) collective-permute-start(f32[8,8,128]{2,1,0:T(8,128)S(1)} %get-tuple-element.65), channel_id=1, source_target_pairs={{32,0},{64,32},{96,64},{0,96},{33,1},{65,33},{97,65},{1,97},{34,2}... | collective-permute-start | bytes 98312 | tf_op jit(solution)/shard_map/ppermute | solution.py:734
  74.9 2.2 %shard_map.88 = (f32[32,128,128]{2,1,0:T(8,128)S(1)}, f32[256,128]{1,0:T(8,128)S(1)}) custom-call(f32[32,704,128]{2,1,0:T(8,128)S(1)} %get-tuple-element.66.state), custom_call_target="tpu_custom_call" | custom-call | tf_op jit(solution)/shard_map/pallas_call | solution.py:781
  77.1 0.0 collective-permute-done.2.south
  77.1 0.0 collective-permute-done.3.north
  77.1 1.0 shard_map.89
  78.2 12.8 %all_to_all.39.earlier_ref = f32[32,16,128]{2,1,0:T(8,128)S(1)} all-to-all(f32[32,16,128]{2,1,0:T(8,128)S(1)} %shard_map.89), channel_id=1, replica_groups=mesh['grp'=4,'dev'=32] {'dev'}, dimensions={0} | all-to-all | bytes 524288 | tf_op jit(solution)/shard_map/all_to_all | solution.py:723
  91.0 10.0 %shard_map.90 = (f32[32,128,128]{2,1,0:T(8,128)S(1)}, f32[32,128,128]{2,1,0:T(8,128)S(1)}, f32[32,128,128]{2,1,0:T(8,128)S(1)}, f32[1024,128]{1,0:T(8,128)S(1)}) custom-call(s32[144]{0:T(256)S(1)} %get-tuple-element.45.codes, f32[512,128]{1,0:T(8,128)S(1)} %bitcast.45, f32[32,704,128]{2,1,0:T(8,128)S(1)} %get-tuple-element.66.state, ...), custom_call_target="tpu_custom_call" | custom-call | tf_op jit(solution)/shard_map/pallas_call | solution.py:791
  101.0 15.1 %all_to_all.40.received_ref = f32[32,32,128]{2,1,0:T(8,128)S(1)} all-to-all(f32[32,32,128]{2,1,0:T(8,128)S(1)} %bitcast.48), channel_id=1, replica_groups=mesh['grp'=4,'dev'=32] {'dev'}, dimensions={0} | all-to-all | bytes 1048576 | tf_op jit(solution)/shard_map/all_to_all | solution.py:723
  116.1 0.7 shard_map.91
  116.8 1.4 %collective-permute-start.4 = (f32[8,8,128]{2,1,0:T(8,128)S(1)}, f32[8,8,128]{2,1,0:T(8,128)S(1)}, u32[]{:S(2)}, u32[]{:S(2)}) collective-permute-start(f32[8,8,128]{2,1,0:T(8,128)S(1)} %get-tuple-element.76), channel_id=1, source_target_pairs={{0,32},{32,64},{64,96},{96,0},{1,33},{33,65},{65,97},{97,1},{2,34}... | collective-permute-start | bytes 98312 | tf_op jit(solution)/shard_map/ppermute | solution.py:734
  118.2 1.3 collective-permute-start.5
  119.6 1.5 %shard_map.92.sums_ref = f32[6,8,128]{2,1,0:T(8,128)S(1)} custom-call(f32[32,704,128]{2,1,0:T(8,128)S(1)} %get-tuple-element.66.state, f32[32,128,128]{2,1,0:T(8,128)S(1)} %get-tuple-element.78.d_ref, f32[32,128,128]{2,1,0:T(8,128)S(1)} %get-tuple-element.79.p_ref), custom_call_target="tpu_custom_call" | custom-call | tf_op jit(solution)/shard_map/pallas_call | solution.py:801
  121.0 0.0 collective-permute-done.4.south
  121.0 0.0 collective-permute-done.5.north
  121.0 1.3 shard_map.93
  122.3 16.3 %all_to_all.41 = f32[128,1,128]{2,1,0:T(1,128)S(1)} all-to-all(f32[128,1,128]{2,1,0:T(1,128)S(1)} %bitcast.51), channel_id=1, replica_groups=mesh['grp'=4,'dev'=32] {'grp','dev'}, dimensions={0} | all-to-all | bytes 131072 | tf_op jit(solution)/shard_map/all_to_all | solution.py:805
  138.6 2.7 %shard_map.94 = f32[64,64,128]{2,1,0:T(8,128)} custom-call(s32[72]{0:T(128)S(1)} %get-tuple-element.43.table, f32[128,128]{1,0:T(8,128)S(1)} %bitcast.49, f32[32,192,128]{2,1,0:T(8,128)S(1)} %get-tuple-element.55.pairs, f32[32,704,128]{2,1,0:T(8,128)S(1)} %get-tuple-element.66.state, f32[32,128,128]{2,1,0:T(8,128)S(1)} %get-tuple-element.80.z1), custom_call_target="tpu_custom_call" | custom-call | tf_op jit(solution)/shard_map/pallas_call | solution.py:807
Async XLA Ops:
  27.2 5.9 %collective-permute-start = (f32[8,16,128]{2,1,0:T(8,128)S(1)}, f32[8,16,128]{2,1,0:T(8,128)S(1)}, u32[]{:S(2)}, u32[]{:S(2)}) collective-permute-start(f32[8,16,128]{2,1,0:T(8,128)S(1)} %get-tuple-element.50), channel_id=1, source_target_pairs={{0,32},{32,64},{64,96},{96,0},{1,33},{33,65},{65,97},{97,1},{2,34}... | collective-permute-start | bytes 196616 | tf_op jit(solution)/shard_map/ppermute | solution.py:734
  28.9 4.2 %collective-permute-start.1 = (f32[8,16,128]{2,1,0:T(8,128)S(1)}, f32[8,16,128]{2,1,0:T(8,128)S(1)}, u32[]{:S(2)}, u32[]{:S(2)}) collective-permute-start(f32[8,16,128]{2,1,0:T(8,128)S(1)} %get-tuple-element.51), channel_id=1, source_target_pairs={{32,0},{64,32},{96,64},{0,96},{33,1},{65,33},{97,65},{1,97},{34,2}... | collective-permute-start | bytes 196616 | tf_op jit(solution)/shard_map/ppermute | solution.py:734
  71.7 5.4 %collective-permute-start.2 = (f32[8,8,128]{2,1,0:T(8,128)S(1)}, f32[8,8,128]{2,1,0:T(8,128)S(1)}, u32[]{:S(2)}, u32[]{:S(2)}) collective-permute-start(f32[8,8,128]{2,1,0:T(8,128)S(1)} %get-tuple-element.64), channel_id=1, source_target_pairs={{0,32},{32,64},{64,96},{96,0},{1,33},{33,65},{65,97},{97,1},{2,34}... | collective-permute-start | bytes 98312 | tf_op jit(solution)/shard_map/ppermute | solution.py:734
  73.3 3.8 %collective-permute-start.3 = (f32[8,8,128]{2,1,0:T(8,128)S(1)}, f32[8,8,128]{2,1,0:T(8,128)S(1)}, u32[]{:S(2)}, u32[]{:S(2)}) collective-permute-start(f32[8,8,128]{2,1,0:T(8,128)S(1)} %get-tuple-element.65), channel_id=1, source_target_pairs={{32,0},{64,32},{96,64},{0,96},{33,1},{65,33},{97,65},{1,97},{34,2}... | collective-permute-start | bytes 98312 | tf_op jit(solution)/shard_map/ppermute | solution.py:734
  116.8 4.2 %collective-permute-start.4 = (f32[8,8,128]{2,1,0:T(8,128)S(1)}, f32[8,8,128]{2,1,0:T(8,128)S(1)}, u32[]{:S(2)}, u32[]{:S(2)}) collective-permute-start(f32[8,8,128]{2,1,0:T(8,128)S(1)} %get-tuple-element.76), channel_id=1, source_target_pairs={{0,32},{32,64},{64,96},{96,0},{1,33},{33,65},{65,97},{97,1},{2,34}... | collective-permute-start | bytes 98312 | tf_op jit(solution)/shard_map/ppermute | solution.py:734
  118.2 2.8 %collective-permute-start.5 = (f32[8,8,128]{2,1,0:T(8,128)S(1)}, f32[8,8,128]{2,1,0:T(8,128)S(1)}, u32[]{:S(2)}, u32[]{:S(2)}) collective-permute-start(f32[8,8,128]{2,1,0:T(8,128)S(1)} %get-tuple-element.77), channel_id=1, source_target_pairs={{32,0},{64,32},{96,64},{0,96},{33,1},{65,33},{97,65},{1,97},{34,2}... | collective-permute-start | bytes 98312 | tf_op jit(solution)/shard_map/ppermute | solution.py:734

commit v7 on v6

--- a/solution.py
+++ b/solution.py
@@ -302,7 +302,7 @@
         copy.wait()
 
 
-def prepare(table, p_ref, weight, natural):
+def prepare(table, p_ref, a_ref, f_ref, weight, fields, natural):
     low = iota((32, 128), 1) < 64
 
     def lines(i, carry):
@@ -324,6 +324,8 @@
             high = turned.astype(BF16)
             weight[j, :, 0:128] = high
             weight[j, :, 128:256] = (turned - high.astype(F32)).astype(BF16)
+            fields[j, 0:64, :] = load_field(a_ref, table, j, 1.0)
+            fields[j, 64:128, :] = load_field(f_ref, table, j, 0.0)
         return carry
 
     lax.fori_loop(0, CHUNKS, lines, 0)
@@ -339,7 +341,7 @@
 
 
 def first_step(
-    table, codes, halo_ref, pairs, b_ref, a_ref, f_ref, weight,
+    table, codes, halo_ref, pairs, b_ref, fields, weight,
     state, message_ref,
     acc_z, hv, hz, turned,
 ):
@@ -351,8 +353,7 @@
         u0 = pairs[j, 0:64, :], pairs[j, 64:128, :]
         z = pairs[j, 128:192, :]
         b = load_vector(b_ref, table, j)
-        a = load_field(a_ref, table, j, 1.0)
-        f = load_field(f_ref, table, j, 0.0)
+        a, f = fields[j, 0:64, :], fields[j, 64:128, :]
         side_v = get_columns(hv[...], j)
         side_z = get_columns(hz[0:64, :], j)
         rows = halo_ref[pl.ds(pl.multiple_of(16 * j, 16), 16), :]
@@ -757,23 +758,23 @@
     received = exchange(message.reshape(PAIRS, 32, 128))
     south, north = boundaries(arrival, received, 2)
     south, north, p = lax.optimization_barrier((south, north, p))
-    weight = call(
-        prepare, resident(PAIRS, 128, 256, dtype=BF16), [smem(), vmem()],
-        [buffer(CHUNK, 128, 128)], vmem(),
-    )(table, held(p))
+    weight, fields = call(
+        prepare, (resident(PAIRS, 128, 256, dtype=BF16), resident(PAIRS, 128, 128)), [smem()] + [vmem()] * 3,
+        [buffer(CHUNK, 128, 128)],
+    )(table, held(p), held(a), held(f))
     halo, face = call(
         first_return, (struct(PAIRS, 16, 128), struct(TILES, 8, 128)), [smem()] + [vmem()] * 3
     )(arrival, received, *from_groups(south, north))
-    halo, weight = lax.optimization_barrier((halo, weight))
+    halo, weight, fields = lax.optimization_barrier((halo, weight, fields))
     halo = exchange(halo).reshape(PAIRS * 16, 128)
 
     state, message = call(
         first_step,
         (resident(PAIRS, STATE, 128), struct(PAIRS * 16, 128)),
-        [smem()] * 2 + [vmem()] * 6,
+        [smem()] * 2 + [vmem()] * 5,
         [square()] * 4,
         mebibytes=8,
-    )(table, codes, halo, held(pairs), held(b), held(a), held(f), held(weight))
+    )(table, codes, halo, held(pairs), held(b), held(fields), held(weight))
     received = exchange(message.reshape(PAIRS, 16, 128))
     south, north = boundaries(arrival, received, 1)
     south, north, state = lax.optimization_barrier((south, north, state))

time: 142 us -> 142 us (level)
    ppermute x3, starting transfers between devices: 4.71 us -> 2.88 us  [from_groups(): lax.ppermute(north, 'grp', ahead)]
    ppermute x3, starting transfers between devices: 5.1 us -> 6.53 us  [from_groups(): lax.ppermute(south, 'grp', [(j, i) for i, j in ahead])]
  transfers between devices with their start and end apart: 6 -> 6, of which waited for: 1 -> 0; matrix products, arithmetic and copies ran while one was open for 0% -> 0% of each run, Pallas kernels for 4% -> 5%
where the time goes in v7:
time: 142 us; the launch traced here: 141 us
  blocking collectives  89.7 us (63%)
  Pallas kernels  41.8 us (29%)
  starting transfers between devices  9.41 us (7%)
    all_to_all x5, blocking collectives, exchange(): return lax.all_to_all(x, 'dev', split_axis=0, concat_axis=0, tiled=True)  73.4 us
    all_to_all x1, blocking collectives, shards(): lax.all_to_all(partial, ('grp', 'dev'), split_axis=0, concat_axis=0, tile...  16.3 us
    pallas_call x1, Pallas kernels, shards(): call(second_step, (whole, whole, whole, struct(PAIRS * 32, 128)), [smem()...  9.99 us
    pallas_call x1, Pallas kernels, shards(): call(first_step, (resident(PAIRS, STATE, 128), struct(PAIRS * 16, 128)),...  9.89 us
    pallas_call x1, Pallas kernels, shards(): call(first_edges, (struct(PAIRS * 32, 128), struct(TABLE, dtype=jnp.int32...  6.56 us
    ppermute x3, starting transfers between devices, from_groups(): lax.ppermute(south, 'grp', [(j, i) for i, j in ahead])  6.53 us
    pallas_call x1, Pallas kernels, shards(): call(prepare, (resident(PAIRS, 128, 256, dtype=BF16), resident(PAIRS, 128...  3.19 us
    ppermute x3, starting transfers between devices, from_groups(): lax.ppermute(north, 'grp', ahead)  2.88 us
  transfers between devices with their start and end apart: 6, of which 0 were waited for; matrix products, arithmetic and copies ran while one was open for 0% of the time, Pallas kernels for 5%

profile of v7, /device:TPU:1, one launch (start us, length us, event | category | flops | bytes accessed | tf_op | source)
XLA Modules:
  0.0 141.2 jit_solution(11760672206062055577)
XLA Ops:
  0.0 6.6 %shard_map.82 = (f32[1024,128]{1,0:T(8,128)S(1)}, s32[72]{0:T(128)S(1)}, s32[144]{0:T(256)S(1)}, s32[40]{0:T(128)S(1)}, f32[32,192,128]{2,1,0:T(8,128)S(1)}, /*i...) custom-call(s32[64]{0:T(128)} %ocean.1, ...), custom_call_target="tpu_custom_call" | custom-call | tf_op jit(solution)/shard_map/pallas_call | solution.py:743
  6.6 19.9 %all_to_all.36.received_ref = f32[32,32,128]{2,1,0:T(8,128)S(1)} all-to-all(f32[32,32,128]{2,1,0:T(8,128)S(1)} %bitcast.47), channel_id=1, replica_groups=mesh['grp'=4,'dev'=32] {'dev'}, dimensions={0} | all-to-all | bytes 1048576 | tf_op jit(solution)/shard_map/all_to_all | solution.py:724
  26.5 0.7 shard_map.83
  27.2 1.7 %collective-permute-start = (f32[8,16,128]{2,1,0:T(8,128)S(1)}, f32[8,16,128]{2,1,0:T(8,128)S(1)}, u32[]{:S(2)}, u32[]{:S(2)}) collective-permute-start(f32[8,16,128]{2,1,0:T(8,128)S(1)} %get-tuple-element.53), channel_id=1, source_target_pairs={{0,32},{32,64},{64,96},{96,0},{1,33},{33,65},{65,97},{97,1},{2,34}... | collective-permute-start | bytes 196616 | tf_op jit(solution)/shard_map/ppermute | solution.py:735
  28.9 2.2 %collective-permute-start.1 = (f32[8,16,128]{2,1,0:T(8,128)S(1)}, f32[8,16,128]{2,1,0:T(8,128)S(1)}, u32[]{:S(2)}, u32[]{:S(2)}) collective-permute-start(f32[8,16,128]{2,1,0:T(8,128)S(1)} %get-tuple-element.54), channel_id=1, source_target_pairs={{32,0},{64,32},{96,64},{0,96},{33,1},{65,33},{97,65},{1,97},{34,2}... | collective-permute-start | bytes 196616 | tf_op jit(solution)/shard_map/ppermute | solution.py:735
  31.1 3.2 %shard_map.85 = (bf16[32,128,256]{2,1,0:T(8,128)(2,1)S(1)}, f32[32,128,128]{2,1,0:T(8,128)S(1)}) custom-call(s32[72]{0:T(128)S(1)} %get-tuple-element.46.table, f32[8,256,128]{2,1,0:T(8,128)S(1)} %get-tuple-element.56.p_ref, f32[8,256,128]{2,1,0:T(8,128)S(1)} %get-tuple-element.57.a_ref, f32[8,256,128]{2,1,0:T(8,128)S(1)} %get-tuple-element.58.f_ref), custom_call_target="tpu_custom_call" | custom-call | tf_op jit(solution)/shard_map/pallas_call | solution.py:761
  34.3 0.0 collective-permute-done.south
  34.3 0.0 collective-permute-done.1.north
  34.3 1.4 %shard_map.84 = (f32[32,16,128]{2,1,0:T(8,128)S(1)}, f32[32,8,128]{2,1,0:T(8,128)S(1)}) custom-call(s32[40]{0:T(128)S(1)} %get-tuple-element.47.arrival, f32[32,32,128]{2,1,0:T(8,128)S(1)} %all_to_all.36.received_ref, f32[8,16,128]{2,1,0:T(8,128)S(1)} %collective-permute-done.south, f32[8,16,128]{2,1,0:T(8,128)S(1)} %collective-permute-done.1.north), custom_call_target="tpu_custom_call" | custom-call | tf_op jit(solution)/shard_map/pallas_call | solution.py:765
  35.8 12.8 %all_to_all.37 = f32[32,16,128]{2,1,0:T(8,128)S(1)} all-to-all(f32[32,16,128]{2,1,0:T(8,128)S(1)} %get-tuple-element.61), channel_id=1, replica_groups=mesh['grp'=4,'dev'=32] {'dev'}, dimensions={0} | all-to-all | bytes 524288 | tf_op jit(solution)/shard_map/all_to_all | solution.py:724
  48.6 9.9 %shard_map.86 = (f32[32,704,128]{2,1,0:T(8,128)S(1)}, f32[512,128]{1,0:T(8,128)S(1)}) custom-call(s32[72]{0:T(128)S(1)} %get-tuple-element.46.table, s32[144]{0:T(256)S(1)} %get-tuple-element.48.codes, f32[512,128]{1,0:T(8,128)S(1)} %bitcast.46, f32[32,192,128]{2,1,0:T(8,128)S(1)} %get-tuple-element.62.pairs, f32[64,64,128]{2,1,0:T(8,128)S(1)} %get-tuple-element.63.b_ref, ...), custom_call_target="tpu_custom_call" | custom-call | tf_op jit(solution)/shard_map/pallas_call | solution.py:771
  58.5 12.5 %all_to_all.38.received_ref = f32[32,16,128]{2,1,0:T(8,128)S(1)} all-to-all(f32[32,16,128]{2,1,0:T(8,128)S(1)} %bitcast.50), channel_id=1, replica_groups=mesh['grp'=4,'dev'=32] {'dev'}, dimensions={0} | all-to-all | bytes 524288 | tf_op jit(solution)/shard_map/all_to_all | solution.py:724
  71.0 0.7 shard_map.87
  71.7 0.5 collective-permute-start.2
  72.2 2.2 %collective-permute-start.3 = (f32[8,8,128]{2,1,0:T(8,128)S(1)}, f32[8,8,128]{2,1,0:T(8,128)S(1)}, u32[]{:S(2)}, u32[]{:S(2)}) collective-permute-start(f32[8,8,128]{2,1,0:T(8,128)S(1)} %get-tuple-element.71), channel_id=1, source_target_pairs={{32,0},{64,32},{96,64},{0,96},{33,1},{65,33},{97,65},{1,97},{34,2}... | collective-permute-start | bytes 98312 | tf_op jit(solution)/shard_map/ppermute | solution.py:735
  74.4 2.2 %shard_map.88 = (f32[32,128,128]{2,1,0:T(8,128)S(1)}, f32[256,128]{1,0:T(8,128)S(1)}) custom-call(f32[32,704,128]{2,1,0:T(8,128)S(1)} %get-tuple-element.72.state), custom_call_target="tpu_custom_call" | custom-call | tf_op jit(solution)/shard_map/pallas_call | solution.py:782
  76.6 0.0 collective-permute-done.2.south
  76.6 0.0 collective-permute-done.3.north
  76.7 1.0 shard_map.89
  77.7 13.0 %all_to_all.39.earlier_ref = f32[32,16,128]{2,1,0:T(8,128)S(1)} all-to-all(f32[32,16,128]{2,1,0:T(8,128)S(1)} %shard_map.89), channel_id=1, replica_groups=mesh['grp'=4,'dev'=32] {'dev'}, dimensions={0} | all-to-all | bytes 524288 | tf_op jit(solution)/shard_map/all_to_all | solution.py:724
  90.7 10.0 %shard_map.90 = (f32[32,128,128]{2,1,0:T(8,128)S(1)}, f32[32,128,128]{2,1,0:T(8,128)S(1)}, f32[32,128,128]{2,1,0:T(8,128)S(1)}, f32[1024,128]{1,0:T(8,128)S(1)}) custom-call(s32[144]{0:T(256)S(1)} %get-tuple-element.48.codes, f32[512,128]{1,0:T(8,128)S(1)} %bitcast.45, f32[32,704,128]{2,1,0:T(8,128)S(1)} %get-tuple-element.72.state, ...), custom_call_target="tpu_custom_call" | custom-call | tf_op jit(solution)/shard_map/pallas_call | solution.py:792
  100.7 15.1 %all_to_all.40.received_ref = f32[32,32,128]{2,1,0:T(8,128)S(1)} all-to-all(f32[32,32,128]{2,1,0:T(8,128)S(1)} %bitcast.48), channel_id=1, replica_groups=mesh['grp'=4,'dev'=32] {'dev'}, dimensions={0} | all-to-all | bytes 1048576 | tf_op jit(solution)/shard_map/all_to_all | solution.py:724
  115.8 0.7 shard_map.91
  116.5 0.6 collective-permute-start.4
  117.1 2.1 %collective-permute-start.5 = (f32[8,8,128]{2,1,0:T(8,128)S(1)}, f32[8,8,128]{2,1,0:T(8,128)S(1)}, u32[]{:S(2)}, u32[]{:S(2)}) collective-permute-start(f32[8,8,128]{2,1,0:T(8,128)S(1)} %get-tuple-element.83), channel_id=1, source_target_pairs={{32,0},{64,32},{96,64},{0,96},{33,1},{65,33},{97,65},{1,97},{34,2}... | collective-permute-start | bytes 98312 | tf_op jit(solution)/shard_map/ppermute | solution.py:735
  119.3 1.5 %shard_map.92.sums_ref = f32[6,8,128]{2,1,0:T(8,128)S(1)} custom-call(f32[32,704,128]{2,1,0:T(8,128)S(1)} %get-tuple-element.72.state, f32[32,128,128]{2,1,0:T(8,128)S(1)} %get-tuple-element.84.d_ref, f32[32,128,128]{2,1,0:T(8,128)S(1)} %get-tuple-element.85.p_ref), custom_call_target="tpu_custom_call" | custom-call | tf_op jit(solution)/shard_map/pallas_call | solution.py:802
  120.7 0.0 collective-permute-done.4.south
  120.7 0.0 collective-permute-done.5.north
  120.8 1.3 shard_map.93
  122.0 16.3 %all_to_all.41 = f32[128,1,128]{2,1,0:T(1,128)S(1)} all-to-all(f32[128,1,128]{2,1,0:T(1,128)S(1)} %bitcast.51), channel_id=1, replica_groups=mesh['grp'=4,'dev'=32] {'grp','dev'}, dimensions={0} | all-to-all | bytes 131072 | tf_op jit(solution)/shard_map/all_to_all | solution.py:806
  138.3 2.7 %shard_map.94 = f32[64,64,128]{2,1,0:T(8,128)} custom-call(s32[72]{0:T(128)S(1)} %get-tuple-element.46.table, f32[128,128]{1,0:T(8,128)S(1)} %bitcast.49, f32[32,192,128]{2,1,0:T(8,128)S(1)} %get-tuple-element.62.pairs, f32[32,704,128]{2,1,0:T(8,128)S(1)} %get-tuple-element.72.state, f32[32,128,128]{2,1,0:T(8,128)S(1)} %get-tuple-element.86.z1), custom_call_target="tpu_custom_call" | custom-call | tf_op jit(solution)/shard_map/pallas_call | solution.py:808
Async XLA Ops:
  27.2 7.1 %collective-permute-start = (f32[8,16,128]{2,1,0:T(8,128)S(1)}, f32[8,16,128]{2,1,0:T(8,128)S(1)}, u32[]{:S(2)}, u32[]{:S(2)}) collective-permute-start(f32[8,16,128]{2,1,0:T(8,128)S(1)} %get-tuple-element.53), channel_id=1, source_target_pairs={{0,32},{32,64},{64,96},{96,0},{1,33},{33,65},{65,97},{97,1},{2,34}... | collective-permute-start | bytes 196616 | tf_op jit(solution)/shard_map/ppermute | solution.py:735
  28.9 5.4 %collective-permute-start.1 = (f32[8,16,128]{2,1,0:T(8,128)S(1)}, f32[8,16,128]{2,1,0:T(8,128)S(1)}, u32[]{:S(2)}, u32[]{:S(2)}) collective-permute-start(f32[8,16,128]{2,1,0:T(8,128)S(1)} %get-tuple-element.54), channel_id=1, source_target_pairs={{32,0},{64,32},{96,64},{0,96},{33,1},{65,33},{97,65},{1,97},{34,2}... | collective-permute-start | bytes 196616 | tf_op jit(solution)/shard_map/ppermute | solution.py:735
  71.7 4.9 %collective-permute-start.2 = (f32[8,8,128]{2,1,0:T(8,128)S(1)}, f32[8,8,128]{2,1,0:T(8,128)S(1)}, u32[]{:S(2)}, u32[]{:S(2)}) collective-permute-start(f32[8,8,128]{2,1,0:T(8,128)S(1)} %get-tuple-element.70), channel_id=1, source_target_pairs={{0,32},{32,64},{64,96},{96,0},{1,33},{33,65},{65,97},{97,1},{2,34}... | collective-permute-start | bytes 98312 | tf_op jit(solution)/shard_map/ppermute | solution.py:735
  72.2 4.4 %collective-permute-start.3 = (f32[8,8,128]{2,1,0:T(8,128)S(1)}, f32[8,8,128]{2,1,0:T(8,128)S(1)}, u32[]{:S(2)}, u32[]{:S(2)}) collective-permute-start(f32[8,8,128]{2,1,0:T(8,128)S(1)} %get-tuple-element.71), channel_id=1, source_target_pairs={{32,0},{64,32},{96,64},{0,96},{33,1},{65,33},{97,65},{1,97},{34,2}... | collective-permute-start | bytes 98312 | tf_op jit(solution)/shard_map/ppermute | solution.py:735
  116.5 4.2 %collective-permute-start.4 = (f32[8,8,128]{2,1,0:T(8,128)S(1)}, f32[8,8,128]{2,1,0:T(8,128)S(1)}, u32[]{:S(2)}, u32[]{:S(2)}) collective-permute-start(f32[8,8,128]{2,1,0:T(8,128)S(1)} %get-tuple-element.82), channel_id=1, source_target_pairs={{0,32},{32,64},{64,96},{96,0},{1,33},{33,65},{65,97},{97,1},{2,34}... | collective-permute-start | bytes 98312 | tf_op jit(solution)/shard_map/ppermute | solution.py:735
  117.1 3.6 %collective-permute-start.5 = (f32[8,8,128]{2,1,0:T(8,128)S(1)}, f32[8,8,128]{2,1,0:T(8,128)S(1)}, u32[]{:S(2)}, u32[]{:S(2)}) collective-permute-start(f32[8,8,128]{2,1,0:T(8,128)S(1)} %get-tuple-element.83), channel_id=1, source_target_pairs={{32,0},{64,32},{96,64},{0,96},{33,1},{65,33},{97,65},{1,97},{34,2}... | collective-permute-start | bytes 98312 | tf_op jit(solution)/shard_map/ppermute | solution.py:735

commit v8 on v7

--- a/solution.py
+++ b/solution.py
@@ -11,6 +11,7 @@
 PAIRS = 32
 TILES = 32
 CHUNK = 8
+MIDDLE = 16
 LONG = 32
 CHUNKS = PAIRS // CHUNK
 TABLE = 72
@@ -306,8 +307,8 @@
     low = iota((32, 128), 1) < 64
 
     def lines(i, carry):
-        for k in range(CHUNK):
-            j = i * CHUNK + k
+        for k in range(MIDDLE):
+            j = i * MIDDLE + k
             tiles = []
             for r in range(2):
                 s = table[2 * j + r]
@@ -328,7 +329,7 @@
             fields[j, 64:128, :] = load_field(f_ref, table, j, 0.0)
         return carry
 
-    lax.fori_loop(0, CHUNKS, lines, 0)
+    lax.fori_loop(0, PAIRS // MIDDLE, lines, 0)
 
 
 def side_masks():
@@ -760,7 +761,7 @@
     south, north, p = lax.optimization_barrier((south, north, p))
     weight, fields = call(
         prepare, (resident(PAIRS, 128, 256, dtype=BF16), resident(PAIRS, 128, 128)), [smem()] + [vmem()] * 3,
-        [buffer(CHUNK, 128, 128)],
+        [buffer(MIDDLE, 128, 128)],
     )(table, held(p), held(a), held(f))
     halo, face = call(
         first_return, (struct(PAIRS, 16, 128), struct(TILES, 8, 128)), [smem()] + [vmem()] * 3

time: 142 us -> 141 us (level)
  no operation moved by 1% of the time
where the time goes in v8:
time: 141 us
  blocking collectives  89.7 us (64%)
  Pallas kernels  41.7 us (30%)
  starting transfers between devices  9.4 us (7%)
    all_to_all x5, blocking collectives, exchange(): return lax.all_to_all(x, 'dev', split_axis=0, concat_axis=0, tiled=True)  73.4 us
    all_to_all x1, blocking collectives, shards(): lax.all_to_all(partial, ('grp', 'dev'), split_axis=0, concat_axis=0, tile...  16.3 us
    pallas_call x1, Pallas kernels, shards(): call(second_step, (whole, whole, whole, struct(PAIRS * 32, 128)), [smem()...  10 us
    pallas_call x1, Pallas kernels, shards(): call(first_step, (resident(PAIRS, STATE, 128), struct(PAIRS * 16, 128)),...  9.89 us
    pallas_call x1, Pallas kernels, shards(): call(first_edges, (struct(PAIRS * 32, 128), struct(TABLE, dtype=jnp.int32...  6.56 us
    ppermute x3, starting transfers between devices, from_groups(): lax.ppermute(south, 'grp', [(j, i) for i, j in ahead])  6.32 us
    ppermute x3, starting transfers between devices, from_groups(): lax.ppermute(north, 'grp', ahead)  3.08 us
    pallas_call x1, Pallas kernels, shards(): call(prepare, (resident(PAIRS, 128, 256, dtype=BF16), resident(PAIRS, 128...  3.08 us
  transfers between devices with their start and end apart: 6, of which 0 were waited for; matrix products, arithmetic and copies ran while one was open for 0% of the time, Pallas kernels for 5%

profile of v8, /device:TPU:1, one launch (start us, length us, event | category | flops | bytes accessed | tf_op | source)
XLA Modules:
  0.0 141.1 jit_solution(16903010177303653729)
XLA Ops:
  0.0 6.6 %shard_map.82 = (f32[1024,128]{1,0:T(8,128)S(1)}, s32[72]{0:T(128)S(1)}, s32[144]{0:T(256)S(1)}, s32[40]{0:T(128)S(1)}, f32[32,192,128]{2,1,0:T(8,128)S(1)}, /*i...) custom-call(s32[64]{0:T(128)} %ocean.1, ...), custom_call_target="tpu_custom_call" | custom-call | tf_op jit(solution)/shard_map/pallas_call | solution.py:744
  6.6 19.9 %all_to_all.36.received_ref = f32[32,32,128]{2,1,0:T(8,128)S(1)} all-to-all(f32[32,32,128]{2,1,0:T(8,128)S(1)} %bitcast.47), channel_id=1, replica_groups=mesh['grp'=4,'dev'=32] {'dev'}, dimensions={0} | all-to-all | bytes 1048576 | tf_op jit(solution)/shard_map/all_to_all | solution.py:725
  26.5 0.7 shard_map.83
  27.2 1.7 %collective-permute-start = (f32[8,16,128]{2,1,0:T(8,128)S(1)}, f32[8,16,128]{2,1,0:T(8,128)S(1)}, u32[]{:S(2)}, u32[]{:S(2)}) collective-permute-start(f32[8,16,128]{2,1,0:T(8,128)S(1)} %get-tuple-element.53), channel_id=1, source_target_pairs={{0,32},{32,64},{64,96},{96,0},{1,33},{33,65},{65,97},{97,1},{2,34}... | collective-permute-start | bytes 196616 | tf_op jit(solution)/shard_map/ppermute | solution.py:736
  28.9 2.2 %collective-permute-start.1 = (f32[8,16,128]{2,1,0:T(8,128)S(1)}, f32[8,16,128]{2,1,0:T(8,128)S(1)}, u32[]{:S(2)}, u32[]{:S(2)}) collective-permute-start(f32[8,16,128]{2,1,0:T(8,128)S(1)} %get-tuple-element.54), channel_id=1, source_target_pairs={{32,0},{64,32},{96,64},{0,96},{33,1},{65,33},{97,65},{1,97},{34,2}... | collective-permute-start | bytes 196616 | tf_op jit(solution)/shard_map/ppermute | solution.py:736
  31.1 3.1 %shard_map.85 = (bf16[32,128,256]{2,1,0:T(8,128)(2,1)S(1)}, f32[32,128,128]{2,1,0:T(8,128)S(1)}) custom-call(s32[72]{0:T(128)S(1)} %get-tuple-element.46.table, f32[8,256,128]{2,1,0:T(8,128)S(1)} %get-tuple-element.56.p_ref, f32[8,256,128]{2,1,0:T(8,128)S(1)} %get-tuple-element.57.a_ref, f32[8,256,128]{2,1,0:T(8,128)S(1)} %get-tuple-element.58.f_ref), custom_call_target="tpu_custom_call" | custom-call | tf_op jit(solution)/shard_map/pallas_call | solution.py:762
  34.2 0.0 collective-permute-done.south
  34.2 0.0 collective-permute-done.1.north
  34.2 1.4 %shard_map.84 = (f32[32,16,128]{2,1,0:T(8,128)S(1)}, f32[32,8,128]{2,1,0:T(8,128)S(1)}) custom-call(s32[40]{0:T(128)S(1)} %get-tuple-element.47.arrival, f32[32,32,128]{2,1,0:T(8,128)S(1)} %all_to_all.36.received_ref, f32[8,16,128]{2,1,0:T(8,128)S(1)} %collective-permute-done.south, f32[8,16,128]{2,1,0:T(8,128)S(1)} %collective-permute-done.1.north), custom_call_target="tpu_custom_call" | custom-call | tf_op jit(solution)/shard_map/pallas_call | solution.py:766
  35.7 12.8 %all_to_all.37 = f32[32,16,128]{2,1,0:T(8,128)S(1)} all-to-all(f32[32,16,128]{2,1,0:T(8,128)S(1)} %get-tuple-element.61), channel_id=1, replica_groups=mesh['grp'=4,'dev'=32] {'dev'}, dimensions={0} | all-to-all | bytes 524288 | tf_op jit(solution)/shard_map/all_to_all | solution.py:725
  48.5 9.9 %shard_map.86 = (f32[32,704,128]{2,1,0:T(8,128)S(1)}, f32[512,128]{1,0:T(8,128)S(1)}) custom-call(s32[72]{0:T(128)S(1)} %get-tuple-element.46.table, s32[144]{0:T(256)S(1)} %get-tuple-element.48.codes, f32[512,128]{1,0:T(8,128)S(1)} %bitcast.46, f32[32,192,128]{2,1,0:T(8,128)S(1)} %get-tuple-element.62.pairs, f32[64,64,128]{2,1,0:T(8,128)S(1)} %get-tuple-element.63.b_ref, ...), custom_call_target="tpu_custom_call" | custom-call | tf_op jit(solution)/shard_map/pallas_call | solution.py:772
  58.4 12.5 %all_to_all.38.received_ref = f32[32,16,128]{2,1,0:T(8,128)S(1)} all-to-all(f32[32,16,128]{2,1,0:T(8,128)S(1)} %bitcast.50), channel_id=1, replica_groups=mesh['grp'=4,'dev'=32] {'dev'}, dimensions={0} | all-to-all | bytes 524288 | tf_op jit(solution)/shard_map/all_to_all | solution.py:725
  70.9 0.7 shard_map.87
  71.6 0.7 collective-permute-start.2
  72.2 2.1 %collective-permute-start.3 = (f32[8,8,128]{2,1,0:T(8,128)S(1)}, f32[8,8,128]{2,1,0:T(8,128)S(1)}, u32[]{:S(2)}, u32[]{:S(2)}) collective-permute-start(f32[8,8,128]{2,1,0:T(8,128)S(1)} %get-tuple-element.71), channel_id=1, source_target_pairs={{32,0},{64,32},{96,64},{0,96},{33,1},{65,33},{97,65},{1,97},{34,2}... | collective-permute-start | bytes 98312 | tf_op jit(solution)/shard_map/ppermute | solution.py:736
  74.3 2.2 %shard_map.88 = (f32[32,128,128]{2,1,0:T(8,128)S(1)}, f32[256,128]{1,0:T(8,128)S(1)}) custom-call(f32[32,704,128]{2,1,0:T(8,128)S(1)} %get-tuple-element.72.state), custom_call_target="tpu_custom_call" | custom-call | tf_op jit(solution)/shard_map/pallas_call | solution.py:783
  76.5 0.0 collective-permute-done.2.south
  76.5 0.0 collective-permute-done.3.north
  76.6 1.0 shard_map.89
  77.6 13.0 %all_to_all.39.earlier_ref = f32[32,16,128]{2,1,0:T(8,128)S(1)} all-to-all(f32[32,16,128]{2,1,0:T(8,128)S(1)} %shard_map.89), channel_id=1, replica_groups=mesh['grp'=4,'dev'=32] {'dev'}, dimensions={0} | all-to-all | bytes 524288 | tf_op jit(solution)/shard_map/all_to_all | solution.py:725
  90.6 10.0 %shard_map.90 = (f32[32,128,128]{2,1,0:T(8,128)S(1)}, f32[32,128,128]{2,1,0:T(8,128)S(1)}, f32[32,128,128]{2,1,0:T(8,128)S(1)}, f32[1024,128]{1,0:T(8,128)S(1)}) custom-call(s32[144]{0:T(256)S(1)} %get-tuple-element.48.codes, f32[512,128]{1,0:T(8,128)S(1)} %bitcast.45, f32[32,704,128]{2,1,0:T(8,128)S(1)} %get-tuple-element.72.state, ...), custom_call_target="tpu_custom_call" | custom-call | tf_op jit(solution)/shard_map/pallas_call | solution.py:793
  100.6 15.1 %all_to_all.40.received_ref = f32[32,32,128]{2,1,0:T(8,128)S(1)} all-to-all(f32[32,32,128]{2,1,0:T(8,128)S(1)} %bitcast.48), channel_id=1, replica_groups=mesh['grp'=4,'dev'=32] {'dev'}, dimensions={0} | all-to-all | bytes 1048576 | tf_op jit(solution)/shard_map/all_to_all | solution.py:725
  115.7 0.7 shard_map.91
  116.4 0.7 collective-permute-start.4
  117.1 2.0 %collective-permute-start.5 = (f32[8,8,128]{2,1,0:T(8,128)S(1)}, f32[8,8,128]{2,1,0:T(8,128)S(1)}, u32[]{:S(2)}, u32[]{:S(2)}) collective-permute-start(f32[8,8,128]{2,1,0:T(8,128)S(1)} %get-tuple-element.83), channel_id=1, source_target_pairs={{32,0},{64,32},{96,64},{0,96},{33,1},{65,33},{97,65},{1,97},{34,2}... | collective-permute-start | bytes 98312 | tf_op jit(solution)/shard_map/ppermute | solution.py:736
  119.2 1.5 %shard_map.92.sums_ref = f32[6,8,128]{2,1,0:T(8,128)S(1)} custom-call(f32[32,704,128]{2,1,0:T(8,128)S(1)} %get-tuple-element.72.state, f32[32,128,128]{2,1,0:T(8,128)S(1)} %get-tuple-element.84.d_ref, f32[32,128,128]{2,1,0:T(8,128)S(1)} %get-tuple-element.85.p_ref), custom_call_target="tpu_custom_call" | custom-call | tf_op jit(solution)/shard_map/pallas_call | solution.py:803
  120.6 0.0 collective-permute-done.4.south
  120.6 0.0 collective-permute-done.5.north
  120.7 1.3 shard_map.93
  121.9 16.3 %all_to_all.41 = f32[128,1,128]{2,1,0:T(1,128)S(1)} all-to-all(f32[128,1,128]{2,1,0:T(1,128)S(1)} %bitcast.51), channel_id=1, replica_groups=mesh['grp'=4,'dev'=32] {'grp','dev'}, dimensions={0} | all-to-all | bytes 131072 | tf_op jit(solution)/shard_map/all_to_all | solution.py:807
  138.2 2.7 %shard_map.94 = f32[64,64,128]{2,1,0:T(8,128)} custom-call(s32[72]{0:T(128)S(1)} %get-tuple-element.46.table, f32[128,128]{1,0:T(8,128)S(1)} %bitcast.49, f32[32,192,128]{2,1,0:T(8,128)S(1)} %get-tuple-element.62.pairs, f32[32,704,128]{2,1,0:T(8,128)S(1)} %get-tuple-element.72.state, f32[32,128,128]{2,1,0:T(8,128)S(1)} %get-tuple-element.86.z1), custom_call_target="tpu_custom_call" | custom-call | tf_op jit(solution)/shard_map/pallas_call | solution.py:809
Async XLA Ops:
  27.2 7.0 %collective-permute-start = (f32[8,16,128]{2,1,0:T(8,128)S(1)}, f32[8,16,128]{2,1,0:T(8,128)S(1)}, u32[]{:S(2)}, u32[]{:S(2)}) collective-permute-start(f32[8,16,128]{2,1,0:T(8,128)S(1)} %get-tuple-element.53), channel_id=1, source_target_pairs={{0,32},{32,64},{64,96},{96,0},{1,33},{33,65},{65,97},{97,1},{2,34}... | collective-permute-start | bytes 196616 | tf_op jit(solution)/shard_map/ppermute | solution.py:736
  28.9 5.3 %collective-permute-start.1 = (f32[8,16,128]{2,1,0:T(8,128)S(1)}, f32[8,16,128]{2,1,0:T(8,128)S(1)}, u32[]{:S(2)}, u32[]{:S(2)}) collective-permute-start(f32[8,16,128]{2,1,0:T(8,128)S(1)} %get-tuple-element.54), channel_id=1, source_target_pairs={{32,0},{64,32},{96,64},{0,96},{33,1},{65,33},{97,65},{1,97},{34,2}... | collective-permute-start | bytes 196616 | tf_op jit(solution)/shard_map/ppermute | solution.py:736
  71.6 4.9 %collective-permute-start.2 = (f32[8,8,128]{2,1,0:T(8,128)S(1)}, f32[8,8,128]{2,1,0:T(8,128)S(1)}, u32[]{:S(2)}, u32[]{:S(2)}) collective-permute-start(f32[8,8,128]{2,1,0:T(8,128)S(1)} %get-tuple-element.70), channel_id=1, source_target_pairs={{0,32},{32,64},{64,96},{96,0},{1,33},{33,65},{65,97},{97,1},{2,34}... | collective-permute-start | bytes 98312 | tf_op jit(solution)/shard_map/ppermute | solution.py:736
  72.2 4.3 %collective-permute-start.3 = (f32[8,8,128]{2,1,0:T(8,128)S(1)}, f32[8,8,128]{2,1,0:T(8,128)S(1)}, u32[]{:S(2)}, u32[]{:S(2)}) collective-permute-start(f32[8,8,128]{2,1,0:T(8,128)S(1)} %get-tuple-element.71), channel_id=1, source_target_pairs={{32,0},{64,32},{96,64},{0,96},{33,1},{65,33},{97,65},{1,97},{34,2}... | collective-permute-start | bytes 98312 | tf_op jit(solution)/shard_map/ppermute | solution.py:736
  116.4 4.2 %collective-permute-start.4 = (f32[8,8,128]{2,1,0:T(8,128)S(1)}, f32[8,8,128]{2,1,0:T(8,128)S(1)}, u32[]{:S(2)}, u32[]{:S(2)}) collective-permute-start(f32[8,8,128]{2,1,0:T(8,128)S(1)} %get-tuple-element.82), channel_id=1, source_target_pairs={{0,32},{32,64},{64,96},{96,0},{1,33},{33,65},{65,97},{97,1},{2,34}... | collective-permute-start | bytes 98312 | tf_op jit(solution)/shard_map/ppermute | solution.py:736
  117.1 3.5 %collective-permute-start.5 = (f32[8,8,128]{2,1,0:T(8,128)S(1)}, f32[8,8,128]{2,1,0:T(8,128)S(1)}, u32[]{:S(2)}, u32[]{:S(2)}) collective-permute-start(f32[8,8,128]{2,1,0:T(8,128)S(1)} %get-tuple-element.83), channel_id=1, source_target_pairs={{32,0},{64,32},{96,64},{0,96},{33,1},{65,33},{97,65},{1,97},{34,2}... | collective-permute-start | bytes 98312 | tf_op jit(solution)/shard_map/ppermute | solution.py:736
